TPU v7x, 256 devices: a whole 4x4x8 slice. The times are simulated.
256 devices in a mesh: row: 8 (over y, core), sim: 32 (over x, z).
Axes of the slice: x: 4, y: 4, z: 8, core: 2. Of those that a mesh axis runs over, the one named last changes fastest.
Arguments:
- sim_points: float32 [24, 131072], P(None, ('row', 'sim')), may hold values from 0 to 1
- weights: float32 [131072], P(('row', 'sim')), may hold values from -0.06629126 to 0.06629126
- hw_points: float32 [24, 32768], P(None, ('row', 'sim')), may hold values from 0 to 1
- high_values: float32 [32768], P(('row', 'sim')), may hold values from -6 to 6
- len_low: float32 [24], replicated, may hold values from 0.6 to 3
- len_high: float32 [24], replicated, may hold values from 0.6 to 3
- rho: float32 [1], replicated, may hold values from 0.5 to 1.5
- noise: float32 [1], replicated, may hold values from 0.3 to 1
Outputs:
- mu_low: float32 [32768], P(('row', 'sim'))
- solution: float32 [32768], P(('row', 'sim'))
- residual: float32 [32768], P(('row', 'sim'))
All inputs are finite; a program needn't handle non-finite values.
Results may differ from a plain program's by a relative error of at most 0.0003.
Values sent between devices are 32-bit elements; how exact they have to be, the bound alone decides.
No kernel may reach another device: no remote copies, remote signals or barrier semaphores. Data moves between devices by JAX's collectives and lax.ppermute only.
A program may use at most 64 MiB of HBM per device.

v0:
```python
import jax
import jax.numpy as jnp
from jax import lax
from jax.sharding import PartitionSpec as P

ITERS = 2


def row_blocks(row_pts):
    feats, count = row_pts.shape
    block = 512
    return jnp.moveaxis(row_pts.reshape(feats, count // block, block), 1, 0)


def kernel_block(piece, col_pts, col_norms):
    norms = jnp.sum(piece * piece, axis=0)
    cross = lax.dot_general(
        piece,
        col_pts,
        (((0,), (0,)), ((), ())),
        precision=lax.Precision.HIGHEST,
        preferred_element_type=jnp.float32,
    )
    return jnp.exp(-0.5 * (norms[:, None] + col_norms[None, :] - 2.0 * cross))


def kernel_apply(row_pts, col_pts, col_norms, vector):
    count = row_pts.shape[1]

    def single(piece):
        return jnp.dot(
            kernel_block(piece, col_pts, col_norms),
            vector,
            precision=lax.Precision.HIGHEST,
            preferred_element_type=jnp.float32,
        )

    return lax.map(single, row_blocks(row_pts)).reshape(count)


def kernel_tile(row_pts, col_pts, col_norms):
    count = row_pts.shape[1]
    tiles = lax.map(lambda piece: kernel_block(piece, col_pts, col_norms), row_blocks(row_pts))
    return tiles.reshape(count, col_pts.shape[1])


def local(sim_points, weights, hw_points, high_values, len_low, len_high, rho, noise):
    local_rows = high_values.shape[0]
    feats = hw_points.shape[0]
    row_count = lax.axis_size("row")
    sim_count = lax.axis_size("sim")
    row_index = lax.axis_index("row")
    sim_index = lax.axis_index("sim")
    everything = lax.all_gather(hw_points, ("row", "sim"), axis=1, tiled=True)
    block_rows = lax.dynamic_slice_in_dim(
        everything, row_index * local_rows * sim_count, local_rows * sim_count, 1
    )
    grid = everything.reshape(feats, row_count, sim_count, local_rows)
    block_cols = lax.dynamic_index_in_dim(grid, sim_index, 2, False).reshape(
        feats, row_count * local_rows
    )
    runs_scaled = sim_points / len_low[:, None]
    runs_norms = jnp.sum(runs_scaled * runs_scaled, axis=0)
    every_low = everything / len_low[:, None]
    mu_low = lax.psum_scatter(
        kernel_apply(every_low, runs_scaled, runs_norms, weights),
        ("row", "sim"),
        scatter_dimension=0,
        tiled=True,
    )
    target = high_values - rho[0] * mu_low
    rows_high = block_rows / len_high[:, None]
    cols_high = block_cols / len_high[:, None]
    cols_norms = jnp.sum(cols_high * cols_high, axis=0)
    stored = kernel_tile(rows_high, cols_high, cols_norms)

    def squares(vector):
        return lax.psum(jnp.sum(vector * vector), ("row", "sim"))

    solution = jnp.zeros_like(target)
    residual = target
    direction = target
    norm_now = squares(residual)
    for step in range(ITERS):
        vector_cols = lax.all_gather(direction, "row", axis=0, tiled=True)
        image = (
            lax.psum_scatter(
                jnp.dot(
                    stored,
                    vector_cols,
                    precision=lax.Precision.HIGHEST,
                    preferred_element_type=jnp.float32,
                ),
                "sim",
                scatter_dimension=0,
                tiled=True,
            )
            + noise[0] * direction
        )
        alpha = norm_now / lax.psum(jnp.sum(direction * image), ("row", "sim"))
        solution = solution + alpha * direction
        residual = residual - alpha * image
        norm_next = squares(residual)
        direction = residual + norm_next / norm_now * direction
        norm_now = norm_next
    return (mu_low, solution, residual)


def solution(mesh):
    placed = (
        P(None, ("row", "sim")),
        P(("row", "sim")),
        P(None, ("row", "sim")),
        P(("row", "sim")),
        P(),
        P(),
        P(),
        P(),
    )
    return jax.shard_map(
        local,
        mesh=mesh,
        in_specs=placed,
        out_specs=(P(("row", "sim")), P(("row", "sim")), P(("row", "sim"))),
        check_vma=False,
    )
```

profile of v0, /device:TPU:32, one launch (start us, length us, event | category | flops | bytes accessed | tf_op | source)
XLA Modules:
  0.0 1145.6 jit_solution(6105718144799165119)
XLA Ops:
  9.3 1.3 dynamic-slice.1
  12.1 108.7 %all-gather.4.cloned.1.call-done = f32[24,32768]{1,0:T(8,128)} async-done(((f32[24,128]{1,0:T(8,128)}), f32[24,32768]{1,0:T(8,128)}) %all-gather.4.cloned.1.call-update) | async-done | bytes 3145744 | tf_op jit(solution)/shard_map/all_gather | solution.py:54
  120.8 2.2 broadcast_divide_fusion
  123.0 3.5 copy.21
  126.5 211.3 %while.20 = (s32[]{:T(128)}, f32[64,512]{1,0:T(8,128)S(1)}, f32[64,24,512]{2,0,1:T(8,128)}, f32[512]{0:T(512)S(1)}, f32[24,512]{1,0:T(8,128)S(1)}, /*index=5*/f32[512]{0:T(512)S(1)}, s32[]{:T(128)}, s32[]{:T(128)}) while((s32[]{:T(128)}, f32[64,512]{1,0:T(8,128)S(1)}, f32[64,24,512]{2,0,1:T(8,128)}, f32[512]{0:T(512)S(1)}, ...), condition=%wide.region_3.4_spmd, body=%wide.region_1.3_spmd.sunk | while | flops 79715840 | bytes 2357349 | solution.py:38
  339.8 28.8 %while.21 = (s32[]{:T(128)}, f32[8,512,1024]{2,1,0:T(8,128)}, f32[8,24,512]{2,0,1:T(8,128)S(1)}, f32[1024]{0:T(1024)S(1)}, f32[24,1024]{1,0:T(8,128)S(1)}, /*index=5*/s32[]{:T(128)}) while((s32[]{:T(128)}, f32[8,512,1024]{2,1,0:T(8,128)}, f32[8,24,512]{2,0,1:T(8,128)S(1)}, f32[1024]{0:T(1024)S(1)}, f32[24,1024]{1,0:T(8,128)S(1)}, ...), condition=%wide.region_10.11_spmd, body=%wide.region_8.10_spmd.sunk | while | flops 153116160 | bytes 2400341 | solution.py:43
  339.8 3.5 bitcast_dynamic-update-slice_fusion.2
  343.5 3.5 bitcast_dynamic-update-slice_fusion.2
  347.0 3.5 bitcast_dynamic-update-slice_fusion.2
  350.6 3.5 bitcast_dynamic-update-slice_fusion.2
  354.2 3.6 bitcast_dynamic-update-slice_fusion.2
  357.9 3.5 bitcast_dynamic-update-slice_fusion.2
  361.4 3.6 bitcast_dynamic-update-slice_fusion.2
  365.0 3.5 bitcast_dynamic-update-slice_fusion.2
  368.5 209.6 %all-reduce.6.cloned.1.call-done = f32[32768]{0:T(1024)} async-done(((f32[32768]{0:T(1024)}), f32[32768]{0:T(1024)}) %all-reduce.6.cloned.1.call-update) | async-done | bytes 131088
  579.4 10.4 all-gather
  589.8 17.5 %fusion.5 = f32[1,4096]{1,0:T(1,128)S(1)} fusion(f32[4096,1024]{1,0:T(8,128)} %bitcast.83, f32[8,1,128]{2,1,0:T(1,128)S(1)} %all-gather), kind=kOutput, calls=%fused_computation.19 | convolution fusion | flops 50331648 | bytes 16797696 | tf_op jit(solution)/shard_map/dot_general | solution.py:88
  607.3 136.2 %all-reduce.1 = f32[4096]{0:T(1024)S(1)} all-reduce(f32[4096]{0:T(1024)S(1)} %bitcast.96), channel_id=3, replica_groups=mesh['row'=8,'sim'=32] {'sim'}, use_global_device_ids=true, to_apply=%region_11.12.clone | all-reduce | flops 4096 | bytes 32768
  744.2 74.6 %all-reduce.3 = (f32[]{:T(128)}, f32[]{:T(128)}) all-reduce(f32[]{:T(128)} %get-tuple-element.87, f32[]{:T(128)} %get-tuple-element.86), channel_id=1, replica_groups=mesh['row'=8,'sim'=32] {'row','sim'}, use_global_device_ids=true, to_apply=%region_6.7 | all-reduce | flops 2 | bytes 16 | tf_op jit(solution)/shard_map/psum | solution.py:78
  820.9 73.5 %psum.30 = f32[]{:T(128)} all-reduce(f32[]{:T(128)} %get-tuple-element.112), channel_id=1, replica_groups=mesh['row'=8,'sim'=32] {'row','sim'}, use_global_device_ids=true, to_apply=%region_15.16 | all-reduce | flops 1 | bytes 8 | tf_op jit(solution)/shard_map/psum | solution.py:78
  895.7 10.6 all-gather.1
  906.3 17.5 %fusion.3 = f32[1,4096]{1,0:T(1,128)S(1)} fusion(f32[4096,1024]{1,0:T(8,128)} %bitcast.84, f32[8,1,128]{2,1,0:T(1,128)S(1)} %all-gather.1), kind=kOutput, calls=%fused_computation.17 | convolution fusion | flops 50331648 | bytes 16797696 | tf_op jit(solution)/shard_map/dot_general | solution.py:88
  923.8 135.2 %all-reduce.2 = f32[4096]{0:T(1024)S(1)} all-reduce(f32[4096]{0:T(1024)S(1)} %bitcast.95), channel_id=4, replica_groups=mesh['row'=8,'sim'=32] {'sim'}, use_global_device_ids=true, to_apply=%region_16.17.clone | all-reduce | flops 4096 | bytes 32768
  1059.7 77.1 %psum.31 = f32[]{:T(128)} all-reduce(f32[]{:T(128)} %multiply_reduce_fusion.4), channel_id=1, replica_groups=mesh['row'=8,'sim'=32] {'row','sim'}, use_global_device_ids=true, to_apply=%region_18.19 | all-reduce | flops 1 | bytes 8 | tf_op jit(solution)/shard_map/psum | solution.py:100
  (364 shorter events, 216.9 us)
Async XLA Ops:
  7.2 113.7 %all-gather.4.cloned.1.call-start = ((), (), s32[]{:S(2)}) async-start(), calls=%async_computation | async-start | bytes 3158016 | tf_op jit(solution)/shard_map/all_gather | solution.py:54
  7.9 570.3 %all-reduce.6.cloned.1.call-start = ((), (), s32[]{:S(2)}) async-start(), calls=%async_computation.1 | async-start | bytes 262144
  123.0 3.6 copy-start.1
  123.0 215.5 %copy-start = (f32[24,32768]{1,0:T(8,128)S(1)}, f32[24,32768]{1,0:T(8,128)}, u32[]{:S(2)}) copy-start(f32[24,32768]{1,0:T(8,128)} %all-gather.4.cloned.1.call-done) | copy-start | bytes 9437188
  126.5 212.0 %copy-start.2 = (f32[24]{0:T(128)S(1)}, f32[24]{0:T(128)}, u32[]{:S(2)}) copy-start(f32[24]{0:T(128)} %param.17) | copy-start | bytes 292
  339.7 238.4 %copy-start.3 = (f32[128]{0:T(128)S(1)}, f32[128]{0:T(128)}, u32[]{:S(2)}) copy-start(f32[128]{0:T(128)} %param.15) | copy-start | bytes 1540
Sparse Core Ops, SparseCore 0:
  11.8 108.9 all-gather.3
  338.6 239.4 all-reduce.5
where the time goes:
time: 1150 us
  blocking collectives  518 us (45%)
  waiting for transfers between devices  319 us (28%)
  matrix products  201 us (17%)
  local copies, waits for them, and re-layouts  76.4 us (7%)
  between operations  20.1 us (2%)
    unnamed x2, blocking collectives  271 us
    unnamed x3, waiting for transfers between devices  210 us
    psum x2, blocking collectives, squares(): return lax.psum(jnp.sum(vector * vector), ('row', 'sim'))  148 us
    all_gather x1, waiting for transfers between devices, local(): everything = lax.all_gather(hw_points, ('row', 'sim'), axis=1, tiled=True)  109 us
    dot_general x72, matrix products, kernel_block(): lax.dot_general(piece, col_pts, (((0,), (0,)), ((), ())), precision=lax.P...  103 us
    psum x1, blocking collectives, local(): alpha = norm_now / lax.psum(jnp.sum(direction * image), ('row', 'sim'))  77.1 us
    dynamic_slice x64, local copies, waits for them, and re-layouts, kernel_apply(): return lax.map(single, row_blocks(row_pts)).reshape(count)  66.5 us
    dot_general x64, matrix products, single(): jnp.dot(kernel_block(piece, col_pts, col_norms), vector, precision=lax.Pr...  62.9 us
  transfers between devices with their start and end apart: 2, of which 2 were waited for; matrix products, arithmetic and copies ran while one was open for 3% of the time, Pallas kernels for 0%

commit v1 on v0

v1 whole, which is shorter than its diff:
```python
import math

import jax
import jax.numpy as jnp
from jax import lax
from jax.experimental import pallas as pl
from jax.experimental.pallas import tpu as pltpu
from jax.sharding import PartitionSpec as P

F32 = jnp.float32
BF16 = jnp.bfloat16
FEATS = 24
LANES = 128
DEPTH = 160
ROOT = math.sqrt(math.log2(math.e))
VMEM = pl.BlockSpec(memory_space=pltpu.VMEM)
SMEM = pl.BlockSpec(memory_space=pltpu.SMEM)


def params(mib):
    return pltpu.CompilerParams(vmem_limit_bytes=mib * 1024 * 1024)


def shape(dims, kind=F32):
    return jax.ShapeDtypeStruct(dims, kind)


def split(x):
    high = x.astype(BF16).astype(F32)
    rest = x - high
    mid = rest.astype(BF16).astype(F32)
    return high, mid, rest - mid


def norm_rows(norm, at):
    high, mid, low = split(norm)
    row = lax.broadcasted_iota(jnp.int32, (8, norm.shape[1]), 0)
    ones = jnp.where((row >= 3 - at) & (row < 6 - at), 1.0, 0.0)
    return jnp.where(row == at, high, jnp.where(row == at + 1, mid, jnp.where(row == at + 2, low, ones)))


def scaled(points, scale):
    return (points - 0.5) * scale


def half_norm(points):
    return -0.5 * jnp.sum(points * points, axis=0, keepdims=True)


def left(points, scale):
    u = scaled(points, scale)
    high, mid, low = split(u)
    norms = norm_rows(half_norm(u), 0)
    return jnp.concatenate([high, high, high, mid, mid, low, norms, jnp.zeros_like(norms)], 0).astype(BF16)


def right(points, scale):
    v = scaled(points, scale)
    high, mid, low = split(v)
    norms = norm_rows(half_norm(v), 3)
    return jnp.concatenate([high, mid, low, high, mid, high, norms, jnp.zeros_like(norms)], 0)


def pack_kernel(runs, weights, points, len_low, len_high, out_row, out_sim, scale_low, scale_high):
    row = lax.broadcasted_iota(jnp.int32, (FEATS, LANES), 0)
    for lengths, out in ((len_low, scale_low), (len_high, scale_high)):
        column = jnp.ones((FEATS, LANES), F32)
        for i in range(FEATS):
            column = jnp.where(row == i, lengths[i], column)
        out[...] = ROOT / column
    own = points[...]
    for i in range(out_row.shape[0]):
        out_row[i, :FEATS, :512] = runs[...]
        out_row[i, FEATS:, :512] = jnp.broadcast_to(weights[...], (8, 512))
        out_row[i, :FEATS, 512:] = own
        out_row[i, FEATS:, 512:] = jnp.zeros((8, LANES), F32)
    for i in range(out_sim.shape[0]):
        out_sim[i] = own


def prep_kernel(held, scale_low, scale_high, runs_out, cols_out, weights_out):
    wide = jnp.concatenate([scale_low[...]] * 4, 1)

    def step(r, carry):
        parts = right(held[r, :FEATS, :512], wide)
        for q in range(4):
            lanes = slice(q * LANES, (q + 1) * LANES)
            rows = pl.ds(pl.multiple_of(r * 512 + q * LANES, LANES), LANES)
            runs_out[rows, :] = parts[:, lanes].T.astype(BF16)
            weights_out[rows, :] = jnp.broadcast_to(held[r, FEATS : FEATS + 1, lanes], (LANES, LANES)).T
        rows = pl.ds(pl.multiple_of(r * LANES, LANES), LANES)
        cols_out[rows, :] = right(held[r, :FEATS, 512:], scale_high[...]).T.astype(BF16)
        return carry

    lax.fori_loop(0, held.shape[0], step, 0)


def build_left(points, scale, out):
    def step(g, carry):
        for q in range(8):
            k = g * 8 + q
            out[:, pl.ds(pl.multiple_of(k * LANES, LANES), LANES)] = left(points[k], scale[...])
        return carry

    lax.fori_loop(0, points.shape[0] // 8, step, 0)


def mu_kernel(points, scale, runs, weights, high, rho, at, out, parts, total):
    build_left(points, scale, parts)
    wide, chunk = 512, 512

    def step(c, carry):
        u = parts[:, pl.ds(pl.multiple_of(c * wide, wide), wide)]
        acc = jnp.zeros((8, wide), F32)
        for j in range(0, runs.shape[0], chunk):
            power = jnp.dot(runs[j : j + chunk, :], u, preferred_element_type=F32)
            w = weights[j : j + chunk, :]
            term = jnp.exp2(power) * jnp.concatenate([w] * (wide // LANES), 1)
            acc = acc + jnp.sum(term.reshape(chunk // 8, 8, wide), axis=0)
        line = jnp.sum(acc, axis=0, keepdims=True)
        for q in range(wide // LANES):
            total[pl.ds(c * (wide // LANES) + q, 1), :] = line[:, q * LANES : (q + 1) * LANES]
        return carry

    lax.fori_loop(0, parts.shape[1] // wide, step, 0)
    mu = total[...]
    row = lax.broadcasted_iota(jnp.int32, mu.shape, 0)
    target = -rho[0] * mu
    target = jnp.where(row == at[0], target + high[...], target)
    for i in range(out.shape[0]):
        out[i] = jnp.where(row == i, mu, target)


def tile_kernel(points, scale, cols, out, parts):
    build_left(points, scale, parts)
    wide, chunk = 512, 512

    def step(c, carry):
        lanes = pl.ds(pl.multiple_of(c * wide, wide), wide)
        u = parts[:, lanes]
        for j in range(0, cols.shape[0], chunk):
            power = jnp.dot(cols[j : j + chunk, :], u, preferred_element_type=F32)
            out[j : j + chunk, lanes] = jnp.exp2(power)
        return carry

    lax.fori_loop(0, parts.shape[1] // wide, step, 0)


def first_kernel(held, tile, high, rho, noise, at, out, target_out, mu_out, cols):
    total = jnp.sum(held[...], axis=0)
    row = lax.broadcasted_iota(jnp.int32, total.shape, 0)
    own = row == at[0]
    target = jnp.where(own, high[...] - rho[0] * total, total)
    target_out[...] = target
    mu_out[...] = jnp.sum(jnp.where(own, total, 0.0), axis=0, keepdims=True)
    own_target = jnp.sum(jnp.where(own, target, 0.0), axis=0, keepdims=True)

    def step(k, carry):
        rows = pl.ds(pl.multiple_of(k * LANES, LANES), LANES)
        acc = jnp.zeros((LANES, LANES), F32)
        for s in range(held.shape[1]):
            acc = acc + tile[rows, s * LANES : (s + 1) * LANES] * target_out[s : s + 1, :]
        cols[pl.ds(k, 1), :] = jnp.sum(acc.T, axis=0, keepdims=True)
        return carry

    lax.fori_loop(0, cols.shape[0], step, 0)
    image = cols[...]
    image = jnp.where(lax.broadcasted_iota(jnp.int32, image.shape, 0) == at[1], image + noise[0] * own_target, image)
    for i in range(out.shape[0]):
        out[i] = image


def second_kernel(held, tile, noise, at, out, column, rows_out):
    image = jnp.sum(held[...], axis=0)
    mine = lax.broadcasted_iota(jnp.int32, image.shape, 0) == at[1]
    own = jnp.sum(jnp.where(mine, image, 0.0), axis=0, keepdims=True)
    for k in range(image.shape[0]):
        column[k * LANES : (k + 1) * LANES, :] = jnp.broadcast_to(image[k : k + 1, :], (LANES, LANES)).T

    def step(s, carry):
        lanes = pl.ds(pl.multiple_of(s * 2 * LANES, 2 * LANES), 2 * LANES)
        acc = jnp.zeros((8, 2 * LANES), F32)
        for k in range(image.shape[0]):
            rows = slice(k * LANES, (k + 1) * LANES)
            c = column[rows, :]
            term = tile[rows, lanes] * jnp.concatenate([c, c], 1)
            acc = acc + jnp.sum(term.reshape(LANES // 8, 8, 2 * LANES), axis=0)
        line = jnp.sum(acc, axis=0, keepdims=True)
        for q in range(2):
            rows_out[pl.ds(s * 2 + q, 1), :] = line[:, q * LANES : (q + 1) * LANES]
        return carry

    lax.fori_loop(0, rows_out.shape[0] // 2, step, 0)
    total = rows_out[...]
    row = lax.broadcasted_iota(jnp.int32, total.shape, 0)
    total = jnp.where(row == at[0], total + noise[0] * own, total)
    extra = jnp.broadcast_to(own, (8, LANES))
    for i in range(out.shape[0]):
        out[i, : total.shape[0], :] = total
        out[i, total.shape[0] :, :] = extra


def two_sum(a, b):
    s = a + b
    t = s - a
    return s, (a - (s - t)) + (b - t)


def pair_add(x, y):
    s, e = two_sum(x[0], y[0])
    return two_sum(s, e + (x[1] + y[1]))


def product(a, b):
    ah = a.astype(BF16).astype(F32)
    bh = b.astype(BF16).astype(F32)
    al, bl = a - ah, b - bh
    s, e = two_sum(ah * bh, ah * bl + al * bh)
    return two_sum(s, e + al * bl)


def pair_product(x, y):
    s, e = product(x[0], y[0])
    return two_sum(s, e + (x[0] * y[1] + x[1] * y[0]))


def minus(x):
    return -x[0], -x[1]


def pair_ratio(x, y):
    q = x[0] / y[0]
    rest = pair_add(x, minus(pair_product((q, jnp.zeros_like(q)), y)))
    return two_sum(q, (rest[0] + rest[1]) / y[0])


def fold_rows(x):
    high, low = x
    count = high.shape[0]
    while count > 8:
        count //= 2
        high, low = pair_add((high[:count], low[:count]), (high[count:], low[count:]))
    return high, low


def moments_kernel(held, target, at, out, own_out):
    count = target.shape[0]
    last = jnp.sum(held[:, :count, :], axis=0)
    image = held[:, count, :]
    b = target[...]
    for i, (p, q) in enumerate(((b, b), (b, image), (image, image), (image, last))):
        high, low = fold_rows(product(p, q))
        for shift in (4, 2, 1):
            high, low = pair_add((high, low), (pltpu.roll(high, shift, 0), pltpu.roll(low, shift, 0)))
        for j in range(out.shape[0]):
            out[j, 2 * i : 2 * i + 1, :] = high[:1]
            out[j, 2 * i + 1 : 2 * i + 2, :] = low[:1]
    own = lax.broadcasted_iota(jnp.int32, b.shape, 0) == at[0]
    for i, v in enumerate((b, image, last)):
        own_out[i : i + 1, :] = jnp.sum(jnp.where(own, v, 0.0), axis=0, keepdims=True)


def final_kernel(held, own, x_out, r_out):
    sums = []
    for i in range(4):
        h = jnp.concatenate([held[j, 2 * i : 2 * i + 1, :] for j in range(held.shape[0])], 0)
        l = jnp.concatenate([held[j, 2 * i + 1 : 2 * i + 2, :] for j in range(held.shape[0])], 0)
        for axis, shifts in ((0, (4, 2, 1)), (1, (64, 32, 16, 8, 4, 2, 1))):
            for shift in shifts:
                h, l = pair_add((h, l), (pltpu.roll(h, shift, axis), pltpu.roll(l, shift, axis)))
        sums.append((h[:1], l[:1]))
    m0, m1, m2, m3 = sums
    alpha = pair_ratio(m0, m1)
    ratio = pair_ratio(m2, m1)
    v1 = pair_add(m2, minus(pair_product(m1, pair_ratio(m1, m0))))
    v2 = pair_add(m3, minus(pair_product(m2, ratio)))
    scale = pair_product(alpha, ratio)
    alpha0, grow = alpha[0], scale[0]
    alpha1 = (v1[0] + v1[1]) / (v2[0] + v2[1])
    b, image, last = own[0:1, :], own[1:2, :], own[2:3, :]
    x_out[...] = alpha0 * b + alpha1 * (grow * b - alpha0 * image)
    r_out[...] = (b - alpha0 * image) - alpha1 * (grow * image - alpha0 * last)


def exchange(blocks, axes):
    return lax.all_to_all(blocks, axes, 0, 0, tiled=True)


def local(runs, weights, points, high, len_low, len_high, rho, noise):
    n_row, n_sim = lax.axis_size("row"), lax.axis_size("sim")
    at = jnp.stack([lax.axis_index("sim"), lax.axis_index("row")]).astype(jnp.int32)
    high = high.reshape(1, LANES)
    n_runs = n_row * 512
    n_cols = n_row * LANES
    n_rows = n_sim * LANES
    to_row, to_sim, scale_low, scale_high = pl.pallas_call(
        pack_kernel,
        out_shape=(shape((n_row, 32, 640)), shape((n_sim, FEATS, LANES)), shape((FEATS, LANES)), shape((FEATS, LANES))),
        in_specs=[VMEM, VMEM, VMEM, SMEM, SMEM],
        out_specs=(VMEM,) * 4,
        compiler_params=params(16),
        name="pack",
    )(runs, weights.reshape(1, 512), points, len_low, len_high)
    by_row = exchange(to_row, "row")
    by_sim = exchange(to_sim, "sim")
    run_parts, col_parts, weight_cols = pl.pallas_call(
        prep_kernel,
        out_shape=(shape((n_runs, DEPTH), BF16), shape((n_cols, DEPTH), BF16), shape((n_runs, LANES))),
        in_specs=[VMEM] * 3,
        out_specs=(VMEM,) * 3,
        compiler_params=params(20),
        name="prep",
    )(by_row, scale_low, scale_high)
    mu_terms = pl.pallas_call(
        mu_kernel,
        out_shape=shape((n_sim, n_sim, LANES)),
        in_specs=[VMEM] * 5 + [SMEM] * 2,
        out_specs=VMEM,
        scratch_shapes=[pltpu.VMEM((DEPTH, n_rows), BF16), pltpu.VMEM((n_sim, LANES), F32)],
        compiler_params=params(24),
        name="mu",
    )(by_sim, scale_low, run_parts, weight_cols, high, rho, at)
    mu_held = exchange(mu_terms, "sim")
    tile = pl.pallas_call(
        tile_kernel,
        out_shape=shape((n_cols, n_rows)),
        in_specs=[VMEM] * 3,
        out_specs=VMEM,
        scratch_shapes=[pltpu.VMEM((DEPTH, n_rows), BF16)],
        compiler_params=params(28),
        name="tile",
    )(by_sim, scale_high, col_parts)
    image_terms, target, mu = pl.pallas_call(
        first_kernel,
        out_shape=(shape((n_row, n_row, LANES)), shape((n_sim, LANES)), shape((1, LANES))),
        in_specs=[VMEM] * 3 + [SMEM] * 3,
        out_specs=(VMEM,) * 3,
        scratch_shapes=[pltpu.VMEM((n_row, LANES), F32)],
        compiler_params=params(28),
        name="first",
    )(mu_held, tile, high, rho, noise, at)
    image_held = exchange(image_terms, "row")
    last_terms = pl.pallas_call(
        second_kernel,
        out_shape=shape((n_sim, n_sim + 8, LANES)),
        in_specs=[VMEM] * 2 + [SMEM] * 2,
        out_specs=VMEM,
        scratch_shapes=[pltpu.VMEM((n_cols, LANES), F32), pltpu.VMEM((n_sim, LANES), F32)],
        compiler_params=params(28),
        name="second",
    )(image_held, tile, noise, at)
    last_held = exchange(last_terms, "sim")
    moments, own = pl.pallas_call(
        moments_kernel,
        out_shape=(shape((n_row, 8, LANES)), shape((8, LANES))),
        in_specs=[VMEM] * 2 + [SMEM],
        out_specs=(VMEM,) * 2,
        compiler_params=params(16),
        name="moments",
    )(last_held, target, at)
    moments_held = exchange(moments, "row")
    x, r = pl.pallas_call(
        final_kernel,
        out_shape=(shape((1, LANES)), shape((1, LANES))),
        in_specs=[VMEM] * 2,
        out_specs=(VMEM,) * 2,
        compiler_params=params(16),
        name="final",
    )(moments_held, own)
    return mu.reshape(LANES), x.reshape(LANES), r.reshape(LANES)


def solution(mesh):
    placed = (
        P(None, ("row", "sim")),
        P(("row", "sim")),
        P(None, ("row", "sim")),
        P(("row", "sim")),
        P(),
        P(),
        P(),
        P(),
    )
    return jax.shard_map(
        local,
        mesh=mesh,
        in_specs=placed,
        out_specs=(P(("row", "sim")), P(("row", "sim")), P(("row", "sim"))),
        check_vma=False,
    )
```

time: 1150 us -> 140 us (0.12)
  blocking collectives: 518 us -> 56.9 us
  waiting for transfers between devices: 319 us -> 15.6 us
  matrix products: 201 us -> 0 us
  local copies, waits for them, and re-layouts: 76.4 us -> 20.5 us
  Pallas kernels: 0 us -> 27 us
  between operations: 20.1 us -> 2.04 us
  starting transfers between devices: 0.08 us -> 15.9 us
    unnamed x2 -> x0, blocking collectives: 271 us -> none
    psum x3 -> x0, blocking collectives: 225 us -> none  [the longest x2 148 us: squares(): return lax.psum(jnp.sum(vector * vector), ('row', 'sim'))]
    unnamed x3 -> x0, waiting for transfers between devices: 210 us -> none
    dot_general x138 -> x0, matrix products: 201 us -> none  [the longest x72 103 us: kernel_block(): lax.dot_general(piece, col_pts, (((0,), (0,)), ((), ())), precision=lax.P...]
    all_gather x1 -> x0, waiting for transfers between devices: 109 us -> none  [local(): everything = lax.all_gather(hw_points, ('row', 'sim'), axis=1, tiled=True)]
    dynamic_slice x73 -> x0, local copies, waits for them, and re-layouts: 66.9 us -> none  [the longest x64 66.5 us: kernel_apply(): return lax.map(single, row_blocks(row_pts)).reshape(count)]
    all_to_all x0 -> x4, blocking collectives: none -> 56.9 us  [exchange(): return lax.all_to_all(blocks, axes, 0, 0, tiled=True)]
    pallas_call x0 -> x8, Pallas kernels: none -> 27 us  [the longest x1 11 us: local(): pl.pallas_call(mu_kernel, out_shape=shape((n_sim, n_sim, LANES)), in_spec...]
  transfers between devices with their start and end apart: 2 -> 2, of which waited for: 2 -> 2; matrix products, arithmetic and copies ran while one was open for 3% -> 0% of each run, Pallas kernels for 0% -> 4%
where the time goes in v1:
time: 140 us; the launch traced here: 138 us
  blocking collectives  56.9 us (41%)
  Pallas kernels  27 us (19%)
  local copies, waits for them, and re-layouts  20.5 us (15%)
  starting transfers between devices  15.9 us (11%)
  waiting for transfers between devices  15.6 us (11%)
  between operations  2.04 us (1%)
    all_to_all x4, blocking collectives, exchange(): return lax.all_to_all(blocks, axes, 0, 0, tiled=True)  56.9 us
    unnamed x28, local copies, waits for them, and re-layouts  20.5 us
    all_to_all x2, starting transfers between devices, exchange(): return lax.all_to_all(blocks, axes, 0, 0, tiled=True)  15.9 us
    all_to_all x2, waiting for transfers between devices, exchange(): return lax.all_to_all(blocks, axes, 0, 0, tiled=True)  15.6 us
    pallas_call x1, Pallas kernels, local(): pl.pallas_call(mu_kernel, out_shape=shape((n_sim, n_sim, LANES)), in_spec...  11 us
    pallas_call x1, Pallas kernels, local(): pl.pallas_call(tile_kernel, out_shape=shape((n_cols, n_rows)), in_specs=[...  3.85 us
    pallas_call x1, Pallas kernels, local(): pl.pallas_call(second_kernel, out_shape=shape((n_sim, n_sim + 8, LANES)),...  3.62 us
    pallas_call x1, Pallas kernels, local(): pl.pallas_call(first_kernel, out_shape=(shape((n_row, n_row, LANES)), sha...  3.02 us
  transfers between devices with their start and end apart: 2, of which 2 were waited for; matrix products, arithmetic and copies ran while one was open for 0% of the time, Pallas kernels for 4%

profile of v1, /device:TPU:32, one launch (start us, length us, event | category | flops | bytes accessed | tf_op | source)
XLA Modules:
  0.0 138.0 jit_solution(13633513615251791947)
XLA Ops:
  0.7 0.8 copy-done.8
  4.1 1.4 pack.1
  5.5 16.1 %all_to_all.30.held = f32[8,32,640]{2,1,0:T(8,128)S(1)} all-to-all(f32[8,32,640]{2,1,0:T(8,128)S(1)} %get-tuple-element.19), channel_id=1, replica_groups=mesh['row'=8,'sim'=32] {'row'}, dimensions={0} | all-to-all | bytes 1310720 | tf_op jit(solution)/shard_map/all_to_all | solution.py:286
  21.6 11.2 %all-to-all-start = ((f32[32,24,128]{2,1,0:T(8,128)}), f32[32,24,128]{2,1,0:T(8,128)S(1)}, u32[]{:S(2)}, u32[]{:S(2)}) async-start(f32[32,24,128]{2,1,0:T(8,128)} %get-tuple-element.17), calls=%async_computation | async-start | bytes 786432 | tf_op jit(solution)/shard_map/all_to_all | solution.py:286
  33.5 2.1 %prep.1 = (bf16[4096,160]{1,0:T(8,128)(2,1)S(1)}, bf16[1024,160]{1,0:T(8,128)(2,1)S(1)}, f32[4096,128]{1,0:T(8,128)S(1)}) custom-call(f32[8,32,640]{2,1,0:T(8,128)S(1)} %all_to_all.30.held, f32[24,128]{1,0:T(8,128)S(1)} %get-tuple-element.18.scale_low.scale, f32[24,128]{1,0:T(8,128)S(1)} %get-tuple-element.20.scale_high.scale), custom_call_target="tpu_custom_call" | custom-call | tf_op jit(solution)/shard_map/prep/pallas_call | solution.py:306
  35.6 1.3 copy-done.3
  36.9 0.8 copy-done.6
  37.7 9.9 %all-to-all-done.points = f32[32,24,128]{2,1,0:T(8,128)S(1)} async-done(((f32[32,24,128]{2,1,0:T(8,128)}), f32[32,24,128]{2,1,0:T(8,128)S(1)}, u32[]{:S(2)}, u32[]{:S(2)}) %all-to-all-start) | async-done | bytes 393248 | tf_op jit(solution)/shard_map/all_to_all | solution.py:286
  47.6 1.6 %copy-done.4 = f32[4096,128]{1,0:T(8,128)S(1)} copy-done((f32[4096,128]{1,0:T(8,128)S(1)}, f32[4096,128]{1,0:T(8,128)}, u32[]{:S(2)}) %copy-start.4) | copy-done | bytes 2097176
  49.2 11.0 %mu.1 = f32[32,32,128]{2,1,0:T(8,128)S(1)} custom-call(f32[32,24,128]{2,1,0:T(8,128)S(1)} %all-to-all-done.points, f32[24,128]{1,0:T(8,128)S(1)} %get-tuple-element.18.scale_low.scale, bf16[4096,160]{1,0:T(8,128)(2,1)S(1)} %get-tuple-element.21.runs, f32[4096,128]{1,0:T(8,128)S(1)} %copy-done.4, f32[1,128]{1,0:T(1,128)S(1)} %bitcast.7, f32[1]{0:T(128)S(6)} %copy.11.rho, ...), custom_call_target="tpu_custom_call" | custom-call | tf_op jit(solution)/shard_map/mu/pallas_call | solution.py:314
  60.2 0.8 copy-done.5
  61.0 4.7 %all-to-all-start.2 = ((f32[32,32,128]{2,1,0:T(8,128)}), f32[32,32,128]{2,1,0:T(8,128)S(1)}, u32[]{:S(2)}, u32[]{:S(2)}) async-start(f32[32,32,128]{2,1,0:T(8,128)} %copy-done.5), calls=%async_computation.2 | async-start | bytes 1048576 | tf_op jit(solution)/shard_map/all_to_all | solution.py:286
  66.3 1.0 copy-done.7
  67.4 3.8 %tile.1 = f32[1024,4096]{1,0:T(8,128)S(1)} custom-call(f32[32,24,128]{2,1,0:T(8,128)S(1)} %all-to-all-done.points, f32[24,128]{1,0:T(8,128)S(1)} %get-tuple-element.20.scale_high.scale, bf16[1024,160]{1,0:T(8,128)(2,1)S(1)} %copy-done.7), custom_call_target="tpu_custom_call" | custom-call | tf_op jit(solution)/shard_map/tile/pallas_call | solution.py:324
  71.2 5.7 %copy-done = f32[1024,4096]{1,0:T(8,128)} copy-done((f32[1024,4096]{1,0:T(8,128)}, f32[1024,4096]{1,0:T(8,128)S(1)}, u32[]{:S(2)}) %copy-start) | copy-done | bytes 16777240
  77.0 5.7 %all-to-all-done.2.held = f32[32,32,128]{2,1,0:T(8,128)S(1)} async-done(((f32[32,32,128]{2,1,0:T(8,128)}), f32[32,32,128]{2,1,0:T(8,128)S(1)}, u32[]{:S(2)}, u32[]{:S(2)}) %all-to-all-start.2) | async-done | bytes 524320 | tf_op jit(solution)/shard_map/all_to_all | solution.py:286
  82.7 5.8 %copy-done.1 = f32[1024,4096]{1,0:T(8,128)S(1)} copy-done((f32[1024,4096]{1,0:T(8,128)S(1)}, f32[1024,4096]{1,0:T(8,128)}, u32[]{:S(2)}) %copy-start.1) | copy-done | bytes 16777240
  88.5 3.0 %first.1 = (f32[8,8,128]{2,1,0:T(8,128)S(1)}, f32[32,128]{1,0:T(8,128)S(1)}, f32[1,128]{1,0:T(1,128)}) custom-call(f32[32,32,128]{2,1,0:T(8,128)S(1)} %all-to-all-done.2.held, f32[1024,4096]{1,0:T(8,128)S(1)} %copy-done.1, f32[1,128]{1,0:T(1,128)S(1)} %bitcast.8, f32[1]{0:T(128)S(6)} %copy.11.rho, f32[1]{0:T(128)S(6)} %copy.12.noise, s32[2]{0:T(128)S(1)} %pad_add_fusion.at), custom_call_target="tpu_custom_call" | custom-call | tf_op jit(solution)/shard_map/first/pallas_call | solution.py:333
  91.5 8.2 %all_to_all.31.held = f32[8,8,128]{2,1,0:T(8,128)S(1)} all-to-all(f32[8,8,128]{2,1,0:T(8,128)S(1)} %get-tuple-element.25), channel_id=1, replica_groups=mesh['row'=8,'sim'=32] {'row'}, dimensions={0} | all-to-all | bytes 65536 | tf_op jit(solution)/shard_map/all_to_all | solution.py:286
  99.7 3.6 %second.1 = f32[32,40,128]{2,1,0:T(8,128)S(1)} custom-call(f32[8,8,128]{2,1,0:T(8,128)S(1)} %all_to_all.31.held, f32[1024,4096]{1,0:T(8,128)S(1)} %copy-done.2, f32[1]{0:T(128)S(6)} %copy.12.noise, s32[2]{0:T(128)S(1)} %pad_add_fusion.at), custom_call_target="tpu_custom_call" | custom-call | tf_op jit(solution)/shard_map/second/pallas_call | solution.py:343
  103.3 24.9 %all_to_all.32.held = f32[32,40,128]{2,1,0:T(8,128)S(1)} all-to-all(f32[32,40,128]{2,1,0:T(8,128)S(1)} %second.1), channel_id=1, replica_groups=mesh['row'=8,'sim'=32] {'sim'}, dimensions={0} | all-to-all | bytes 1310720 | tf_op jit(solution)/shard_map/all_to_all | solution.py:286
  128.2 0.9 moments.1
  129.1 7.8 %all_to_all.33.held = f32[8,8,128]{2,1,0:T(8,128)S(1)} all-to-all(f32[8,8,128]{2,1,0:T(8,128)S(1)} %get-tuple-element.27), channel_id=1, replica_groups=mesh['row'=8,'sim'=32] {'row'}, dimensions={0} | all-to-all | bytes 65536 | tf_op jit(solution)/shard_map/all_to_all | solution.py:286
  136.9 1.2 final.1
  (21 shorter events, 2.8 us)
Async XLA Ops:
  0.6 46.9 %copy-start.10 = (f32[128]{0:T(128)S(1)}, f32[128]{0:T(128)}, u32[]{:S(2)}) copy-start(f32[128]{0:T(128)} %param.11) | copy-start | bytes 1540
  0.6 0.8 copy-start.8
  1.4 0.7 copy-start.9
  2.2 0.7 copy-start.11
  2.8 0.7 copy-start.12
  3.5 0.7 copy-start.13
  21.6 26.0 %all-to-all-start = ((f32[32,24,128]{2,1,0:T(8,128)}), f32[32,24,128]{2,1,0:T(8,128)S(1)}, u32[]{:S(2)}, u32[]{:S(2)}) async-start(f32[32,24,128]{2,1,0:T(8,128)} %get-tuple-element.17), calls=%async_computation | async-start | bytes 786432 | tf_op jit(solution)/shard_map/all_to_all | solution.py:286
  35.6 1.3 copy-start.3
  36.9 0.8 copy-start.6
  47.6 1.6 %copy-start.4 = (f32[4096,128]{1,0:T(8,128)S(1)}, f32[4096,128]{1,0:T(8,128)}, u32[]{:S(2)}) copy-start(f32[4096,128]{1,0:T(8,128)} %copy-done.3) | copy-start | bytes 6291460
  60.2 0.8 copy-start.5
  61.0 21.7 %all-to-all-start.2 = ((f32[32,32,128]{2,1,0:T(8,128)}), f32[32,32,128]{2,1,0:T(8,128)S(1)}, u32[]{:S(2)}, u32[]{:S(2)}) async-start(f32[32,32,128]{2,1,0:T(8,128)} %copy-done.5), calls=%async_computation.2 | async-start | bytes 1048576 | tf_op jit(solution)/shard_map/all_to_all | solution.py:286
  66.3 1.0 copy-start.7
  71.2 5.7 %copy-start = (f32[1024,4096]{1,0:T(8,128)}, f32[1024,4096]{1,0:T(8,128)S(1)}, u32[]{:S(2)}) copy-start(f32[1024,4096]{1,0:T(8,128)S(1)} %tile.1) | copy-start | bytes 50331652
  82.7 5.8 %copy-start.1 = (f32[1024,4096]{1,0:T(8,128)S(1)}, f32[1024,4096]{1,0:T(8,128)}, u32[]{:S(2)}) copy-start(f32[1024,4096]{1,0:T(8,128)} %copy-done) | copy-start | bytes 50331652
  88.5 11.2 %copy-start.2 = (f32[1024,4096]{1,0:T(8,128)S(1)}, f32[1024,4096]{1,0:T(8,128)}, u32[]{:S(2)}) copy-start(f32[1024,4096]{1,0:T(8,128)} %copy-done) | copy-start | bytes 50331652

commit v2 on v1

v2 whole, which is shorter than its diff:
```python
import math

import jax
import jax.numpy as jnp
from jax import lax
from jax.experimental import pallas as pl
from jax.experimental.pallas import tpu as pltpu
from jax.sharding import Mesh
from jax.sharding import PartitionSpec as P

F32 = jnp.float32
BF16 = jnp.bfloat16
FEATS = 24
LANES = 128
RUN_BLOCKS = 4
WIDE = CHUNK = 512
PACKED = RUN_BLOCKS * FEATS + FEATS + 8
DEPTH = 160
ROOT = math.sqrt(math.log2(math.e))
VMEM = pl.BlockSpec(memory_space=pltpu.VMEM)
AXES = ("y", "core", "x", "z")
ROWS = ("core", "z")
COLS = ("y", "x")
HBM = pl.BlockSpec(memory_space=pltpu.HBM)
SMEM = pl.BlockSpec(memory_space=pltpu.SMEM)


def params(mib):
    return pltpu.CompilerParams(vmem_limit_bytes=mib * 1024 * 1024)


def shape(dims, kind=F32):
    return jax.ShapeDtypeStruct(dims, kind)


def split(x):
    high = x.astype(BF16).astype(F32)
    rest = x - high
    mid = rest.astype(BF16).astype(F32)
    return high, mid, rest - mid


def norm_rows(norm, at):
    high, mid, low = split(norm)
    row = lax.broadcasted_iota(jnp.int32, (8, norm.shape[1]), 0)
    ones = jnp.where((row >= 3 - at) & (row < 6 - at), 1.0, 0.0)
    return jnp.where(row == at, high, jnp.where(row == at + 1, mid, jnp.where(row == at + 2, low, ones)))


def scaled(points, scale):
    return (points - 0.5) * scale


def half_norm(points):
    return -0.5 * jnp.sum(points * points, axis=0, keepdims=True)


def left(points, scale):
    u = scaled(points, scale)
    high, mid, low = split(u)
    norms = norm_rows(half_norm(u), 0)
    return jnp.concatenate([high, high, high, mid, mid, low, norms, jnp.zeros_like(norms)], 0).astype(BF16)


def right(points, scale):
    v = scaled(points, scale)
    high, mid, low = split(v)
    norms = norm_rows(half_norm(v), 3)
    return jnp.concatenate([high, mid, low, high, mid, high, norms, jnp.zeros_like(norms)], 0)


def pack_kernel(*refs):
    sources, (out_col, out_row, scale_low, scale_high), held, sems = refs[:5], refs[5:9], refs[9:14], refs[14]
    copies = [pltpu.make_async_copy(a, b, sems.at[i]) for i, (a, b) in enumerate(zip(sources, held))]
    for copy in copies:
        copy.start()
    for copy in copies:
        copy.wait()
    runs, weights, points, len_low, len_high = held
    row = lax.broadcasted_iota(jnp.int32, (FEATS, LANES), 0)
    for lengths, out in ((len_low, scale_low), (len_high, scale_high)):
        column = jnp.ones((FEATS, LANES), F32)
        for i in range(FEATS):
            column = jnp.where(row == i, lengths[i], column)
        out[...] = ROOT / column
    own = points[...]
    for i in range(out_row.shape[0]):
        out_row[i] = own
    last = jnp.broadcast_to(weights[:, :LANES], (8, LANES))
    row = lax.broadcasted_iota(jnp.int32, (8, LANES), 0)
    for q in range(1, RUN_BLOCKS):
        last = jnp.where(row == q, weights[:, q * LANES : (q + 1) * LANES], last)
    for i in range(out_col.shape[0]):
        for q in range(RUN_BLOCKS):
            out_col[i, q * FEATS : (q + 1) * FEATS, :] = runs[:, q * LANES : (q + 1) * LANES]
        out_col[i, RUN_BLOCKS * FEATS : PACKED - 8, :] = own
        out_col[i, PACKED - 8 :, :] = last


def prep_kernel(held, scale_low, scale_high, runs_out, cols_out, weights_out):
    def step(r, carry):
        for q in range(RUN_BLOCKS):
            rows = pl.ds(pl.multiple_of((r * RUN_BLOCKS + q) * LANES, LANES), LANES)
            runs_out[rows, :] = right(held[r, q * FEATS : (q + 1) * FEATS, :], scale_low[...]).T.astype(BF16)
        weights_out[pl.ds(pl.multiple_of(r * 8, 8), 8), :] = held[r, PACKED - 8 :, :]
        rows = pl.ds(pl.multiple_of(r * LANES, LANES), LANES)
        cols_out[rows, :] = right(held[r, RUN_BLOCKS * FEATS : PACKED - 8, :], scale_high[...]).T.astype(BF16)
        return carry

    lax.fori_loop(0, held.shape[0], step, 0)


def column_of(line, out, rows):
    out[rows, :] = jnp.broadcast_to(line, (LANES, LANES)).T


def weighted(cols, rows, column):
    term = jnp.exp2(jnp.dot(cols, rows, preferred_element_type=F32))
    count, wide = term.shape
    term = term * jnp.concatenate([column] * (wide // LANES), 1)
    return jnp.sum(term.reshape(count // 8, 8, wide), axis=0)


def build_left(points, scale, out):
    def step(g, carry):
        for q in range(8):
            k = g * 8 + q
            out[:, pl.ds(pl.multiple_of(k * LANES, LANES), LANES)] = left(points[k], scale[...])
        return carry

    lax.fori_loop(0, points.shape[0] // 8, step, 0)


def mu_kernel(points, scale, runs_hbm, weights, high, rho, at, out, parts, runs, column, total, sems):
    pieces = sems.shape[0]
    size = runs.shape[0] // pieces
    blocks = size // (RUN_BLOCKS * LANES)

    def copy(i):
        rows = pl.ds(pl.multiple_of(i * size, size), size)
        return pltpu.make_async_copy(runs_hbm.at[rows, :], runs.at[rows, :], sems.at[i])

    for i in range(pieces):
        copy(i).start()
    build_left(points, scale, parts)
    total[...] = jnp.zeros_like(total)

    def step(i, carry):
        copy(i).wait()
        for r in range(blocks):
            lines = weights[pl.ds(pl.multiple_of((i * blocks + r) * 8, 8), 8), :]
            for q in range(RUN_BLOCKS):
                first = (r * RUN_BLOCKS + q) * LANES
                column_of(lines[q : q + 1, :], column, slice(first, first + LANES))
        for c in range(0, parts.shape[1], WIDE):
            acc = total[:, c : c + WIDE]
            for j in range(0, size, CHUNK):
                rows = pl.ds(pl.multiple_of(i * size + j, CHUNK), CHUNK)
                acc = acc + weighted(runs[rows, :], parts[:, c : c + WIDE], column[j : j + CHUNK, :])
            total[:, c : c + WIDE] = acc
        return carry

    lax.fori_loop(0, pieces, step, 0)
    mu = lines_of(total)
    row = lax.broadcasted_iota(jnp.int32, mu.shape, 0)
    target = -rho[0] * mu
    target = jnp.where(row == at[0], target + high[...], target)
    for i in range(out.shape[0]):
        out[i] = jnp.where(row == i, mu, target)


def lines_of(total):
    line = jnp.sum(total[...], axis=0, keepdims=True)
    return jnp.concatenate([line[:, k : k + LANES] for k in range(0, line.shape[1], LANES)], 0)


def sides_kernel(points, scale, out):
    build_left(points, scale, out)


def first_kernel(held, rows_in, cols_in, high, rho, noise, at, out, target_out, mu_out, sums):
    total = jnp.sum(held[...], axis=0)
    row = lax.broadcasted_iota(jnp.int32, total.shape, 0)
    own = row == at[0]
    target = jnp.where(own, high[...] - rho[0] * total, total)
    target_out[...] = target
    mu_out[...] = jnp.sum(jnp.where(own, total, 0.0), axis=0, keepdims=True)
    own_target = jnp.sum(jnp.where(own, target, 0.0), axis=0, keepdims=True)
    size = 2 * LANES

    def step(k, carry):
        cols = cols_in[pl.ds(pl.multiple_of(k * size, size), size), :]
        acc = jnp.zeros((size, LANES), F32)
        for c in range(0, rows_in.shape[1], WIDE):
            term = jnp.exp2(jnp.dot(cols, rows_in[:, c : c + WIDE], preferred_element_type=F32))
            for q in range(0, WIDE, LANES):
                s = (c + q) // LANES
                acc = acc + term[:, q : q + LANES] * target_out[s : s + 1, :]
        for q in range(2):
            block = acc[q * LANES : (q + 1) * LANES, :]
            sums[pl.ds(k * 2 + q, 1), :] = jnp.sum(block.T, axis=0, keepdims=True)
        return carry

    lax.fori_loop(0, cols_in.shape[0] // size, step, 0)
    image = sums[...]
    image = jnp.where(lax.broadcasted_iota(jnp.int32, image.shape, 0) == at[1], image + noise[0] * own_target, image)
    for i in range(out.shape[0]):
        out[i] = image


def second_kernel(held, rows_in, cols_in, noise, at, out, column, total):
    image = jnp.sum(held[...], axis=0)
    mine = lax.broadcasted_iota(jnp.int32, image.shape, 0) == at[1]
    own = jnp.sum(jnp.where(mine, image, 0.0), axis=0, keepdims=True)
    for k in range(image.shape[0]):
        column_of(image[k : k + 1, :], column, slice(k * LANES, (k + 1) * LANES))
    total[...] = jnp.zeros_like(total)

    def step(i, carry):
        rows = pl.ds(pl.multiple_of(i * CHUNK, CHUNK), CHUNK)
        for c in range(0, rows_in.shape[1], WIDE):
            total[:, c : c + WIDE] += weighted(cols_in[rows, :], rows_in[:, c : c + WIDE], column[rows, :])
        return carry

    lax.fori_loop(0, cols_in.shape[0] // CHUNK, step, 0)
    last = lines_of(total)
    row = lax.broadcasted_iota(jnp.int32, last.shape, 0)
    last = jnp.where(row == at[0], last + noise[0] * own, last)
    extra = jnp.broadcast_to(own, (8, LANES))
    for i in range(out.shape[0]):
        out[i, : last.shape[0], :] = last
        out[i, last.shape[0] :, :] = extra


def two_sum(a, b):
    s = a + b
    t = s - a
    return s, (a - (s - t)) + (b - t)


def pair_add(x, y):
    s, e = two_sum(x[0], y[0])
    return two_sum(s, e + (x[1] + y[1]))


def product(a, b):
    ah = a.astype(BF16).astype(F32)
    bh = b.astype(BF16).astype(F32)
    al, bl = a - ah, b - bh
    s, e = two_sum(ah * bh, ah * bl + al * bh)
    return two_sum(s, e + al * bl)


def pair_product(x, y):
    s, e = product(x[0], y[0])
    return two_sum(s, e + (x[0] * y[1] + x[1] * y[0]))


def minus(x):
    return -x[0], -x[1]


def pair_ratio(x, y):
    q = x[0] / y[0]
    rest = pair_add(x, minus(pair_product((q, jnp.zeros_like(q)), y)))
    return two_sum(q, (rest[0] + rest[1]) / y[0])


def fold_rows(x):
    high, low = x
    count = high.shape[0]
    while count > 8:
        count //= 2
        high, low = pair_add((high[:count], low[:count]), (high[count:], low[count:]))
    return high, low


def moments_kernel(held, target, at, out, own_out):
    count = target.shape[0]
    last = jnp.sum(held[:, :count, :], axis=0)
    image = held[:, count, :]
    b = target[...]
    for i, (p, q) in enumerate(((b, b), (b, image), (image, image), (image, last))):
        high, low = fold_rows(product(p, q))
        for shift in (4, 2, 1):
            high, low = pair_add((high, low), (pltpu.roll(high, shift, 0), pltpu.roll(low, shift, 0)))
        for j in range(out.shape[0]):
            out[j, 2 * i : 2 * i + 1, :] = high[:1]
            out[j, 2 * i + 1 : 2 * i + 2, :] = low[:1]
    own = lax.broadcasted_iota(jnp.int32, b.shape, 0) == at[0]
    for i, v in enumerate((b, image, last)):
        own_out[i : i + 1, :] = jnp.sum(jnp.where(own, v, 0.0), axis=0, keepdims=True)


def final_kernel(held, own, x_out, r_out):
    sums = []
    for i in range(4):
        h = jnp.concatenate([held[j, 2 * i : 2 * i + 1, :] for j in range(held.shape[0])], 0)
        l = jnp.concatenate([held[j, 2 * i + 1 : 2 * i + 2, :] for j in range(held.shape[0])], 0)
        h, l = fold_rows((h, l))
        for axis, shifts in ((0, (4, 2, 1)), (1, (64, 32, 16, 8, 4, 2, 1))):
            for shift in shifts:
                h, l = pair_add((h, l), (pltpu.roll(h, shift, axis), pltpu.roll(l, shift, axis)))
        sums.append((h[:1], l[:1]))
    m0, m1, m2, m3 = sums
    alpha = pair_ratio(m0, m1)
    ratio = pair_ratio(m2, m1)
    v1 = pair_add(m2, minus(pair_product(m1, pair_ratio(m1, m0))))
    v2 = pair_add(m3, minus(pair_product(m2, ratio)))
    scale = pair_product(alpha, ratio)
    alpha0, grow = alpha[0], scale[0]
    alpha1 = (v1[0] + v1[1]) / (v2[0] + v2[1])
    b, image, last = own[0:1, :], own[1:2, :], own[2:3, :]
    x_out[...] = alpha0 * b + alpha1 * (grow * b - alpha0 * image)
    r_out[...] = (b - alpha0 * image) - alpha1 * (grow * image - alpha0 * last)


def exchange(blocks, axes):
    return lax.all_to_all(blocks, axes, 0, 0, tiled=True)


def local(runs, weights, points, high, len_low, len_high, rho, noise):
    n_row, n_col = lax.axis_size(ROWS), lax.axis_size(COLS)
    at = jnp.stack([lax.axis_index(ROWS), lax.axis_index(COLS)]).astype(jnp.int32)
    high = high.reshape(1, LANES)
    runs_len, cols_len, rows_len = n_col * RUN_BLOCKS * LANES, n_col * LANES, n_row * LANES
    to_col, to_row, scale_low, scale_high = pl.pallas_call(
        pack_kernel,
        out_shape=(shape((n_col, PACKED, LANES)), shape((n_row, FEATS, LANES)), shape((FEATS, LANES)), shape((FEATS, LANES))),
        in_specs=[HBM] * 5,
        out_specs=(VMEM,) * 4,
        scratch_shapes=[
            pltpu.VMEM((FEATS, RUN_BLOCKS * LANES), F32),
            pltpu.VMEM((1, RUN_BLOCKS * LANES), F32),
            pltpu.VMEM((FEATS, LANES), F32),
            pltpu.SMEM((FEATS,), F32),
            pltpu.SMEM((FEATS,), F32),
            pltpu.SemaphoreType.DMA((5,)),
        ],
        compiler_params=params(60),
        name="pack",
    )(runs, weights.reshape(1, RUN_BLOCKS * LANES), points, len_low, len_high)
    by_col = exchange(to_col, COLS)
    by_row = exchange(to_row, ROWS)
    run_parts, col_parts, weight_lines = pl.pallas_call(
        prep_kernel,
        out_shape=(shape((runs_len, DEPTH), BF16), shape((cols_len, DEPTH), BF16), shape((n_col * 8, LANES))),
        in_specs=[VMEM] * 3,
        out_specs=(VMEM,) * 3,
        compiler_params=params(60),
        name="prep",
    )(by_col, scale_low, scale_high)
    mu_terms = pl.pallas_call(
        mu_kernel,
        out_shape=shape((n_row, n_row, LANES)),
        in_specs=[VMEM, VMEM, HBM, VMEM, VMEM, SMEM, SMEM],
        out_specs=VMEM,
        scratch_shapes=[
            pltpu.VMEM((DEPTH, rows_len), BF16),
            pltpu.VMEM((runs_len, DEPTH), BF16),
            pltpu.VMEM((runs_len // 8, LANES), F32),
            pltpu.VMEM((8, rows_len), F32),
            pltpu.SemaphoreType.DMA((8,)),
        ],
        compiler_params=params(60),
        name="mu",
    )(by_row, scale_low, run_parts, weight_lines, high, rho, at)
    mu_held = exchange(mu_terms, ROWS)
    row_parts = pl.pallas_call(
        sides_kernel,
        out_shape=shape((DEPTH, rows_len), BF16),
        in_specs=[VMEM] * 2,
        out_specs=VMEM,
        compiler_params=params(4),
        name="sides",
    )(by_row, scale_high)
    image_terms, target, mu = pl.pallas_call(
        first_kernel,
        out_shape=(shape((n_col, n_col, LANES)), shape((n_row, LANES)), shape((1, LANES))),
        in_specs=[VMEM] * 4 + [SMEM] * 3,
        out_specs=(VMEM,) * 3,
        scratch_shapes=[pltpu.VMEM((n_col, LANES), F32)],
        compiler_params=params(4),
        name="first",
    )(mu_held, row_parts, col_parts, high, rho, noise, at)
    image_held = exchange(image_terms, COLS)
    last_terms = pl.pallas_call(
        second_kernel,
        out_shape=shape((n_row, n_row + 8, LANES)),
        in_specs=[VMEM] * 3 + [SMEM] * 2,
        out_specs=VMEM,
        scratch_shapes=[pltpu.VMEM((cols_len, LANES), F32), pltpu.VMEM((8, rows_len), F32)],
        compiler_params=params(8),
        name="second",
    )(image_held, row_parts, col_parts, noise, at)
    last_held = exchange(last_terms, ROWS)
    moments, own = pl.pallas_call(
        moments_kernel,
        out_shape=(shape((n_col, 8, LANES)), shape((8, LANES))),
        in_specs=[VMEM] * 2 + [SMEM],
        out_specs=(VMEM,) * 2,
        compiler_params=params(4),
        name="moments",
    )(last_held, target, at)
    moments_held = exchange(moments, COLS)
    x, r = pl.pallas_call(
        final_kernel,
        out_shape=(shape((1, LANES)), shape((1, LANES))),
        in_specs=[VMEM] * 2,
        out_specs=(VMEM,) * 2,
        compiler_params=params(4),
        name="final",
    )(moments_held, own)
    return mu.reshape(LANES), x.reshape(LANES), r.reshape(LANES)


def solution(mesh):
    spread = P(AXES)
    wide = P(None, AXES)
    fine = Mesh(mesh.devices.reshape(4, 2, 4, 8), AXES)
    return jax.shard_map(
        local,
        mesh=fine,
        in_specs=(wide, spread, wide, spread, P(), P(), P(), P()),
        out_specs=(spread,) * 3,
        check_vma=False,
    )
```

time: 140 us -> 118 us (0.84); the launches traced: 138 us -> 117 us
  local copies, waits for them, and re-layouts: 20.5 us -> 1.63 us
  waiting for transfers between devices: 15.6 us -> 8.18 us
  Pallas kernels: 27 us -> 32 us
  blocking collectives: 56.9 us -> 59 us
  starting transfers between devices: 15.9 us -> 14 us
    unnamed x28 -> x12, local copies, waits for them, and re-layouts: 20.5 us -> 1.63 us
    all_to_all x2, waiting for transfers between devices: 15.6 us -> 8.18 us  [exchange(): return lax.all_to_all(blocks, axes, 0, 0, tiled=True)]
    pallas_call x7, Pallas kernels: 25.8 us -> 30.8 us  [the longest x1 13 us: local(): pl.pallas_call(mu_kernel, out_shape=shape((n_row, n_row, LANES)), in_spec...]
    all_to_all x4, blocking collectives: 56.9 us -> 59 us  [exchange(): return lax.all_to_all(blocks, axes, 0, 0, tiled=True)]
    all_to_all x2, starting transfers between devices: 15.9 us -> 14 us  [exchange(): return lax.all_to_all(blocks, axes, 0, 0, tiled=True)]
  transfers between devices with their start and end apart: 2 -> 2, of which waited for: 2 -> 2; matrix products, arithmetic and copies ran while one was open for 0% -> 0% of each run, Pallas kernels for 4% -> 6%
where the time goes in v2:
time: 118 us; the launch traced here: 117 us
  blocking collectives  59 us (50%)
  Pallas kernels  32 us (27%)
  starting transfers between devices  14 us (12%)
  waiting for transfers between devices  8.18 us (7%)
  between operations  2.02 us (2%)
  local copies, waits for them, and re-layouts  1.63 us (1%)
    all_to_all x4, blocking collectives, exchange(): return lax.all_to_all(blocks, axes, 0, 0, tiled=True)  59 us
    all_to_all x2, starting transfers between devices, exchange(): return lax.all_to_all(blocks, axes, 0, 0, tiled=True)  14 us
    pallas_call x1, Pallas kernels, local(): pl.pallas_call(mu_kernel, out_shape=shape((n_row, n_row, LANES)), in_spec...  13 us
    all_to_all x2, waiting for transfers between devices, exchange(): return lax.all_to_all(blocks, axes, 0, 0, tiled=True)  8.18 us
    pallas_call x1, Pallas kernels, local(): pl.pallas_call(prep_kernel, out_shape=(shape((runs_len, DEPTH), BF16), sh...  6.6 us
    pallas_call x1, Pallas kernels, local(): pl.pallas_call(first_kernel, out_shape=(shape((n_col, n_col, LANES)), sha...  4.63 us
    pallas_call x1, Pallas kernels, local(): pl.pallas_call(second_kernel, out_shape=shape((n_row, n_row + 8, LANES)),...  3.72 us
  transfers between devices with their start and end apart: 2, of which 2 were waited for; matrix products, arithmetic and copies ran while one was open for 0% of the time, Pallas kernels for 6%

profile of v2, /device:TPU:32, one launch (start us, length us, event | category | flops | bytes accessed | tf_op | source)
XLA Modules:
  0.0 117.5 jit_solution(5785540391606951933)
XLA Ops:
  0.6 2.0 %pack.1 = (f32[16,128,128]{2,1,0:T(8,128)}, f32[16,24,128]{2,1,0:T(8,128)}, f32[24,128]{1,0:T(8,128)}, f32[24,128]{1,0:T(8,128)}) custom-call(f32[24,512]{1,0:T(8,128)} %refs_0_.1, f32[1,512]{1,0:T(1,128)} %bitcast.9, f32[24,128]{1,0:T(8,128)} %refs_2_.1, f32[24]{0:T(128)} %refs_3_.1, f32[24]{0:T(128)} %refs_4_.1), custom_call_target="tpu_custom_call" | custom-call | tf_op jit(solution)/shard_map/pack/pallas_call | solution.py:327
  2.7 0.0 copy-start.3
  2.7 0.0 copy-start.5
  2.7 24.3 %all_to_all.30.held = f32[16,128,128]{2,1,0:T(8,128)} all-to-all(f32[16,128,128]{2,1,0:T(8,128)} %get-tuple-element.19), channel_id=1, replica_groups=mesh['y'=4,'core'=2,'x'=4,'z'=8] {'y','x'}, dimensions={0} | all-to-all | bytes 2097152 | tf_op jit(solution)/shard_map/all_to_all | solution.py:319
  27.0 8.6 %all-to-all-start = ((f32[16,24,128]{2,1,0:T(8,128)}), f32[16,24,128]{2,1,0:T(8,128)S(1)}, u32[]{:S(2)}, u32[]{:S(2)}) async-start(f32[16,24,128]{2,1,0:T(8,128)} %get-tuple-element.17), calls=%async_computation | async-start | bytes 393216 | tf_op jit(solution)/shard_map/all_to_all | solution.py:319
  36.2 0.6 pad_add_fusion.at
  36.8 6.6 %prep.1 = (bf16[8192,160]{1,0:T(8,128)(2,1)}, bf16[2048,160]{1,0:T(8,128)(2,1)}, f32[128,128]{1,0:T(8,128)}) custom-call(f32[16,128,128]{2,1,0:T(8,128)} %all_to_all.30.held, f32[24,128]{1,0:T(8,128)} %get-tuple-element.18.scale_low.scale, f32[24,128]{1,0:T(8,128)} %get-tuple-element.20.scale_high.scale), custom_call_target="tpu_custom_call" | custom-call | tf_op jit(solution)/shard_map/prep/pallas_call | solution.py:345
  43.4 1.8 %all-to-all-done.points = f32[16,24,128]{2,1,0:T(8,128)S(1)} async-done(((f32[16,24,128]{2,1,0:T(8,128)}), f32[16,24,128]{2,1,0:T(8,128)S(1)}, u32[]{:S(2)}, u32[]{:S(2)}) %all-to-all-start) | async-done | bytes 196640 | tf_op jit(solution)/shard_map/all_to_all | solution.py:319
  45.2 0.7 copy-done.1
  45.9 13.0 %mu.1 = f32[16,16,128]{2,1,0:T(8,128)} custom-call(f32[16,24,128]{2,1,0:T(8,128)} %copy-done.1, f32[24,128]{1,0:T(8,128)} %get-tuple-element.18.scale_low.scale, bf16[8192,160]{1,0:T(8,128)(2,1)} %get-tuple-element.21.runs_hbm, f32[128,128]{1,0:T(8,128)} %get-tuple-element.22.weights, f32[1,128]{1,0:T(1,128)} %bitcast.7, f32[1]{0:T(128)S(6)} %copy.11.rho, ...), custom_call_target="tpu_custom_call" | custom-call | tf_op jit(solution)/shard_map/mu/pallas_call | solution.py:353
  58.8 5.5 %all-to-all-start.2 = ((f32[16,16,128]{2,1,0:T(8,128)}), f32[16,16,128]{2,1,0:T(8,128)S(1)}, u32[]{:S(2)}, u32[]{:S(2)}) async-start(f32[16,16,128]{2,1,0:T(8,128)} %mu.1), calls=%async_computation.2 | async-start | bytes 262144 | tf_op jit(solution)/shard_map/all_to_all | solution.py:319
  65.0 0.0 copy-done.3
  65.0 0.0 copy-start.2
  65.0 0.9 copy-done.2
  65.9 0.2 sides.1.rows_in
  66.1 6.4 %all-to-all-done.2.held = f32[16,16,128]{2,1,0:T(8,128)S(1)} async-done(((f32[16,16,128]{2,1,0:T(8,128)}), f32[16,16,128]{2,1,0:T(8,128)S(1)}, u32[]{:S(2)}, u32[]{:S(2)}) %all-to-all-start.2) | async-done | bytes 131104 | tf_op jit(solution)/shard_map/all_to_all | solution.py:319
  72.5 0.0 copy-done
  72.5 4.6 %first.1 = (f32[16,16,128]{2,1,0:T(8,128)S(1)}, f32[16,128]{1,0:T(8,128)S(1)}, f32[1,128]{1,0:T(1,128)}) custom-call(f32[16,16,128]{2,1,0:T(8,128)S(1)} %all-to-all-done.2.held, bf16[160,2048]{1,0:T(8,128)(2,1)S(1)} %sides.1.rows_in, bf16[2048,160]{1,0:T(8,128)(2,1)S(1)} %copy-done, f32[1,128]{1,0:T(1,128)S(1)} %bitcast.8, f32[1]{0:T(128)S(6)} %copy.11.rho, ...), custom_call_target="tpu_custom_call" | custom-call | tf_op jit(solution)/shard_map/first/pallas_call | solution.py:377
  77.2 11.0 %all_to_all.31.held = f32[16,16,128]{2,1,0:T(8,128)S(1)} all-to-all(f32[16,16,128]{2,1,0:T(8,128)S(1)} %get-tuple-element.25), channel_id=1, replica_groups=mesh['y'=4,'core'=2,'x'=4,'z'=8] {'y','x'}, dimensions={0} | all-to-all | bytes 262144 | tf_op jit(solution)/shard_map/all_to_all | solution.py:319
  88.1 3.7 %second.1 = f32[16,24,128]{2,1,0:T(8,128)S(1)} custom-call(f32[16,16,128]{2,1,0:T(8,128)S(1)} %all_to_all.31.held, bf16[160,2048]{1,0:T(8,128)(2,1)S(1)} %sides.1.rows_in, bf16[2048,160]{1,0:T(8,128)(2,1)S(1)} %copy-done, f32[1]{0:T(128)S(6)} %copy.12.noise, s32[2]{0:T(128)S(1)} %copy-done.4), custom_call_target="tpu_custom_call" | custom-call | tf_op jit(solution)/shard_map/second/pallas_call | solution.py:387
  91.9 13.0 %all_to_all.32.held = f32[16,24,128]{2,1,0:T(8,128)S(1)} all-to-all(f32[16,24,128]{2,1,0:T(8,128)S(1)} %second.1), channel_id=1, replica_groups=mesh['y'=4,'core'=2,'x'=4,'z'=8] {'core','z'}, dimensions={0} | all-to-all | bytes 393216 | tf_op jit(solution)/shard_map/all_to_all | solution.py:319
  104.8 0.7 moments.1
  105.5 10.7 %all_to_all.33.held = f32[16,8,128]{2,1,0:T(8,128)S(1)} all-to-all(f32[16,8,128]{2,1,0:T(8,128)S(1)} %get-tuple-element.27), channel_id=1, replica_groups=mesh['y'=4,'core'=2,'x'=4,'z'=8] {'y','x'}, dimensions={0} | all-to-all | bytes 131072 | tf_op jit(solution)/shard_map/all_to_all | solution.py:319
  116.3 1.2 %final.1 = (f32[1,128]{1,0:T(1,128)}, f32[1,128]{1,0:T(1,128)}) custom-call(f32[16,8,128]{2,1,0:T(8,128)S(1)} %all_to_all.33.held, f32[8,128]{1,0:T(8,128)S(1)} %get-tuple-element.28.own), custom_call_target="tpu_custom_call" | custom-call | tf_op jit(solution)/shard_map/final/pallas_call | solution.py:406
  (5 shorter events, 0.0 us)
Async XLA Ops:
  2.7 62.3 %copy-start.3 = (f32[24,128]{1,0:T(8,128)S(1)}, f32[24,128]{1,0:T(8,128)}, u32[]{:S(2)}) copy-start(f32[24,128]{1,0:T(8,128)} %get-tuple-element.20.scale_high.scale) | copy-start | bytes 36868
  2.7 69.9 %copy-start.5 = (f32[128]{0:T(128)S(1)}, f32[128]{0:T(128)}, u32[]{:S(2)}) copy-start(f32[128]{0:T(128)} %param.11) | copy-start | bytes 1540
  27.0 18.2 %all-to-all-start = ((f32[16,24,128]{2,1,0:T(8,128)}), f32[16,24,128]{2,1,0:T(8,128)S(1)}, u32[]{:S(2)}, u32[]{:S(2)}) async-start(f32[16,24,128]{2,1,0:T(8,128)} %get-tuple-element.17), calls=%async_computation | async-start | bytes 393216 | tf_op jit(solution)/shard_map/all_to_all | solution.py:319
  36.8 35.7 %copy-start.4 = (s32[2]{0:T(128)S(1)}, s32[2]{0:T(128)}, u32[]{:S(2)}) copy-start(s32[2]{0:T(128)} %pad_add_fusion.at) | copy-start | bytes 28
  43.4 29.1 %copy-start = (bf16[2048,160]{1,0:T(8,128)(2,1)S(1)}, bf16[2048,160]{1,0:T(8,128)(2,1)}, u32[]{:S(2)}) copy-start(bf16[2048,160]{1,0:T(8,128)(2,1)} %get-tuple-element.23.cols_in) | copy-start | bytes 1966084
  45.2 0.7 copy-start.1
  58.8 13.7 %all-to-all-start.2 = ((f32[16,16,128]{2,1,0:T(8,128)}), f32[16,16,128]{2,1,0:T(8,128)S(1)}, u32[]{:S(2)}, u32[]{:S(2)}) async-start(f32[16,16,128]{2,1,0:T(8,128)} %mu.1), calls=%async_computation.2 | async-start | bytes 262144 | tf_op jit(solution)/shard_map/all_to_all | solution.py:319
  65.0 0.9 copy-start.2

commit v3 on v2

--- a/solution.py
+++ b/solution.py
@@ -14,6 +14,7 @@
 LANES = 128
 RUN_BLOCKS = 4
 WIDE = CHUNK = 512
+MU_CHUNK = 1024
 PACKED = RUN_BLOCKS * FEATS + FEATS + 8
 DEPTH = 160
 ROOT = math.sqrt(math.log2(math.e))
@@ -59,7 +60,7 @@
     u = scaled(points, scale)
     high, mid, low = split(u)
     norms = norm_rows(half_norm(u), 0)
-    return jnp.concatenate([high, high, high, mid, mid, low, norms, jnp.zeros_like(norms)], 0).astype(BF16)
+    return jnp.concatenate([high, high, high, mid, mid, low, norms, jnp.zeros_like(norms)], 0)
 
 
 def right(points, scale):
@@ -70,7 +71,7 @@
 
 
 def pack_kernel(*refs):
-    sources, (out_col, out_row, scale_low, scale_high), held, sems = refs[:5], refs[5:9], refs[9:14], refs[14]
+    sources, (out_col, scale_low, scale_high), held, sems = refs[:5], refs[5:8], refs[8:13], refs[13]
     copies = [pltpu.make_async_copy(a, b, sems.at[i]) for i, (a, b) in enumerate(zip(sources, held))]
     for copy in copies:
         copy.start()
@@ -84,8 +85,6 @@
             column = jnp.where(row == i, lengths[i], column)
         out[...] = ROOT / column
     own = points[...]
-    for i in range(out_row.shape[0]):
-        out_row[i] = own
     last = jnp.broadcast_to(weights[:, :LANES], (8, LANES))
     row = lax.broadcasted_iota(jnp.int32, (8, LANES), 0)
     for q in range(1, RUN_BLOCKS):
@@ -97,17 +96,12 @@
         out_col[i, PACKED - 8 :, :] = last
 
 
-def prep_kernel(held, scale_low, scale_high, runs_out, cols_out, weights_out):
-    def step(r, carry):
-        for q in range(RUN_BLOCKS):
-            rows = pl.ds(pl.multiple_of((r * RUN_BLOCKS + q) * LANES, LANES), LANES)
-            runs_out[rows, :] = right(held[r, q * FEATS : (q + 1) * FEATS, :], scale_low[...]).T.astype(BF16)
-        weights_out[pl.ds(pl.multiple_of(r * 8, 8), 8), :] = held[r, PACKED - 8 :, :]
-        rows = pl.ds(pl.multiple_of(r * LANES, LANES), LANES)
-        cols_out[rows, :] = right(held[r, RUN_BLOCKS * FEATS : PACKED - 8, :], scale_high[...]).T.astype(BF16)
+def prep_kernel(points, scale, out):
+    def step(k, carry):
+        out[pl.ds(pl.multiple_of(k * LANES, LANES), LANES), :] = left(points[k], scale[...]).T.astype(BF16)
         return carry
 
-    lax.fori_loop(0, held.shape[0], step, 0)
+    lax.fori_loop(0, points.shape[0], step, 0, unroll=4)
 
 
 def column_of(line, out, rows):
@@ -121,47 +115,39 @@
     return jnp.sum(term.reshape(count // 8, 8, wide), axis=0)
 
 
-def build_left(points, scale, out):
-    def step(g, carry):
-        for q in range(8):
-            k = g * 8 + q
-            out[:, pl.ds(pl.multiple_of(k * LANES, LANES), LANES)] = left(points[k], scale[...])
+def mu_kernel(held, rows_in, scale, high, rho, at, out, cols_out, even, odd, total, lines):
+    blocks = held.shape[0]
+
+    def side(r):
+        parts = [right(held[r, q * FEATS : (q + 1) * FEATS, :], scale[...]) for q in range(RUN_BLOCKS)]
+        return jnp.concatenate([p.astype(BF16) for p in parts], 1)
+
+    def work(r, runs):
+        weights = held[r, PACKED - 8 :, :]
+        for i in range(0, rows_in.shape[0], MU_CHUNK):
+            rows = slice(i, i + MU_CHUNK)
+            acc = total[rows, :]
+            term = jnp.exp2(jnp.dot(rows_in[rows, :], runs[...], preferred_element_type=F32))
+            for q in range(RUN_BLOCKS):
+                acc = acc + term[:, q * LANES : (q + 1) * LANES] * weights[q : q + 1, :]
+            total[rows, :] = acc
+
+    total[...] = jnp.zeros_like(total)
+    even[...] = side(0)
+
+    def step(k, carry):
+        odd[...] = side(2 * k + 1)
+        work(2 * k, even)
+        even[...] = side(jnp.minimum(2 * k + 2, blocks - 1))
+        work(2 * k + 1, odd)
         return carry
 
-    lax.fori_loop(0, points.shape[0] // 8, step, 0)
-
-
-def mu_kernel(points, scale, runs_hbm, weights, high, rho, at, out, parts, runs, column, total, sems):
-    pieces = sems.shape[0]
-    size = runs.shape[0] // pieces
-    blocks = size // (RUN_BLOCKS * LANES)
-
-    def copy(i):
-        rows = pl.ds(pl.multiple_of(i * size, size), size)
-        return pltpu.make_async_copy(runs_hbm.at[rows, :], runs.at[rows, :], sems.at[i])
-
-    for i in range(pieces):
-        copy(i).start()
-    build_left(points, scale, parts)
-    total[...] = jnp.zeros_like(total)
-
-    def step(i, carry):
-        copy(i).wait()
-        for r in range(blocks):
-            lines = weights[pl.ds(pl.multiple_of((i * blocks + r) * 8, 8), 8), :]
-            for q in range(RUN_BLOCKS):
-                first = (r * RUN_BLOCKS + q) * LANES
-                column_of(lines[q : q + 1, :], column, slice(first, first + LANES))
-        for c in range(0, parts.shape[1], WIDE):
-            acc = total[:, c : c + WIDE]
-            for j in range(0, size, CHUNK):
-                rows = pl.ds(pl.multiple_of(i * size + j, CHUNK), CHUNK)
-                acc = acc + weighted(runs[rows, :], parts[:, c : c + WIDE], column[j : j + CHUNK, :])
-            total[:, c : c + WIDE] = acc
-        return carry
-
-    lax.fori_loop(0, pieces, step, 0)
-    mu = lines_of(total)
+    lax.fori_loop(0, blocks // 2, step, 0)
+    for r in range(blocks):
+        cols_out[r] = held[r, RUN_BLOCKS * FEATS : PACKED - 8, :]
+    for k in range(lines.shape[0]):
+        lines[k : k + 1, :] = jnp.sum(total[k * LANES : (k + 1) * LANES, :].T, axis=0, keepdims=True)
+    mu = lines[...]
     row = lax.broadcasted_iota(jnp.int32, mu.shape, 0)
     target = -rho[0] * mu
     target = jnp.where(row == at[0], target + high[...], target)
@@ -174,8 +160,14 @@
     return jnp.concatenate([line[:, k : k + LANES] for k in range(0, line.shape[1], LANES)], 0)
 
 
-def sides_kernel(points, scale, out):
-    build_left(points, scale, out)
+def sides_kernel(rows, cols, scale, rows_out, cols_out):
+    def step(k, carry):
+        place = pl.ds(pl.multiple_of(k * LANES, LANES), LANES)
+        rows_out[:, place] = left(rows[k], scale[...]).astype(BF16)
+        cols_out[place, :] = right(cols[k], scale[...]).T.astype(BF16)
+        return carry
+
+    lax.fori_loop(0, rows.shape[0], step, 0, unroll=4)
 
 
 def first_kernel(held, rows_in, cols_in, high, rho, noise, at, out, target_out, mu_out, sums):
@@ -323,12 +315,12 @@
     n_row, n_col = lax.axis_size(ROWS), lax.axis_size(COLS)
     at = jnp.stack([lax.axis_index(ROWS), lax.axis_index(COLS)]).astype(jnp.int32)
     high = high.reshape(1, LANES)
-    runs_len, cols_len, rows_len = n_col * RUN_BLOCKS * LANES, n_col * LANES, n_row * LANES
-    to_col, to_row, scale_low, scale_high = pl.pallas_call(
+    cols_len, rows_len = n_col * LANES, n_row * LANES
+    to_col, scale_low, scale_high = pl.pallas_call(
         pack_kernel,
-        out_shape=(shape((n_col, PACKED, LANES)), shape((n_row, FEATS, LANES)), shape((FEATS, LANES)), shape((FEATS, LANES))),
+        out_shape=(shape((n_col, PACKED, LANES)), shape((FEATS, LANES)), shape((FEATS, LANES))),
         in_specs=[HBM] * 5,
-        out_specs=(VMEM,) * 4,
+        out_specs=(VMEM,) * 3,
         scratch_shapes=[
             pltpu.VMEM((FEATS, RUN_BLOCKS * LANES), F32),
             pltpu.VMEM((1, RUN_BLOCKS * LANES), F32),
@@ -341,39 +333,39 @@
         name="pack",
     )(runs, weights.reshape(1, RUN_BLOCKS * LANES), points, len_low, len_high)
     by_col = exchange(to_col, COLS)
-    by_row = exchange(to_row, ROWS)
-    run_parts, col_parts, weight_lines = pl.pallas_call(
+    by_row = lax.all_gather(points, "z", axis=0)
+    by_row = lax.all_gather(by_row, "core", axis=0).reshape(n_row, FEATS, LANES)
+    row_low = pl.pallas_call(
         prep_kernel,
-        out_shape=(shape((runs_len, DEPTH), BF16), shape((cols_len, DEPTH), BF16), shape((n_col * 8, LANES))),
-        in_specs=[VMEM] * 3,
-        out_specs=(VMEM,) * 3,
-        compiler_params=params(60),
-        name="prep",
-    )(by_col, scale_low, scale_high)
-    mu_terms = pl.pallas_call(
-        mu_kernel,
-        out_shape=shape((n_row, n_row, LANES)),
-        in_specs=[VMEM, VMEM, HBM, VMEM, VMEM, SMEM, SMEM],
-        out_specs=VMEM,
-        scratch_shapes=[
-            pltpu.VMEM((DEPTH, rows_len), BF16),
-            pltpu.VMEM((runs_len, DEPTH), BF16),
-            pltpu.VMEM((runs_len // 8, LANES), F32),
-            pltpu.VMEM((8, rows_len), F32),
-            pltpu.SemaphoreType.DMA((8,)),
-        ],
-        compiler_params=params(60),
-        name="mu",
-    )(by_row, scale_low, run_parts, weight_lines, high, rho, at)
-    mu_held = exchange(mu_terms, ROWS)
-    row_parts = pl.pallas_call(
-        sides_kernel,
-        out_shape=shape((DEPTH, rows_len), BF16),
+        out_shape=shape((rows_len, DEPTH), BF16),
         in_specs=[VMEM] * 2,
         out_specs=VMEM,
         compiler_params=params(4),
+        name="prep",
+    )(by_row, scale_low)
+    mu_terms, col_points = pl.pallas_call(
+        mu_kernel,
+        out_shape=(shape((n_row, n_row, LANES)), shape((n_col, FEATS, LANES))),
+        in_specs=[VMEM] * 4 + [SMEM] * 2,
+        out_specs=(VMEM,) * 2,
+        scratch_shapes=[
+            pltpu.VMEM((DEPTH, RUN_BLOCKS * LANES), BF16),
+            pltpu.VMEM((DEPTH, RUN_BLOCKS * LANES), BF16),
+            pltpu.VMEM((rows_len, LANES), F32),
+            pltpu.VMEM((n_row, LANES), F32),
+        ],
+        compiler_params=params(16),
+        name="mu",
+    )(by_col, row_low, scale_low, high, rho, at)
+    mu_held = exchange(mu_terms, ROWS)
+    row_parts, col_parts = pl.pallas_call(
+        sides_kernel,
+        out_shape=(shape((DEPTH, rows_len), BF16), shape((cols_len, DEPTH), BF16)),
+        in_specs=[VMEM] * 3,
+        out_specs=(VMEM,) * 2,
+        compiler_params=params(4),
         name="sides",
-    )(by_row, scale_high)
+    )(by_row, col_points, scale_high)
     image_terms, target, mu = pl.pallas_call(
         first_kernel,
         out_shape=(shape((n_col, n_col, LANES)), shape((n_row, LANES)), shape((1, LANES))),

time: 118 us -> 117 us (level)
  blocking collectives: 59 us -> 68.1 us
  Pallas kernels: 32 us -> 25.9 us
  waiting for transfers between devices: 8.18 us -> 6.8 us
    all_gather x0 -> x2, blocking collectives: none -> 29.4 us  [the longest x1 27.3 us: local(): by_row = lax.all_gather(points, 'z', axis=0)]
    all_to_all x4 -> x3, blocking collectives: 59 us -> 38.7 us  [exchange(): return lax.all_to_all(blocks, axes, 0, 0, tiled=True)]
    pallas_call x3, Pallas kernels: 19.8 us -> 13.6 us  [the longest x1 12.2 us: local(): pl.pallas_call(mu_kernel, out_shape=(shape((n_row, n_row, LANES)), shape(...]
    all_to_all x2, waiting for transfers between devices: 8.18 us -> 6.8 us  [exchange(): return lax.all_to_all(blocks, axes, 0, 0, tiled=True)]
  transfers between devices with their start and end apart: 2 -> 2, of which waited for: 2 -> 1; matrix products, arithmetic and copies ran while one was open for 0% -> 0% of each run, Pallas kernels for 6% -> 1%
where the time goes in v3:
time: 117 us
  blocking collectives  68.1 us (58%)
  Pallas kernels  25.9 us (22%)
  starting transfers between devices  13 us (11%)
  waiting for transfers between devices  6.8 us (6%)
  between operations  2.03 us (2%)
    all_to_all x3, blocking collectives, exchange(): return lax.all_to_all(blocks, axes, 0, 0, tiled=True)  38.7 us
    all_gather x1, blocking collectives, local(): by_row = lax.all_gather(points, 'z', axis=0)  27.3 us
    all_to_all x2, starting transfers between devices, exchange(): return lax.all_to_all(blocks, axes, 0, 0, tiled=True)  13 us
    pallas_call x1, Pallas kernels, local(): pl.pallas_call(mu_kernel, out_shape=(shape((n_row, n_row, LANES)), shape(...  12.2 us
    all_to_all x2, waiting for transfers between devices, exchange(): return lax.all_to_all(blocks, axes, 0, 0, tiled=True)  6.8 us
    pallas_call x1, Pallas kernels, local(): pl.pallas_call(first_kernel, out_shape=(shape((n_col, n_col, LANES)), sha...  4.69 us
    pallas_call x1, Pallas kernels, local(): pl.pallas_call(second_kernel, out_shape=shape((n_row, n_row + 8, LANES)),...  3.74 us
  transfers between devices with their start and end apart: 2, of which 1 were waited for; matrix products, arithmetic and copies ran while one was open for 0% of the time, Pallas kernels for 1%

profile of v3, /device:TPU:32, one launch (start us, length us, event | category | flops | bytes accessed | tf_op | source)
XLA Modules:
  0.0 116.6 jit_solution(8999742529771417251)
XLA Ops:
  0.6 1.9 %pack.1 = (f32[16,128,128]{2,1,0:T(8,128)}, f32[24,128]{1,0:T(8,128)}, f32[24,128]{1,0:T(8,128)}) custom-call(f32[24,512]{1,0:T(8,128)} %refs_0_.1, f32[1,512]{1,0:T(1,128)} %bitcast.11, f32[24,128]{1,0:T(8,128)} %refs_2_.1, f32[24]{0:T(128)} %refs_3_.1, f32[24]{0:T(128)} %refs_4_.1), custom_call_target="tpu_custom_call" | custom-call | tf_op jit(solution)/shard_map/pack/pallas_call | solution.py:319
  2.6 7.0 %all-to-all-start = ((f32[16,128,128]{2,1,0:T(8,128)}), f32[16,128,128]{2,1,0:T(8,128)S(1)}, u32[]{:S(2)}, u32[]{:S(2)}) async-start(f32[16,128,128]{2,1,0:T(8,128)} %get-tuple-element.17), calls=%async_computation | async-start | bytes 2097152 | tf_op jit(solution)/shard_map/all_to_all | solution.py:311
  9.6 0.0 copy-start.3
  10.3 0.0 copy-done.3
  10.4 27.3 %all-gather = f32[192,128]{1,0:T(8,128)S(1)} all-gather(f32[24,128]{1,0:T(8,128)S(1)} %copy-done.3), channel_id=2, replica_groups=mesh['y'=4,'core'=2,'x'=4,'z'=8] {'z'}, dimensions={0}, use_global_device_ids=true | all-gather | bytes 110592 | tf_op jit(solution)/shard_map/all_gather | solution.py:336
  37.7 2.1 %all-gather.1.points.rows = f32[16,24,128]{2,1,0:T(8,128)S(1)} all-gather(f32[8,24,128]{2,1,0:T(8,128)S(1)} %bitcast.10), channel_id=3, replica_groups=mesh['y'=4,'core'=2,'x'=4,'z'=8] {'core'}, dimensions={0}, use_global_device_ids=true | all-gather | bytes 294912 | tf_op jit(solution)/shard_map/all_gather | solution.py:337
  39.7 0.0 copy-done
  39.7 0.6 prep.1.rows_in
  40.4 0.1 pad_add_fusion.at
  40.5 0.0 copy-start.2
  40.5 0.0 all-to-all-done.held
  40.5 0.7 copy-done.2
  41.1 12.2 %mu.1 = (f32[16,16,128]{2,1,0:T(8,128)}, f32[16,24,128]{2,1,0:T(8,128)S(1)}) custom-call(f32[16,128,128]{2,1,0:T(8,128)S(1)} %all-to-all-done.held, bf16[2048,160]{1,0:T(8,128)(2,1)S(1)} %prep.1.rows_in, f32[24,128]{1,0:T(8,128)S(1)} %copy-done, f32[1,128]{1,0:T(1,128)S(1)} %bitcast.8, f32[1]{0:T(128)S(6)} %copy.11.rho, s32[2]{0:T(128)S(1)} %pad_add_fusion.at), custom_call_target="tpu_custom_call" | custom-call | tf_op jit(solution)/shard_map/mu/pallas_call | solution.py:346
  53.3 6.0 %all-to-all-start.1 = ((f32[16,16,128]{2,1,0:T(8,128)}), f32[16,16,128]{2,1,0:T(8,128)S(1)}, u32[]{:S(2)}, u32[]{:S(2)}) async-start(f32[16,16,128]{2,1,0:T(8,128)} %get-tuple-element.19), calls=%async_computation.1 | async-start | bytes 262144 | tf_op jit(solution)/shard_map/all_to_all | solution.py:311
  60.0 0.0 copy-done.1
  60.0 0.8 sides.1
  60.7 6.8 %all-to-all-done.1.held = f32[16,16,128]{2,1,0:T(8,128)S(1)} async-done(((f32[16,16,128]{2,1,0:T(8,128)}), f32[16,16,128]{2,1,0:T(8,128)S(1)}, u32[]{:S(2)}, u32[]{:S(2)}) %all-to-all-start.1) | async-done | bytes 131104 | tf_op jit(solution)/shard_map/all_to_all | solution.py:311
  67.5 4.7 %first.1 = (f32[16,16,128]{2,1,0:T(8,128)S(1)}, f32[16,128]{1,0:T(8,128)S(1)}, f32[1,128]{1,0:T(1,128)}) custom-call(f32[16,16,128]{2,1,0:T(8,128)S(1)} %all-to-all-done.1.held, bf16[160,2048]{1,0:T(8,128)(2,1)S(1)} %get-tuple-element.22.rows_in, bf16[2048,160]{1,0:T(8,128)(2,1)S(1)} %get-tuple-element.23.cols_in, f32[1,128]{1,0:T(1,128)S(1)} %bitcast.9, ...), custom_call_target="tpu_custom_call" | custom-call | tf_op jit(solution)/shard_map/first/pallas_call | solution.py:369
  72.2 15.0 %all_to_all.25.held = f32[16,16,128]{2,1,0:T(8,128)S(1)} all-to-all(f32[16,16,128]{2,1,0:T(8,128)S(1)} %get-tuple-element.25), channel_id=1, replica_groups=mesh['y'=4,'core'=2,'x'=4,'z'=8] {'y','x'}, dimensions={0} | all-to-all | bytes 262144 | tf_op jit(solution)/shard_map/all_to_all | solution.py:311
  87.2 3.7 %second.1 = f32[16,24,128]{2,1,0:T(8,128)S(1)} custom-call(f32[16,16,128]{2,1,0:T(8,128)S(1)} %all_to_all.25.held, bf16[160,2048]{1,0:T(8,128)(2,1)S(1)} %get-tuple-element.22.rows_in, bf16[2048,160]{1,0:T(8,128)(2,1)S(1)} %get-tuple-element.23.cols_in, f32[1]{0:T(128)S(6)} %copy.12.noise, s32[2]{0:T(128)S(1)} %pad_add_fusion.at), custom_call_target="tpu_custom_call" | custom-call | tf_op jit(solution)/shard_map/second/pallas_call | solution.py:379
  91.0 13.0 %all_to_all.26.held = f32[16,24,128]{2,1,0:T(8,128)S(1)} all-to-all(f32[16,24,128]{2,1,0:T(8,128)S(1)} %second.1), channel_id=1, replica_groups=mesh['y'=4,'core'=2,'x'=4,'z'=8] {'core','z'}, dimensions={0} | all-to-all | bytes 393216 | tf_op jit(solution)/shard_map/all_to_all | solution.py:311
  104.0 0.7 moments.1
  104.7 10.7 %all_to_all.27.held = f32[16,8,128]{2,1,0:T(8,128)S(1)} all-to-all(f32[16,8,128]{2,1,0:T(8,128)S(1)} %get-tuple-element.27), channel_id=1, replica_groups=mesh['y'=4,'core'=2,'x'=4,'z'=8] {'y','x'}, dimensions={0} | all-to-all | bytes 131072 | tf_op jit(solution)/shard_map/all_to_all | solution.py:311
  115.4 1.2 %final.1 = (f32[1,128]{1,0:T(1,128)}, f32[1,128]{1,0:T(1,128)}) custom-call(f32[16,8,128]{2,1,0:T(8,128)S(1)} %all_to_all.27.held, f32[8,128]{1,0:T(8,128)S(1)} %get-tuple-element.28.own), custom_call_target="tpu_custom_call" | custom-call | tf_op jit(solution)/shard_map/final/pallas_call | solution.py:398
  (2 shorter events, 0.0 us)
Async XLA Ops:
  2.6 37.9 %all-to-all-start = ((f32[16,128,128]{2,1,0:T(8,128)}), f32[16,128,128]{2,1,0:T(8,128)S(1)}, u32[]{:S(2)}, u32[]{:S(2)}) async-start(f32[16,128,128]{2,1,0:T(8,128)} %get-tuple-element.17), calls=%async_computation | async-start | bytes 2097152 | tf_op jit(solution)/shard_map/all_to_all | solution.py:311
  9.6 0.7 copy-start.3
  37.7 2.1 %copy-start = (f32[24,128]{1,0:T(8,128)S(1)}, f32[24,128]{1,0:T(8,128)}, u32[]{:S(2)}) copy-start(f32[24,128]{1,0:T(8,128)} %get-tuple-element.18.scale) | copy-start | bytes 36868
  40.5 0.7 copy-start.2
  53.3 6.7 %copy-start.1 = (f32[24,128]{1,0:T(8,128)S(1)}, f32[24,128]{1,0:T(8,128)}, u32[]{:S(2)}) copy-start(f32[24,128]{1,0:T(8,128)} %get-tuple-element.21.scale) | copy-start | bytes 36868
  53.3 14.2 %all-to-all-start.1 = ((f32[16,16,128]{2,1,0:T(8,128)}), f32[16,16,128]{2,1,0:T(8,128)S(1)}, u32[]{:S(2)}, u32[]{:S(2)}) async-start(f32[16,16,128]{2,1,0:T(8,128)} %get-tuple-element.19), calls=%async_computation.1 | async-start | bytes 262144 | tf_op jit(solution)/shard_map/all_to_all | solution.py:311

commit v4 on v3

--- a/solution.py
+++ b/solution.py
@@ -13,6 +13,7 @@
 FEATS = 24
 LANES = 128
 RUN_BLOCKS = 4
+STEPS = (4, 2, 1)
 WIDE = CHUNK = 512
 MU_CHUNK = 1024
 PACKED = RUN_BLOCKS * FEATS + FEATS + 8
@@ -96,12 +97,16 @@
         out_col[i, PACKED - 8 :, :] = last
 
 
-def prep_kernel(points, scale, out):
-    def step(k, carry):
-        out[pl.ds(pl.multiple_of(k * LANES, LANES), LANES), :] = left(points[k], scale[...]).T.astype(BF16)
-        return carry
-
-    lax.fori_loop(0, points.shape[0], step, 0, unroll=4)
+def place_of(k, at):
+    depth = len(STEPS)
+    offset = sum(step for i, step in enumerate(STEPS) if k >> i & 1)
+    block = (k >> depth << depth) + ((at[0] & (1 << depth) - 1) ^ offset)
+    return pl.ds(pl.multiple_of(block * LANES, LANES), LANES)
+
+
+def prep_kernel(points, scale, at, out):
+    for k in range(points.shape[0]):
+        out[place_of(k, at), :] = left(points[k], scale[...]).T.astype(BF16)
 
 
 def column_of(line, out, rows):
@@ -160,14 +165,11 @@
     return jnp.concatenate([line[:, k : k + LANES] for k in range(0, line.shape[1], LANES)], 0)
 
 
-def sides_kernel(rows, cols, scale, rows_out, cols_out):
-    def step(k, carry):
-        place = pl.ds(pl.multiple_of(k * LANES, LANES), LANES)
-        rows_out[:, place] = left(rows[k], scale[...]).astype(BF16)
-        cols_out[place, :] = right(cols[k], scale[...]).T.astype(BF16)
-        return carry
-
-    lax.fori_loop(0, rows.shape[0], step, 0, unroll=4)
+def sides_kernel(rows, cols, scale, at, rows_out, cols_out):
+    for k in range(rows.shape[0]):
+        rows_out[:, place_of(k, at)] = left(rows[k], scale[...]).astype(BF16)
+    for k in range(cols.shape[0]):
+        cols_out[k * LANES : (k + 1) * LANES, :] = right(cols[k], scale[...]).T.astype(BF16)
 
 
 def first_kernel(held, rows_in, cols_in, high, rho, noise, at, out, target_out, mu_out, sums):
@@ -333,16 +335,19 @@
         name="pack",
     )(runs, weights.reshape(1, RUN_BLOCKS * LANES), points, len_low, len_high)
     by_col = exchange(to_col, COLS)
-    by_row = lax.all_gather(points, "z", axis=0)
-    by_row = lax.all_gather(by_row, "core", axis=0).reshape(n_row, FEATS, LANES)
+    by_row = points[None]
+    for step in STEPS:
+        pairs = [(i, i ^ step) for i in range(lax.axis_size("z"))]
+        by_row = jnp.concatenate([by_row, lax.ppermute(by_row, "z", pairs)], 0)
+    by_row = lax.all_gather(by_row, "core", axis=0, tiled=True)
     row_low = pl.pallas_call(
         prep_kernel,
         out_shape=shape((rows_len, DEPTH), BF16),
-        in_specs=[VMEM] * 2,
+        in_specs=[VMEM, VMEM, SMEM],
         out_specs=VMEM,
         compiler_params=params(4),
         name="prep",
-    )(by_row, scale_low)
+    )(by_row, scale_low, at)
     mu_terms, col_points = pl.pallas_call(
         mu_kernel,
         out_shape=(shape((n_row, n_row, LANES)), shape((n_col, FEATS, LANES))),
@@ -361,11 +366,11 @@
     row_parts, col_parts = pl.pallas_call(
         sides_kernel,
         out_shape=(shape((DEPTH, rows_len), BF16), shape((cols_len, DEPTH), BF16)),
-        in_specs=[VMEM] * 3,
+        in_specs=[VMEM] * 3 + [SMEM],
         out_specs=(VMEM,) * 2,
         compiler_params=params(4),
         name="sides",
-    )(by_row, col_points, scale_high)
+    )(by_row, col_points, scale_high, at)
     image_terms, target, mu = pl.pallas_call(
         first_kernel,
         out_shape=(shape((n_col, n_col, LANES)), shape((n_row, LANES)), shape((1, LANES))),

time: 117 us -> 108 us (0.923)
  blocking collectives: 68.1 us -> 40.7 us
  starting transfers between devices: 13 us -> 25.7 us
  waiting for transfers between devices: 6.8 us -> 12.3 us
    all_gather x2 -> x1, blocking collectives: 29.4 us -> 1.95 us  [local(): by_row = lax.all_gather(by_row, 'core', axis=0, tiled=True)]
    ppermute x0 -> x3, starting transfers between devices: none -> 10.3 us  [local(): by_row = jnp.concatenate([by_row, lax.ppermute(by_row, 'z', pairs)], 0)]
    ppermute x0 -> x3, waiting for transfers between devices: none -> 5.86 us  [local(): by_row = jnp.concatenate([by_row, lax.ppermute(by_row, 'z', pairs)], 0)]
    all_to_all x2, starting transfers between devices: 13 us -> 15.4 us  [exchange(): return lax.all_to_all(blocks, axes, 0, 0, tiled=True)]
  transfers between devices with their start and end apart: 2 -> 5, of which waited for: 1 -> 4; matrix products, arithmetic and copies ran while one was open for 0% -> 0% of each run, Pallas kernels for 1% -> 2%
where the time goes in v4:
time: 108 us
  blocking collectives  40.7 us (38%)
  Pallas kernels  26.5 us (25%)
  starting transfers between devices  25.7 us (24%)
  waiting for transfers between devices  12.3 us (11%)
  between operations  2.04 us (2%)
    all_to_all x3, blocking collectives, exchange(): return lax.all_to_all(blocks, axes, 0, 0, tiled=True)  38.7 us
    all_to_all x2, starting transfers between devices, exchange(): return lax.all_to_all(blocks, axes, 0, 0, tiled=True)  15.4 us
    pallas_call x1, Pallas kernels, local(): pl.pallas_call(mu_kernel, out_shape=(shape((n_row, n_row, LANES)), shape(...  12.2 us
    ppermute x3, starting transfers between devices, local(): by_row = jnp.concatenate([by_row, lax.ppermute(by_row, 'z', pairs)], 0)  10.3 us
    all_to_all x2, waiting for transfers between devices, exchange(): return lax.all_to_all(blocks, axes, 0, 0, tiled=True)  6.44 us
    ppermute x3, waiting for transfers between devices, local(): by_row = jnp.concatenate([by_row, lax.ppermute(by_row, 'z', pairs)], 0)  5.86 us
    pallas_call x1, Pallas kernels, local(): pl.pallas_call(first_kernel, out_shape=(shape((n_col, n_col, LANES)), sha...  4.66 us
    pallas_call x1, Pallas kernels, local(): pl.pallas_call(second_kernel, out_shape=shape((n_row, n_row + 8, LANES)),...  3.74 us
  transfers between devices with their start and end apart: 5, of which 4 were waited for; matrix products, arithmetic and copies ran while one was open for 0% of the time, Pallas kernels for 2%

profile of v4, /device:TPU:32, one launch (start us, length us, event | category | flops | bytes accessed | tf_op | source)
XLA Modules:
  0.0 107.9 jit_solution(18042467284229433954)
XLA Ops:
  0.6 1.9 %pack.1 = (f32[16,128,128]{2,1,0:T(8,128)}, f32[24,128]{1,0:T(8,128)}, f32[24,128]{1,0:T(8,128)}) custom-call(f32[24,512]{1,0:T(8,128)} %refs_0_.1, f32[1,512]{1,0:T(1,128)} %bitcast.14, f32[24,128]{1,0:T(8,128)} %refs_2_.1, f32[24]{0:T(128)} %refs_3_.1, f32[24]{0:T(128)} %refs_4_.1), custom_call_target="tpu_custom_call" | custom-call | tf_op jit(solution)/shard_map/pack/pallas_call | solution.py:321
  2.6 0.0 copy-start.3
  2.6 7.0 %all-to-all-start = ((f32[16,128,128]{2,1,0:T(8,128)}), f32[16,128,128]{2,1,0:T(8,128)S(1)}, u32[]{:S(2)}, u32[]{:S(2)}) async-start(f32[16,128,128]{2,1,0:T(8,128)} %get-tuple-element.17), calls=%async_computation | async-start | bytes 2097152 | tf_op jit(solution)/shard_map/all_to_all | solution.py:313
  9.7 6.4 %collective-permute-start = (f32[1,24,128]{2,1,0:T(8,128)S(1)}, f32[1,24,128]{2,1,0:T(8,128)S(1)}, u32[]{:S(2)}, u32[]{:S(2)}) collective-permute-start(f32[1,24,128]{2,1,0:T(8,128)S(1)} %bitcast.10), channel_id=1, source_target_pairs={{0,4},{1,5},{2,6},{3,7},{4,0},{5,1},{6,2},{7,3},{8,12},{9,13},{10,... | collective-permute-start | bytes 36872 | tf_op jit(solution)/shard_map/ppermute | solution.py:341
  16.0 1.7 %collective-permute-done = f32[1,24,128]{2,1,0:T(8,128)S(1)} collective-permute-done((f32[1,24,128]{2,1,0:T(8,128)S(1)}, f32[1,24,128]{2,1,0:T(8,128)S(1)}, u32[]{:S(2)}, u32[]{:S(2)}) %collective-permute-start) | collective-permute-done | bytes 12320 | tf_op jit(solution)/shard_map/ppermute | solution.py:341
  17.7 2.9 %collective-permute-start.1 = (f32[2,24,128]{2,1,0:T(8,128)S(1)}, f32[2,24,128]{2,1,0:T(8,128)S(1)}, u32[]{:S(2)}, u32[]{:S(2)}) collective-permute-start(f32[2,24,128]{2,1,0:T(8,128)S(1)} %pad_maximum_fusion.2), channel_id=1, source_target_pairs={{0,2},{1,3},{2,0},{3,1},{4,6},{5,7},{6,4},{7,5},{8,10},{9,11},{10,... | collective-permute-start | bytes 73736 | tf_op jit(solution)/shard_map/ppermute | solution.py:341
  20.6 1.8 %collective-permute-done.1 = f32[2,24,128]{2,1,0:T(8,128)S(1)} collective-permute-done((f32[2,24,128]{2,1,0:T(8,128)S(1)}, f32[2,24,128]{2,1,0:T(8,128)S(1)}, u32[]{:S(2)}, u32[]{:S(2)}) %collective-permute-start.1) | collective-permute-done | bytes 24608 | tf_op jit(solution)/shard_map/ppermute | solution.py:341
  22.5 1.0 collective-permute-start.2
  23.5 0.1 pad_add_fusion.at
  24.2 2.4 %collective-permute-done.2 = f32[4,24,128]{2,1,0:T(8,128)S(1)} collective-permute-done((f32[4,24,128]{2,1,0:T(8,128)S(1)}, f32[4,24,128]{2,1,0:T(8,128)S(1)}, u32[]{:S(2)}, u32[]{:S(2)}) %collective-permute-start.2) | collective-permute-done | bytes 49184 | tf_op jit(solution)/shard_map/ppermute | solution.py:341
  26.6 1.9 %all_gather.3.points.rows = f32[16,24,128]{2,1,0:T(8,128)S(1)} all-gather(f32[8,24,128]{2,1,0:T(8,128)S(1)} %pad_maximum_fusion), channel_id=1, replica_groups=mesh['y'=4,'core'=2,'x'=4,'z'=8] {'core'}, dimensions={0}, use_global_device_ids=true | all-gather | bytes 294912 | tf_op jit(solution)/shard_map/all_gather | solution.py:342
  28.5 0.9 prep.1.rows_in
  29.5 0.6 copy-done.2
  30.1 12.2 %mu.1 = (f32[16,16,128]{2,1,0:T(8,128)}, f32[16,24,128]{2,1,0:T(8,128)S(1)}) custom-call(f32[16,128,128]{2,1,0:T(8,128)S(1)} %all-to-all-done.held, bf16[2048,160]{1,0:T(8,128)(2,1)S(1)} %prep.1.rows_in, f32[24,128]{1,0:T(8,128)S(1)} %copy-done, f32[1,128]{1,0:T(1,128)S(1)} %bitcast.8, f32[1]{0:T(128)S(6)} %copy.11.rho, s32[2]{0:T(128)S(1)} %pad_add_fusion.at), custom_call_target="tpu_custom_call" | custom-call | tf_op jit(solution)/shard_map/mu/pallas_call | solution.py:351
  42.3 8.3 %all-to-all-start.1 = ((f32[16,16,128]{2,1,0:T(8,128)}), f32[16,16,128]{2,1,0:T(8,128)S(1)}, u32[]{:S(2)}, u32[]{:S(2)}) async-start(f32[16,16,128]{2,1,0:T(8,128)} %get-tuple-element.19), calls=%async_computation.1 | async-start | bytes 262144 | tf_op jit(solution)/shard_map/all_to_all | solution.py:313
  51.3 1.1 %sides.1 = (bf16[160,2048]{1,0:T(8,128)(2,1)S(1)}, bf16[2048,160]{1,0:T(8,128)(2,1)S(1)}) custom-call(f32[16,24,128]{2,1,0:T(8,128)S(1)} %all_gather.3.points.rows, f32[16,24,128]{2,1,0:T(8,128)S(1)} %get-tuple-element.20.cols, f32[24,128]{1,0:T(8,128)S(1)} %copy-done.1, s32[2]{0:T(128)S(1)} %pad_add_fusion.at), custom_call_target="tpu_custom_call" | custom-call | tf_op jit(solution)/shard_map/sides/pallas_call | solution.py:366
  52.4 6.4 %all-to-all-done.1.held = f32[16,16,128]{2,1,0:T(8,128)S(1)} async-done(((f32[16,16,128]{2,1,0:T(8,128)}), f32[16,16,128]{2,1,0:T(8,128)S(1)}, u32[]{:S(2)}, u32[]{:S(2)}) %all-to-all-start.1) | async-done | bytes 131104 | tf_op jit(solution)/shard_map/all_to_all | solution.py:313
  58.8 4.7 %first.1 = (f32[16,16,128]{2,1,0:T(8,128)S(1)}, f32[16,128]{1,0:T(8,128)S(1)}, f32[1,128]{1,0:T(1,128)}) custom-call(f32[16,16,128]{2,1,0:T(8,128)S(1)} %all-to-all-done.1.held, bf16[160,2048]{1,0:T(8,128)(2,1)S(1)} %get-tuple-element.22.rows_in, bf16[2048,160]{1,0:T(8,128)(2,1)S(1)} %get-tuple-element.23.cols_in, f32[1,128]{1,0:T(1,128)S(1)} %bitcast.9, ...), custom_call_target="tpu_custom_call" | custom-call | tf_op jit(solution)/shard_map/first/pallas_call | solution.py:374
  63.5 15.0 %all_to_all.25.held = f32[16,16,128]{2,1,0:T(8,128)S(1)} all-to-all(f32[16,16,128]{2,1,0:T(8,128)S(1)} %get-tuple-element.25), channel_id=1, replica_groups=mesh['y'=4,'core'=2,'x'=4,'z'=8] {'y','x'}, dimensions={0} | all-to-all | bytes 262144 | tf_op jit(solution)/shard_map/all_to_all | solution.py:313
  78.5 3.7 %second.1 = f32[16,24,128]{2,1,0:T(8,128)S(1)} custom-call(f32[16,16,128]{2,1,0:T(8,128)S(1)} %all_to_all.25.held, bf16[160,2048]{1,0:T(8,128)(2,1)S(1)} %get-tuple-element.22.rows_in, bf16[2048,160]{1,0:T(8,128)(2,1)S(1)} %get-tuple-element.23.cols_in, f32[1]{0:T(128)S(6)} %copy.12.noise, s32[2]{0:T(128)S(1)} %pad_add_fusion.at), custom_call_target="tpu_custom_call" | custom-call | tf_op jit(solution)/shard_map/second/pallas_call | solution.py:384
  82.3 13.0 %all_to_all.26.held = f32[16,24,128]{2,1,0:T(8,128)S(1)} all-to-all(f32[16,24,128]{2,1,0:T(8,128)S(1)} %second.1), channel_id=1, replica_groups=mesh['y'=4,'core'=2,'x'=4,'z'=8] {'core','z'}, dimensions={0} | all-to-all | bytes 393216 | tf_op jit(solution)/shard_map/all_to_all | solution.py:313
  95.3 0.7 moments.1
  96.0 10.7 %all_to_all.27.held = f32[16,8,128]{2,1,0:T(8,128)S(1)} all-to-all(f32[16,8,128]{2,1,0:T(8,128)S(1)} %get-tuple-element.27), channel_id=1, replica_groups=mesh['y'=4,'core'=2,'x'=4,'z'=8] {'y','x'}, dimensions={0} | all-to-all | bytes 131072 | tf_op jit(solution)/shard_map/all_to_all | solution.py:313
  106.7 1.2 %final.1 = (f32[1,128]{1,0:T(1,128)}, f32[1,128]{1,0:T(1,128)}) custom-call(f32[16,8,128]{2,1,0:T(8,128)S(1)} %all_to_all.27.held, f32[8,128]{1,0:T(8,128)S(1)} %get-tuple-element.28.own), custom_call_target="tpu_custom_call" | custom-call | tf_op jit(solution)/shard_map/final/pallas_call | solution.py:403
  (10 shorter events, 0.0 us)
Async XLA Ops:
  2.6 7.1 %copy-start.3 = (f32[24,128]{1,0:T(8,128)S(1)}, f32[24,128]{1,0:T(8,128)}, u32[]{:S(2)}) copy-start(f32[24,128]{1,0:T(8,128)} %refs_2_.1) | copy-start | bytes 36868
  2.6 26.8 %all-to-all-start = ((f32[16,128,128]{2,1,0:T(8,128)}), f32[16,128,128]{2,1,0:T(8,128)S(1)}, u32[]{:S(2)}, u32[]{:S(2)}) async-start(f32[16,128,128]{2,1,0:T(8,128)} %get-tuple-element.17), calls=%async_computation | async-start | bytes 2097152 | tf_op jit(solution)/shard_map/all_to_all | solution.py:313
  9.7 8.1 %collective-permute-start = (f32[1,24,128]{2,1,0:T(8,128)S(1)}, f32[1,24,128]{2,1,0:T(8,128)S(1)}, u32[]{:S(2)}, u32[]{:S(2)}) collective-permute-start(f32[1,24,128]{2,1,0:T(8,128)S(1)} %bitcast.10), channel_id=1, source_target_pairs={{0,4},{1,5},{2,6},{3,7},{4,0},{5,1},{6,2},{7,3},{8,12},{9,13},{10,... | collective-permute-start | bytes 36872 | tf_op jit(solution)/shard_map/ppermute | solution.py:341
  17.7 4.7 %collective-permute-start.1 = (f32[2,24,128]{2,1,0:T(8,128)S(1)}, f32[2,24,128]{2,1,0:T(8,128)S(1)}, u32[]{:S(2)}, u32[]{:S(2)}) collective-permute-start(f32[2,24,128]{2,1,0:T(8,128)S(1)} %pad_maximum_fusion.2), channel_id=1, source_target_pairs={{0,2},{1,3},{2,0},{3,1},{4,6},{5,7},{6,4},{7,5},{8,10},{9,11},{10,... | collective-permute-start | bytes 73736 | tf_op jit(solution)/shard_map/ppermute | solution.py:341
  22.5 4.1 %collective-permute-start.2 = (f32[4,24,128]{2,1,0:T(8,128)S(1)}, f32[4,24,128]{2,1,0:T(8,128)S(1)}, u32[]{:S(2)}, u32[]{:S(2)}) collective-permute-start(f32[4,24,128]{2,1,0:T(8,128)S(1)} %pad_maximum_fusion.1), channel_id=1, source_target_pairs={{0,1},{1,0},{2,3},{3,2},{4,5},{5,4},{6,7},{7,6},{8,9},{9,8},{10,11... | collective-permute-start | bytes 147464 | tf_op jit(solution)/shard_map/ppermute | solution.py:341
  26.6 2.0 %copy-start = (f32[24,128]{1,0:T(8,128)S(1)}, f32[24,128]{1,0:T(8,128)}, u32[]{:S(2)}) copy-start(f32[24,128]{1,0:T(8,128)} %get-tuple-element.18.scale) | copy-start | bytes 36868
  29.4 0.7 copy-start.2
  42.3 9.0 %copy-start.1 = (f32[24,128]{1,0:T(8,128)S(1)}, f32[24,128]{1,0:T(8,128)}, u32[]{:S(2)}) copy-start(f32[24,128]{1,0:T(8,128)} %get-tuple-element.21.scale) | copy-start | bytes 36868
  42.3 16.6 %all-to-all-start.1 = ((f32[16,16,128]{2,1,0:T(8,128)}), f32[16,16,128]{2,1,0:T(8,128)S(1)}, u32[]{:S(2)}, u32[]{:S(2)}) async-start(f32[16,16,128]{2,1,0:T(8,128)} %get-tuple-element.19), calls=%async_computation.1 | async-start | bytes 262144 | tf_op jit(solution)/shard_map/all_to_all | solution.py:313

commit v5 on v4

--- a/solution.py
+++ b/solution.py
@@ -13,9 +13,8 @@
 FEATS = 24
 LANES = 128
 RUN_BLOCKS = 4
-STEPS = (4, 2, 1)
 WIDE = CHUNK = 512
-MU_CHUNK = 1024
+MU_CHUNK = 256
 PACKED = RUN_BLOCKS * FEATS + FEATS + 8
 DEPTH = 160
 ROOT = math.sqrt(math.log2(math.e))
@@ -97,16 +96,16 @@
         out_col[i, PACKED - 8 :, :] = last
 
 
-def place_of(k, at):
-    depth = len(STEPS)
-    offset = sum(step for i, step in enumerate(STEPS) if k >> i & 1)
-    block = (k >> depth << depth) + ((at[0] & (1 << depth) - 1) ^ offset)
+def place_of(j, m, at):
+    block = (m & 1) * 8 + ((at[0] & 7) ^ (j ^ 4 * (m >> 1)))
     return pl.ds(pl.multiple_of(block * LANES, LANES), LANES)
 
 
-def prep_kernel(points, scale, at, out):
-    for k in range(points.shape[0]):
-        out[place_of(k, at), :] = left(points[k], scale[...]).T.astype(BF16)
+def prep_kernel(*refs):
+    points, scale, at, out = refs[:4], refs[4], refs[5], refs[6]
+    for j, ref in enumerate(points):
+        for m in range(ref.shape[0]):
+            out[place_of(j, m, at), :] = left(ref[m], scale[...]).T.astype(BF16)
 
 
 def column_of(line, out, rows):
@@ -138,16 +137,12 @@
             total[rows, :] = acc
 
     total[...] = jnp.zeros_like(total)
+    held_sides = (even, odd)
     even[...] = side(0)
-
-    def step(k, carry):
-        odd[...] = side(2 * k + 1)
-        work(2 * k, even)
-        even[...] = side(jnp.minimum(2 * k + 2, blocks - 1))
-        work(2 * k + 1, odd)
-        return carry
-
-    lax.fori_loop(0, blocks // 2, step, 0)
+    for r in range(blocks):
+        if r + 1 < blocks:
+            held_sides[(r + 1) % 2][...] = side(r + 1)
+        work(r, held_sides[r % 2])
     for r in range(blocks):
         cols_out[r] = held[r, RUN_BLOCKS * FEATS : PACKED - 8, :]
     for k in range(lines.shape[0]):
@@ -165,9 +160,11 @@
     return jnp.concatenate([line[:, k : k + LANES] for k in range(0, line.shape[1], LANES)], 0)
 
 
-def sides_kernel(rows, cols, scale, at, rows_out, cols_out):
-    for k in range(rows.shape[0]):
-        rows_out[:, place_of(k, at)] = left(rows[k], scale[...]).astype(BF16)
+def sides_kernel(*refs):
+    points, (cols, scale, at, rows_out, cols_out) = refs[:4], refs[4:]
+    for j, ref in enumerate(points):
+        for m in range(ref.shape[0]):
+            rows_out[:, place_of(j, m, at)] = left(ref[m], scale[...]).astype(BF16)
     for k in range(cols.shape[0]):
         cols_out[k * LANES : (k + 1) * LANES, :] = right(cols[k], scale[...]).T.astype(BF16)
 
@@ -182,20 +179,17 @@
     own_target = jnp.sum(jnp.where(own, target, 0.0), axis=0, keepdims=True)
     size = 2 * LANES
 
-    def step(k, carry):
-        cols = cols_in[pl.ds(pl.multiple_of(k * size, size), size), :]
+    for k in range(0, cols_in.shape[0], size):
+        cols = cols_in[k : k + size, :]
         acc = jnp.zeros((size, LANES), F32)
         for c in range(0, rows_in.shape[1], WIDE):
             term = jnp.exp2(jnp.dot(cols, rows_in[:, c : c + WIDE], preferred_element_type=F32))
             for q in range(0, WIDE, LANES):
                 s = (c + q) // LANES
                 acc = acc + term[:, q : q + LANES] * target_out[s : s + 1, :]
-        for q in range(2):
-            block = acc[q * LANES : (q + 1) * LANES, :]
-            sums[pl.ds(k * 2 + q, 1), :] = jnp.sum(block.T, axis=0, keepdims=True)
-        return carry
-
-    lax.fori_loop(0, cols_in.shape[0] // size, step, 0)
+        for q in range(0, size, LANES):
+            at_row = (k + q) // LANES
+            sums[at_row : at_row + 1, :] = jnp.sum(acc[q : q + LANES, :].T, axis=0, keepdims=True)
     image = sums[...]
     image = jnp.where(lax.broadcasted_iota(jnp.int32, image.shape, 0) == at[1], image + noise[0] * own_target, image)
     for i in range(out.shape[0]):
@@ -210,13 +204,10 @@
         column_of(image[k : k + 1, :], column, slice(k * LANES, (k + 1) * LANES))
     total[...] = jnp.zeros_like(total)
 
-    def step(i, carry):
-        rows = pl.ds(pl.multiple_of(i * CHUNK, CHUNK), CHUNK)
+    for i in range(0, cols_in.shape[0], CHUNK):
+        rows = slice(i, i + CHUNK)
         for c in range(0, rows_in.shape[1], WIDE):
             total[:, c : c + WIDE] += weighted(cols_in[rows, :], rows_in[:, c : c + WIDE], column[rows, :])
-        return carry
-
-    lax.fori_loop(0, cols_in.shape[0] // CHUNK, step, 0)
     last = lines_of(total)
     row = lax.broadcasted_iota(jnp.int32, last.shape, 0)
     last = jnp.where(row == at[0], last + noise[0] * own, last)
@@ -309,6 +300,10 @@
     r_out[...] = (b - alpha0 * image) - alpha1 * (grow * image - alpha0 * last)
 
 
+def exchange_z(blocks, step, size):
+    return lax.ppermute(blocks, "z", [(i, i ^ step) for i in range(size)])
+
+
 def exchange(blocks, axes):
     return lax.all_to_all(blocks, axes, 0, 0, tiled=True)
 
@@ -318,6 +313,8 @@
     at = jnp.stack([lax.axis_index(ROWS), lax.axis_index(COLS)]).astype(jnp.int32)
     high = high.reshape(1, LANES)
     cols_len, rows_len = n_col * LANES, n_row * LANES
+    near_core = lax.all_gather(points, "core", axis=0)
+    near_core, weights = lax.optimization_barrier((near_core, weights))
     to_col, scale_low, scale_high = pl.pallas_call(
         pack_kernel,
         out_shape=(shape((n_col, PACKED, LANES)), shape((FEATS, LANES)), shape((FEATS, LANES))),
@@ -335,19 +332,18 @@
         name="pack",
     )(runs, weights.reshape(1, RUN_BLOCKS * LANES), points, len_low, len_high)
     by_col = exchange(to_col, COLS)
-    by_row = points[None]
-    for step in STEPS:
-        pairs = [(i, i ^ step) for i in range(lax.axis_size("z"))]
-        by_row = jnp.concatenate([by_row, lax.ppermute(by_row, "z", pairs)], 0)
-    by_row = lax.all_gather(by_row, "core", axis=0, tiled=True)
+    size = lax.axis_size("z")
+    near = exchange_z(near_core, 4, size)
+    near = jnp.concatenate([near_core, near], 0)
+    by_row = [near] + [exchange_z(near, step, size) for step in (1, 2, 3)]
     row_low = pl.pallas_call(
         prep_kernel,
         out_shape=shape((rows_len, DEPTH), BF16),
-        in_specs=[VMEM, VMEM, SMEM],
+        in_specs=[VMEM] * 5 + [SMEM],
         out_specs=VMEM,
         compiler_params=params(4),
         name="prep",
-    )(by_row, scale_low, at)
+    )(*by_row, scale_low, at)
     mu_terms, col_points = pl.pallas_call(
         mu_kernel,
         out_shape=(shape((n_row, n_row, LANES)), shape((n_col, FEATS, LANES))),
@@ -366,11 +362,11 @@
     row_parts, col_parts = pl.pallas_call(
         sides_kernel,
         out_shape=(shape((DEPTH, rows_len), BF16), shape((cols_len, DEPTH), BF16)),
-        in_specs=[VMEM] * 3 + [SMEM],
+        in_specs=[VMEM] * 6 + [SMEM],
         out_specs=(VMEM,) * 2,
         compiler_params=params(4),
         name="sides",
-    )(by_row, col_points, scale_high, at)
+    )(*by_row, col_points, scale_high, at)
     image_terms, target, mu = pl.pallas_call(
         first_kernel,
         out_shape=(shape((n_col, n_col, LANES)), shape((n_row, LANES)), shape((1, LANES))),

time: 108 us -> 104 us (0.963)
  Pallas kernels: 26.5 us -> 22.6 us
    pallas_call x1, Pallas kernels: 12.2 us -> 10.3 us  [local(): pl.pallas_call(mu_kernel, out_shape=(shape((n_row, n_row, LANES)), shape(...]
    all_to_all x2, waiting for transfers between devices: 6.44 us -> 7.92 us  [exchange(): return lax.all_to_all(blocks, axes, 0, 0, tiled=True)]
    pallas_call x1, Pallas kernels: 4.66 us -> 3.49 us  [local(): pl.pallas_call(first_kernel, out_shape=(shape((n_col, n_col, LANES)), sha...]
    ppermute x3 -> x4, waiting for transfers between devices: 5.86 us -> 4.79 us  [exchange_z(): return lax.ppermute(blocks, 'z', [(i, i ^ step) for i in range(size)])]
    ppermute x3 -> x4, starting transfers between devices: 10.3 us -> 9.87 us  [exchange_z(): return lax.ppermute(blocks, 'z', [(i, i ^ step) for i in range(size)])]
  transfers between devices with their start and end apart: 5 -> 6, of which waited for: 4 -> 6; matrix products, arithmetic and copies ran while one was open for 0% -> 0% of each run, Pallas kernels for 2% -> 2%
where the time goes in v5:
time: 104 us
  blocking collectives  40.7 us (39%)
  starting transfers between devices  25.6 us (25%)
  Pallas kernels  22.6 us (22%)
  waiting for transfers between devices  12.7 us (12%)
  between operations  2 us (2%)
    all_to_all x3, blocking collectives, exchange(): return lax.all_to_all(blocks, axes, 0, 0, tiled=True)  38.7 us
    all_to_all x2, starting transfers between devices, exchange(): return lax.all_to_all(blocks, axes, 0, 0, tiled=True)  15.8 us
    pallas_call x1, Pallas kernels, local(): pl.pallas_call(mu_kernel, out_shape=(shape((n_row, n_row, LANES)), shape(...  10.3 us
    ppermute x4, starting transfers between devices, exchange_z(): return lax.ppermute(blocks, 'z', [(i, i ^ step) for i in range(size)])  9.87 us
    all_to_all x2, waiting for transfers between devices, exchange(): return lax.all_to_all(blocks, axes, 0, 0, tiled=True)  7.92 us
    ppermute x4, waiting for transfers between devices, exchange_z(): return lax.ppermute(blocks, 'z', [(i, i ^ step) for i in range(size)])  4.79 us
    pallas_call x1, Pallas kernels, local(): pl.pallas_call(first_kernel, out_shape=(shape((n_col, n_col, LANES)), sha...  3.49 us
    pallas_call x1, Pallas kernels, local(): pl.pallas_call(second_kernel, out_shape=shape((n_row, n_row + 8, LANES)),...  2.98 us
  transfers between devices with their start and end apart: 6, of which 6 were waited for; matrix products, arithmetic and copies ran while one was open for 0% of the time, Pallas kernels for 2%

profile of v5, /device:TPU:32, one launch (start us, length us, event | category | flops | bytes accessed | tf_op | source)
XLA Modules:
  0.0 103.8 jit_solution(17398660950073363004)
XLA Ops:
  0.6 2.0 %all-gather = f32[48,128]{1,0:T(8,128)S(1)} all-gather(f32[24,128]{1,0:T(8,128)} %refs_2_.1), channel_id=2, replica_groups=mesh['y'=4,'core'=2,'x'=4,'z'=8] {'core'}, dimensions={0}, use_global_device_ids=true | all-gather | bytes 36864 | tf_op jit(solution)/shard_map/all_gather | solution.py:316
  2.7 1.9 %pack.1 = (f32[16,128,128]{2,1,0:T(8,128)}, f32[24,128]{1,0:T(8,128)}, f32[24,128]{1,0:T(8,128)}) custom-call(f32[24,512]{1,0:T(8,128)} %refs_0_.1, f32[1,512]{1,0:T(1,128)} %bitcast.12, f32[24,128]{1,0:T(8,128)} %refs_2_.1, f32[24]{0:T(128)} %refs_3_.1, f32[24]{0:T(128)} %refs_4_.1), custom_call_target="tpu_custom_call" | custom-call | tf_op jit(solution)/shard_map/pack/pallas_call | solution.py:318
  4.6 7.0 %all-to-all-start = ((f32[16,128,128]{2,1,0:T(8,128)}), f32[16,128,128]{2,1,0:T(8,128)S(1)}, u32[]{:S(2)}, u32[]{:S(2)}) async-start(f32[16,128,128]{2,1,0:T(8,128)} %get-tuple-element.20), calls=%async_computation | async-start | bytes 2097152 | tf_op jit(solution)/shard_map/all_to_all | solution.py:308
  11.7 6.4 %collective-permute-start = (f32[2,24,128]{2,1,0:T(8,128)S(1)}, f32[2,24,128]{2,1,0:T(8,128)S(1)}, u32[]{:S(2)}, u32[]{:S(2)}) collective-permute-start(f32[2,24,128]{2,1,0:T(8,128)S(1)} %bitcast.10), channel_id=1, source_target_pairs={{0,4},{1,5},{2,6},{3,7},{4,0},{5,1},{6,2},{7,3},{8,12},{9,13},{10,... | collective-permute-start | bytes 73736 | tf_op jit(solution)/shard_map/ppermute | solution.py:304
  18.1 1.8 %collective-permute-done = f32[2,24,128]{2,1,0:T(8,128)S(1)} collective-permute-done((f32[2,24,128]{2,1,0:T(8,128)S(1)}, f32[2,24,128]{2,1,0:T(8,128)S(1)}, u32[]{:S(2)}, u32[]{:S(2)}) %collective-permute-start) | collective-permute-done | bytes 24608 | tf_op jit(solution)/shard_map/ppermute | solution.py:304
  19.9 1.0 collective-permute-start.1
  20.9 2.1 %collective-permute-start.2 = (f32[4,24,128]{2,1,0:T(8,128)S(1)}, f32[4,24,128]{2,1,0:T(8,128)S(1)}, u32[]{:S(2)}, u32[]{:S(2)}) collective-permute-start(f32[4,24,128]{2,1,0:T(8,128)S(1)} %constant_dynamic-update-slice_fusion.refs_0_), channel_id=1, source_target_pairs={{0,2},{1,3},{2,0},{3,1},{4,6},{5,7},{6,4},{7,5},{8,10},{9,11},{10,... | collective-permute-start | bytes 147464 | tf_op jit(solution)/shard_map/ppermute | solution.py:304
  23.0 0.4 collective-permute-start.3
  24.1 0.1 collective-permute-done.1.refs_1_
  24.2 1.8 %collective-permute-done.2.refs_2_ = f32[4,24,128]{2,1,0:T(8,128)S(1)} collective-permute-done((f32[4,24,128]{2,1,0:T(8,128)S(1)}, f32[4,24,128]{2,1,0:T(8,128)S(1)}, u32[]{:S(2)}, u32[]{:S(2)}) %collective-permute-start.2) | collective-permute-done | bytes 49184 | tf_op jit(solution)/shard_map/ppermute | solution.py:304
  25.9 1.1 %collective-permute-done.3.refs_3_ = f32[4,24,128]{2,1,0:T(8,128)S(1)} collective-permute-done((f32[4,24,128]{2,1,0:T(8,128)S(1)}, f32[4,24,128]{2,1,0:T(8,128)S(1)}, u32[]{:S(2)}, u32[]{:S(2)}) %collective-permute-start.3) | collective-permute-done | bytes 49184 | tf_op jit(solution)/shard_map/ppermute | solution.py:304
  27.1 0.9 prep.1.rows_in
  28.0 1.5 %all-to-all-done.held = f32[16,128,128]{2,1,0:T(8,128)S(1)} async-done(((f32[16,128,128]{2,1,0:T(8,128)}), f32[16,128,128]{2,1,0:T(8,128)S(1)}, u32[]{:S(2)}, u32[]{:S(2)}) %all-to-all-start) | async-done | bytes 1048608 | tf_op jit(solution)/shard_map/all_to_all | solution.py:308
  29.5 10.3 %mu.1 = (f32[16,16,128]{2,1,0:T(8,128)}, f32[16,24,128]{2,1,0:T(8,128)S(1)}) custom-call(f32[16,128,128]{2,1,0:T(8,128)S(1)} %all-to-all-done.held, bf16[2048,160]{1,0:T(8,128)(2,1)S(1)} %prep.1.rows_in, f32[24,128]{1,0:T(8,128)S(1)} %copy-done, f32[1,128]{1,0:T(1,128)S(1)} %bitcast.8, f32[1]{0:T(128)S(6)} %copy.12.rho, s32[2]{0:T(128)S(1)} %pad_add_fusion.refs_5_.at.refs_6_), custom_call_target="tpu_custom_call" | custom-call | tf_op jit(solution)/shard_map/mu/pallas_call | solution.py:347
  39.8 8.7 %all-to-all-start.1 = ((f32[16,16,128]{2,1,0:T(8,128)}), f32[16,16,128]{2,1,0:T(8,128)S(1)}, u32[]{:S(2)}, u32[]{:S(2)}) async-start(f32[16,16,128]{2,1,0:T(8,128)} %get-tuple-element.23), calls=%async_computation.1 | async-start | bytes 262144 | tf_op jit(solution)/shard_map/all_to_all | solution.py:308
  49.2 1.1 %sides.1 = (bf16[160,2048]{1,0:T(8,128)(2,1)S(1)}, bf16[2048,160]{1,0:T(8,128)(2,1)S(1)}) custom-call(f32[4,24,128]{2,1,0:T(8,128)S(1)} %constant_dynamic-update-slice_fusion.refs_0_, f32[4,24,128]{2,1,0:T(8,128)S(1)} %collective-permute-done.1.refs_1_, f32[4,24,128]{2,1,0:T(8,128)S(1)} %collective-permute-done.2.refs_2_, ...), custom_call_target="tpu_custom_call" | custom-call | tf_op jit(solution)/shard_map/sides/pallas_call | solution.py:362
  50.3 6.4 %all-to-all-done.1.held = f32[16,16,128]{2,1,0:T(8,128)S(1)} async-done(((f32[16,16,128]{2,1,0:T(8,128)}), f32[16,16,128]{2,1,0:T(8,128)S(1)}, u32[]{:S(2)}, u32[]{:S(2)}) %all-to-all-start.1) | async-done | bytes 131104 | tf_op jit(solution)/shard_map/all_to_all | solution.py:308
  56.7 3.5 %first.1 = (f32[16,16,128]{2,1,0:T(8,128)S(1)}, f32[16,128]{1,0:T(8,128)S(1)}, f32[1,128]{1,0:T(1,128)}) custom-call(f32[16,16,128]{2,1,0:T(8,128)S(1)} %all-to-all-done.1.held, bf16[160,2048]{1,0:T(8,128)(2,1)S(1)} %get-tuple-element.26.rows_in, bf16[2048,160]{1,0:T(8,128)(2,1)S(1)} %get-tuple-element.27.cols_in, f32[1,128]{1,0:T(1,128)S(1)} %bitcast.9, ...), custom_call_target="tpu_custom_call" | custom-call | tf_op jit(solution)/shard_map/first/pallas_call | solution.py:370
  60.2 15.0 %all_to_all.25.held = f32[16,16,128]{2,1,0:T(8,128)S(1)} all-to-all(f32[16,16,128]{2,1,0:T(8,128)S(1)} %get-tuple-element.29), channel_id=1, replica_groups=mesh['y'=4,'core'=2,'x'=4,'z'=8] {'y','x'}, dimensions={0} | all-to-all | bytes 262144 | tf_op jit(solution)/shard_map/all_to_all | solution.py:308
  75.2 3.0 %second.1 = f32[16,24,128]{2,1,0:T(8,128)S(1)} custom-call(f32[16,16,128]{2,1,0:T(8,128)S(1)} %all_to_all.25.held, bf16[160,2048]{1,0:T(8,128)(2,1)S(1)} %get-tuple-element.26.rows_in, bf16[2048,160]{1,0:T(8,128)(2,1)S(1)} %get-tuple-element.27.cols_in, f32[1]{0:T(128)S(6)} %copy.13.noise, s32[2]{0:T(128)S(1)} %pad_add_fusion.refs_5_.at.refs_6_), custom_call_target="tpu_custom_call" | custom-call | tf_op jit(solution)/shard_map/second/pallas_call | solution.py:380
  78.2 13.0 %all_to_all.26.held = f32[16,24,128]{2,1,0:T(8,128)S(1)} all-to-all(f32[16,24,128]{2,1,0:T(8,128)S(1)} %second.1), channel_id=1, replica_groups=mesh['y'=4,'core'=2,'x'=4,'z'=8] {'core','z'}, dimensions={0} | all-to-all | bytes 393216 | tf_op jit(solution)/shard_map/all_to_all | solution.py:308
  91.1 0.7 moments.1
  91.9 10.7 %all_to_all.27.held = f32[16,8,128]{2,1,0:T(8,128)S(1)} all-to-all(f32[16,8,128]{2,1,0:T(8,128)S(1)} %get-tuple-element.31), channel_id=1, replica_groups=mesh['y'=4,'core'=2,'x'=4,'z'=8] {'y','x'}, dimensions={0} | all-to-all | bytes 131072 | tf_op jit(solution)/shard_map/all_to_all | solution.py:308
  102.6 1.2 %final.1 = (f32[1,128]{1,0:T(1,128)}, f32[1,128]{1,0:T(1,128)}) custom-call(f32[16,8,128]{2,1,0:T(8,128)S(1)} %all_to_all.27.held, f32[8,128]{1,0:T(8,128)S(1)} %get-tuple-element.32.own), custom_call_target="tpu_custom_call" | custom-call | tf_op jit(solution)/shard_map/final/pallas_call | solution.py:399
  (9 shorter events, 0.1 us)
Async XLA Ops:
  4.6 24.9 %all-to-all-start = ((f32[16,128,128]{2,1,0:T(8,128)}), f32[16,128,128]{2,1,0:T(8,128)S(1)}, u32[]{:S(2)}, u32[]{:S(2)}) async-start(f32[16,128,128]{2,1,0:T(8,128)} %get-tuple-element.20), calls=%async_computation | async-start | bytes 2097152 | tf_op jit(solution)/shard_map/all_to_all | solution.py:308
  11.7 8.2 %collective-permute-start = (f32[2,24,128]{2,1,0:T(8,128)S(1)}, f32[2,24,128]{2,1,0:T(8,128)S(1)}, u32[]{:S(2)}, u32[]{:S(2)}) collective-permute-start(f32[2,24,128]{2,1,0:T(8,128)S(1)} %bitcast.10), channel_id=1, source_target_pairs={{0,4},{1,5},{2,6},{3,7},{4,0},{5,1},{6,2},{7,3},{8,12},{9,13},{10,... | collective-permute-start | bytes 73736 | tf_op jit(solution)/shard_map/ppermute | solution.py:304
  19.9 7.2 %copy-start = (f32[24,128]{1,0:T(8,128)S(1)}, f32[24,128]{1,0:T(8,128)}, u32[]{:S(2)}) copy-start(f32[24,128]{1,0:T(8,128)} %get-tuple-element.22.refs_4_.scale) | copy-start | bytes 36868
  19.9 4.3 %collective-permute-start.1 = (f32[4,24,128]{2,1,0:T(8,128)S(1)}, f32[4,24,128]{2,1,0:T(8,128)S(1)}, u32[]{:S(2)}, u32[]{:S(2)}) collective-permute-start(f32[4,24,128]{2,1,0:T(8,128)S(1)} %constant_dynamic-update-slice_fusion.refs_0_), channel_id=1, source_target_pairs={{0,1},{1,0},{2,3},{3,2},{4,5},{5,4},{6,7},{7,6},{8,9},{9,8},{10,11... | collective-permute-start | bytes 147464 | tf_op jit(solution)/shard_map/ppermute | solution.py:304
  20.9 5.1 %collective-permute-start.2 = (f32[4,24,128]{2,1,0:T(8,128)S(1)}, f32[4,24,128]{2,1,0:T(8,128)S(1)}, u32[]{:S(2)}, u32[]{:S(2)}) collective-permute-start(f32[4,24,128]{2,1,0:T(8,128)S(1)} %constant_dynamic-update-slice_fusion.refs_0_), channel_id=1, source_target_pairs={{0,2},{1,3},{2,0},{3,1},{4,6},{5,7},{6,4},{7,5},{8,10},{9,11},{10,... | collective-permute-start | bytes 147464 | tf_op jit(solution)/shard_map/ppermute | solution.py:304
  23.0 4.1 %collective-permute-start.3 = (f32[4,24,128]{2,1,0:T(8,128)S(1)}, f32[4,24,128]{2,1,0:T(8,128)S(1)}, u32[]{:S(2)}, u32[]{:S(2)}) collective-permute-start(f32[4,24,128]{2,1,0:T(8,128)S(1)} %constant_dynamic-update-slice_fusion.refs_0_), channel_id=1, source_target_pairs={{0,3},{1,2},{2,1},{3,0},{4,7},{5,6},{6,5},{7,4},{8,11},{9,10},{10,... | collective-permute-start | bytes 147464 | tf_op jit(solution)/shard_map/ppermute | solution.py:304
  28.0 1.5 %copy-start.2 = (f32[128]{0:T(128)S(1)}, f32[128]{0:T(128)}, u32[]{:S(2)}) copy-start(f32[128]{0:T(128)} %param.11) | copy-start | bytes 1540
  39.8 9.4 %copy-start.1 = (f32[24,128]{1,0:T(8,128)S(1)}, f32[24,128]{1,0:T(8,128)}, u32[]{:S(2)}) copy-start(f32[24,128]{1,0:T(8,128)} %get-tuple-element.25.refs_5_) | copy-start | bytes 36868
  39.8 16.9 %all-to-all-start.1 = ((f32[16,16,128]{2,1,0:T(8,128)}), f32[16,16,128]{2,1,0:T(8,128)S(1)}, u32[]{:S(2)}, u32[]{:S(2)}) async-start(f32[16,16,128]{2,1,0:T(8,128)} %get-tuple-element.23), calls=%async_computation.1 | async-start | bytes 262144 | tf_op jit(solution)/shard_map/all_to_all | solution.py:308

commit v6 on v5

--- a/solution.py
+++ b/solution.py
@@ -70,42 +70,48 @@
     return jnp.concatenate([high, mid, low, high, mid, high, norms, jnp.zeros_like(norms)], 0)
 
 
-def pack_kernel(*refs):
-    sources, (out_col, scale_low, scale_high), held, sems = refs[:5], refs[5:8], refs[8:13], refs[13]
+def pack_kernel(runs_hbm, weights_hbm, points_hbm, out, runs, weights, points, block, sems, out_sems):
+    sources, held = (runs_hbm, weights_hbm, points_hbm), (runs, weights, points)
     copies = [pltpu.make_async_copy(a, b, sems.at[i]) for i, (a, b) in enumerate(zip(sources, held))]
     for copy in copies:
         copy.start()
     for copy in copies:
         copy.wait()
-    runs, weights, points, len_low, len_high = held
-    row = lax.broadcasted_iota(jnp.int32, (FEATS, LANES), 0)
-    for lengths, out in ((len_low, scale_low), (len_high, scale_high)):
-        column = jnp.ones((FEATS, LANES), F32)
-        for i in range(FEATS):
-            column = jnp.where(row == i, lengths[i], column)
-        out[...] = ROOT / column
-    own = points[...]
     last = jnp.broadcast_to(weights[:, :LANES], (8, LANES))
     row = lax.broadcasted_iota(jnp.int32, (8, LANES), 0)
-    for q in range(1, RUN_BLOCKS):
-        last = jnp.where(row == q, weights[:, q * LANES : (q + 1) * LANES], last)
-    for i in range(out_col.shape[0]):
-        for q in range(RUN_BLOCKS):
-            out_col[i, q * FEATS : (q + 1) * FEATS, :] = runs[:, q * LANES : (q + 1) * LANES]
-        out_col[i, RUN_BLOCKS * FEATS : PACKED - 8, :] = own
-        out_col[i, PACKED - 8 :, :] = last
-
-
-def place_of(j, m, at):
-    block = (m & 1) * 8 + ((at[0] & 7) ^ (j ^ 4 * (m >> 1)))
+    for q in range(RUN_BLOCKS):
+        lanes = slice(q * LANES, (q + 1) * LANES)
+        block[q * FEATS : (q + 1) * FEATS, :] = runs[:, lanes]
+        if q:
+            last = jnp.where(row == q, weights[:, lanes], last)
+    block[RUN_BLOCKS * FEATS : PACKED - 8, :] = points[...]
+    block[PACKED - 8 :, :] = last
+    copies = [pltpu.make_async_copy(block, out.at[i], out_sems.at[i]) for i in range(out.shape[0])]
+    for copy in copies:
+        copy.start()
+    for copy in copies:
+        copy.wait()
+
+
+def scale_column(lengths):
+    row = lax.broadcasted_iota(jnp.int32, (FEATS, LANES), 0)
+    column = jnp.ones((FEATS, LANES), F32)
+    for i in range(FEATS):
+        column = jnp.where(row == i, lengths[i], column)
+    return ROOT / column
+
+
+def place_of(m, at):
+    block = (m >> 3) * 8 + ((at[0] & 7) ^ (m >> 1 & 3) ^ 4 * (m & 1))
     return pl.ds(pl.multiple_of(block * LANES, LANES), LANES)
 
 
-def prep_kernel(*refs):
-    points, scale, at, out = refs[:4], refs[4], refs[5], refs[6]
-    for j, ref in enumerate(points):
-        for m in range(ref.shape[0]):
-            out[place_of(j, m, at), :] = left(ref[m], scale[...]).T.astype(BF16)
+def prep_kernel(points, len_low, len_high, high, at, out, scale_low, scale_high, high_out):
+    scale_low[...] = scale_column(len_low)
+    scale_high[...] = scale_column(len_high)
+    high_out[...] = high[...]
+    for m in range(points.shape[0]):
+        out[place_of(m, at), :] = left(points[m], scale_low[...]).T.astype(BF16)
 
 
 def column_of(line, out, rows):
@@ -160,11 +166,9 @@
     return jnp.concatenate([line[:, k : k + LANES] for k in range(0, line.shape[1], LANES)], 0)
 
 
-def sides_kernel(*refs):
-    points, (cols, scale, at, rows_out, cols_out) = refs[:4], refs[4:]
-    for j, ref in enumerate(points):
-        for m in range(ref.shape[0]):
-            rows_out[:, place_of(j, m, at)] = left(ref[m], scale[...]).astype(BF16)
+def sides_kernel(points, cols, scale, at, rows_out, cols_out):
+    for m in range(points.shape[0]):
+        rows_out[:, place_of(m, at)] = left(points[m], scale[...]).astype(BF16)
     for k in range(cols.shape[0]):
         cols_out[k * LANES : (k + 1) * LANES, :] = right(cols[k], scale[...]).T.astype(BF16)
 
@@ -270,23 +274,21 @@
         for shift in (4, 2, 1):
             high, low = pair_add((high, low), (pltpu.roll(high, shift, 0), pltpu.roll(low, shift, 0)))
         for j in range(out.shape[0]):
-            out[j, 2 * i : 2 * i + 1, :] = high[:1]
-            out[j, 2 * i + 1 : 2 * i + 2, :] = low[:1]
+            out[j, i : i + 1, :] = high[:1]
+            out[j, 4 + i : 5 + i, :] = low[:1]
     own = lax.broadcasted_iota(jnp.int32, b.shape, 0) == at[0]
     for i, v in enumerate((b, image, last)):
         own_out[i : i + 1, :] = jnp.sum(jnp.where(own, v, 0.0), axis=0, keepdims=True)
 
 
 def final_kernel(held, own, x_out, r_out):
-    sums = []
-    for i in range(4):
-        h = jnp.concatenate([held[j, 2 * i : 2 * i + 1, :] for j in range(held.shape[0])], 0)
-        l = jnp.concatenate([held[j, 2 * i + 1 : 2 * i + 2, :] for j in range(held.shape[0])], 0)
-        h, l = fold_rows((h, l))
-        for axis, shifts in ((0, (4, 2, 1)), (1, (64, 32, 16, 8, 4, 2, 1))):
-            for shift in shifts:
-                h, l = pair_add((h, l), (pltpu.roll(h, shift, axis), pltpu.roll(l, shift, axis)))
-        sums.append((h[:1], l[:1]))
+    pairs = [(held[j], pltpu.roll(held[j], 4, 0)) for j in range(held.shape[0])]
+    while len(pairs) > 1:
+        pairs = [pair_add(a, b) for a, b in zip(pairs[::2], pairs[1::2])]
+    h, l = pairs[0]
+    for shift in (64, 32, 16, 8, 4, 2, 1):
+        h, l = pair_add((h, l), (pltpu.roll(h, shift, 1), pltpu.roll(l, shift, 1)))
+    sums = [(h[i : i + 1], l[i : i + 1]) for i in range(4)]
     m0, m1, m2, m3 = sums
     alpha = pair_ratio(m0, m1)
     ratio = pair_ratio(m2, m1)
@@ -313,37 +315,37 @@
     at = jnp.stack([lax.axis_index(ROWS), lax.axis_index(COLS)]).astype(jnp.int32)
     high = high.reshape(1, LANES)
     cols_len, rows_len = n_col * LANES, n_row * LANES
-    near_core = lax.all_gather(points, "core", axis=0)
-    near_core, weights = lax.optimization_barrier((near_core, weights))
-    to_col, scale_low, scale_high = pl.pallas_call(
+    size = lax.axis_size("z")
+    to_col = pl.pallas_call(
         pack_kernel,
-        out_shape=(shape((n_col, PACKED, LANES)), shape((FEATS, LANES)), shape((FEATS, LANES))),
-        in_specs=[HBM] * 5,
-        out_specs=(VMEM,) * 3,
+        out_shape=shape((n_col, PACKED, LANES)),
+        in_specs=[HBM] * 3,
+        out_specs=HBM,
         scratch_shapes=[
             pltpu.VMEM((FEATS, RUN_BLOCKS * LANES), F32),
             pltpu.VMEM((1, RUN_BLOCKS * LANES), F32),
             pltpu.VMEM((FEATS, LANES), F32),
-            pltpu.SMEM((FEATS,), F32),
-            pltpu.SMEM((FEATS,), F32),
-            pltpu.SemaphoreType.DMA((5,)),
+            pltpu.VMEM((PACKED, LANES), F32),
+            pltpu.SemaphoreType.DMA((3,)),
+            pltpu.SemaphoreType.DMA((n_col,)),
         ],
         compiler_params=params(60),
         name="pack",
-    )(runs, weights.reshape(1, RUN_BLOCKS * LANES), points, len_low, len_high)
+    )(runs, weights.reshape(1, RUN_BLOCKS * LANES), points)
+    far = exchange_z(points, 4, size)
+    to_col, far = lax.optimization_barrier((to_col, far))
     by_col = exchange(to_col, COLS)
-    size = lax.axis_size("z")
-    near = exchange_z(near_core, 4, size)
-    near = jnp.concatenate([near_core, near], 0)
-    by_row = [near] + [exchange_z(near, step, size) for step in (1, 2, 3)]
-    row_low = pl.pallas_call(
+    near = jnp.stack([points, far])
+    by_row = jnp.concatenate([near] + [exchange_z(near, step, size) for step in (1, 2, 3)], 0)
+    by_row = lax.all_gather(by_row, "core", axis=0, tiled=True)
+    row_low, scale_low, scale_high, high = pl.pallas_call(
         prep_kernel,
-        out_shape=shape((rows_len, DEPTH), BF16),
-        in_specs=[VMEM] * 5 + [SMEM],
-        out_specs=VMEM,
+        out_shape=(shape((rows_len, DEPTH), BF16), shape((FEATS, LANES)), shape((FEATS, LANES)), shape((1, LANES))),
+        in_specs=[VMEM, SMEM, SMEM, VMEM, SMEM],
+        out_specs=(VMEM,) * 4,
         compiler_params=params(4),
         name="prep",
-    )(*by_row, scale_low, at)
+    )(by_row, len_low, len_high, high, at)
     mu_terms, col_points = pl.pallas_call(
         mu_kernel,
         out_shape=(shape((n_row, n_row, LANES)), shape((n_col, FEATS, LANES))),
@@ -362,11 +364,11 @@
     row_parts, col_parts = pl.pallas_call(
         sides_kernel,
         out_shape=(shape((DEPTH, rows_len), BF16), shape((cols_len, DEPTH), BF16)),
-        in_specs=[VMEM] * 6 + [SMEM],
+        in_specs=[VMEM] * 3 + [SMEM],
         out_specs=(VMEM,) * 2,
         compiler_params=params(4),
         name="sides",
-    )(*by_row, col_points, scale_high, at)
+    )(by_row, col_points, scale_high, at)
     image_terms, target, mu = pl.pallas_call(
         first_kernel,
         out_shape=(shape((n_col, n_col, LANES)), shape((n_row, LANES)), shape((1, LANES))),

time: 104 us -> 103 us (level)
  blocking collectives: 40.7 us -> 37.2 us
  waiting for transfers between devices: 12.7 us -> 15.7 us
  starting transfers between devices: 25.6 us -> 24.2 us
    all_to_all x2, waiting for transfers between devices: 7.92 us -> 12.3 us  [exchange(): return lax.all_to_all(blocks, axes, 0, 0, tiled=True)]
    all_to_all x3, blocking collectives: 38.7 us -> 35.1 us  [exchange(): return lax.all_to_all(blocks, axes, 0, 0, tiled=True)]
    all_to_all x2, starting transfers between devices: 15.8 us -> 14.3 us  [exchange(): return lax.all_to_all(blocks, axes, 0, 0, tiled=True)]
    ppermute x4, waiting for transfers between devices: 4.79 us -> 3.35 us  [exchange_z(): return lax.ppermute(blocks, 'z', [(i, i ^ step) for i in range(size)])]
  transfers between devices with their start and end apart: 6 -> 6, of which waited for: 6 -> 5; matrix products, arithmetic and copies ran while one was open for 0% -> 0% of each run, Pallas kernels for 2% -> 4%
where the time goes in v6:
time: 103 us
  blocking collectives  37.2 us (36%)
  starting transfers between devices  24.2 us (23%)
  Pallas kernels  22.6 us (22%)
  waiting for transfers between devices  15.7 us (15%)
  between operations  2.04 us (2%)
    all_to_all x3, blocking collectives, exchange(): return lax.all_to_all(blocks, axes, 0, 0, tiled=True)  35.1 us
    all_to_all x2, starting transfers between devices, exchange(): return lax.all_to_all(blocks, axes, 0, 0, tiled=True)  14.3 us
    all_to_all x2, waiting for transfers between devices, exchange(): return lax.all_to_all(blocks, axes, 0, 0, tiled=True)  12.3 us
    pallas_call x1, Pallas kernels, local(): pl.pallas_call(mu_kernel, out_shape=(shape((n_row, n_row, LANES)), shape(...  10.3 us
    ppermute x4, starting transfers between devices, exchange_z(): return lax.ppermute(blocks, 'z', [(i, i ^ step) for i in range(size)])  9.95 us
    pallas_call x1, Pallas kernels, local(): pl.pallas_call(first_kernel, out_shape=(shape((n_col, n_col, LANES)), sha...  3.47 us
    ppermute x4, waiting for transfers between devices, exchange_z(): return lax.ppermute(blocks, 'z', [(i, i ^ step) for i in range(size)])  3.35 us
    pallas_call x1, Pallas kernels, local(): pl.pallas_call(second_kernel, out_shape=shape((n_row, n_row + 8, LANES)),...  2.97 us
  transfers between devices with their start and end apart: 6, of which 5 were waited for; matrix products, arithmetic and copies ran while one was open for 0% of the time, Pallas kernels for 4%

profile of v6, /device:TPU:32, one launch (start us, length us, event | category | flops | bytes accessed | tf_op | source)
XLA Modules:
  0.0 102.6 jit_solution(17665991522075661550)
XLA Ops:
  0.6 6.4 %collective-permute-start = (f32[24,128]{1,0:T(8,128)}, f32[24,128]{1,0:T(8,128)S(1)}, u32[]{:S(2)}, u32[]{:S(2)}) collective-permute-start(f32[24,128]{1,0:T(8,128)} %points_hbm.1), channel_id=1, source_target_pairs={{0,4},{1,5},{2,6},{3,7},{4,0},{5,1},{6,2},{7,3},{8,12},{9,13},{10,... | collective-permute-start | bytes 36872 | tf_op jit(solution)/shard_map/ppermute | solution.py:306
  7.0 2.0 %pack.1 = f32[16,128,128]{2,1,0:T(8,128)} custom-call(f32[24,512]{1,0:T(8,128)} %runs_hbm.1, f32[1,512]{1,0:T(1,128)} %bitcast.14, f32[24,128]{1,0:T(8,128)} %points_hbm.1), custom_call_target="tpu_custom_call" | custom-call | tf_op jit(solution)/shard_map/pack/pallas_call | solution.py:319
  9.0 7.0 %all-to-all-start = ((f32[16,128,128]{2,1,0:T(8,128)}), f32[16,128,128]{2,1,0:T(8,128)S(1)}, u32[]{:S(2)}, u32[]{:S(2)}) async-start(f32[16,128,128]{2,1,0:T(8,128)} %pack.1), calls=%async_computation | async-start | bytes 2097152 | tf_op jit(solution)/shard_map/all_to_all | solution.py:310
  16.8 1.1 %collective-permute-start.1 = (f32[2,24,128]{2,1,0:T(8,128)S(1)}, f32[2,24,128]{2,1,0:T(8,128)S(1)}, u32[]{:S(2)}, u32[]{:S(2)}) collective-permute-start(f32[2,24,128]{2,1,0:T(8,128)S(1)} %pad_maximum_fusion), channel_id=1, source_target_pairs={{0,1},{1,0},{2,3},{3,2},{4,5},{5,4},{6,7},{7,6},{8,9},{9,8},{10,11... | collective-permute-start | bytes 73736 | tf_op jit(solution)/shard_map/ppermute | solution.py:306
  17.9 2.0 %collective-permute-start.2 = (f32[2,24,128]{2,1,0:T(8,128)S(1)}, f32[2,24,128]{2,1,0:T(8,128)S(1)}, u32[]{:S(2)}, u32[]{:S(2)}) collective-permute-start(f32[2,24,128]{2,1,0:T(8,128)S(1)} %pad_maximum_fusion), channel_id=1, source_target_pairs={{0,2},{1,3},{2,0},{3,1},{4,6},{5,7},{6,4},{7,5},{8,10},{9,11},{10,... | collective-permute-start | bytes 73736 | tf_op jit(solution)/shard_map/ppermute | solution.py:306
  19.9 0.5 collective-permute-start.3
  20.4 0.5 collective-permute-done.1
  20.9 1.7 %collective-permute-done.2 = f32[2,24,128]{2,1,0:T(8,128)S(1)} collective-permute-done((f32[2,24,128]{2,1,0:T(8,128)S(1)}, f32[2,24,128]{2,1,0:T(8,128)S(1)}, u32[]{:S(2)}, u32[]{:S(2)}) %collective-permute-start.2) | collective-permute-done | bytes 24608 | tf_op jit(solution)/shard_map/ppermute | solution.py:306
  22.7 1.1 %collective-permute-done.3 = f32[2,24,128]{2,1,0:T(8,128)S(1)} collective-permute-done((f32[2,24,128]{2,1,0:T(8,128)S(1)}, f32[2,24,128]{2,1,0:T(8,128)S(1)}, u32[]{:S(2)}, u32[]{:S(2)}) %collective-permute-start.3) | collective-permute-done | bytes 24608 | tf_op jit(solution)/shard_map/ppermute | solution.py:306
  23.8 2.1 %all_gather.3.points = f32[16,24,128]{2,1,0:T(8,128)S(1)} all-gather(f32[8,24,128]{2,1,0:T(8,128)S(1)} %constant_dynamic-update-slice_fusion), channel_id=1, replica_groups=mesh['y'=4,'core'=2,'x'=4,'z'=8] {'core'}, dimensions={0}, use_global_device_ids=true | all-gather | bytes 294912 | tf_op jit(solution)/shard_map/all_gather | solution.py:340
  25.9 0.6 copy-done
  26.6 0.9 prep.1
  27.5 5.9 %all-to-all-done.held = f32[16,128,128]{2,1,0:T(8,128)S(1)} async-done(((f32[16,128,128]{2,1,0:T(8,128)}), f32[16,128,128]{2,1,0:T(8,128)S(1)}, u32[]{:S(2)}, u32[]{:S(2)}) %all-to-all-start) | async-done | bytes 1048608 | tf_op jit(solution)/shard_map/all_to_all | solution.py:310
  33.4 10.3 %mu.1 = (f32[16,16,128]{2,1,0:T(8,128)}, f32[16,24,128]{2,1,0:T(8,128)S(1)}) custom-call(f32[16,128,128]{2,1,0:T(8,128)S(1)} %all-to-all-done.held, bf16[2048,160]{1,0:T(8,128)(2,1)S(1)} %get-tuple-element.22.rows_in, f32[24,128]{1,0:T(8,128)S(1)} %get-tuple-element.23.scale, f32[1,128]{1,0:T(1,128)S(1)} %get-tuple-element.24.high, f32[1]{0:T(128)S(6)} %copy.15.rho, ...), custom_call_target="tpu_custom_call" | custom-call | tf_op jit(solution)/shard_map/mu/pallas_call | solution.py:349
  43.7 7.2 %all-to-all-start.1 = ((f32[16,16,128]{2,1,0:T(8,128)}), f32[16,16,128]{2,1,0:T(8,128)S(1)}, u32[]{:S(2)}, u32[]{:S(2)}) async-start(f32[16,16,128]{2,1,0:T(8,128)} %get-tuple-element.25), calls=%async_computation.1 | async-start | bytes 262144 | tf_op jit(solution)/shard_map/all_to_all | solution.py:310
  51.5 1.1 %sides.1 = (bf16[160,2048]{1,0:T(8,128)(2,1)S(1)}, bf16[2048,160]{1,0:T(8,128)(2,1)S(1)}) custom-call(f32[16,24,128]{2,1,0:T(8,128)S(1)} %all_gather.3.points, f32[16,24,128]{2,1,0:T(8,128)S(1)} %get-tuple-element.26.cols, f32[24,128]{1,0:T(8,128)S(1)} %get-tuple-element.27.scale, s32[2]{0:T(128)S(1)} %pad_add_fusion.at), custom_call_target="tpu_custom_call" | custom-call | tf_op jit(solution)/shard_map/sides/pallas_call | solution.py:364
  52.7 6.4 %all-to-all-done.1.held = f32[16,16,128]{2,1,0:T(8,128)S(1)} async-done(((f32[16,16,128]{2,1,0:T(8,128)}), f32[16,16,128]{2,1,0:T(8,128)S(1)}, u32[]{:S(2)}, u32[]{:S(2)}) %all-to-all-start.1) | async-done | bytes 131104 | tf_op jit(solution)/shard_map/all_to_all | solution.py:310
  59.1 3.5 %first.1 = (f32[16,16,128]{2,1,0:T(8,128)S(1)}, f32[16,128]{1,0:T(8,128)S(1)}, f32[1,128]{1,0:T(1,128)}) custom-call(f32[16,16,128]{2,1,0:T(8,128)S(1)} %all-to-all-done.1.held, bf16[160,2048]{1,0:T(8,128)(2,1)S(1)} %get-tuple-element.28.rows_in, bf16[2048,160]{1,0:T(8,128)(2,1)S(1)} %get-tuple-element.29.cols_in, f32[1,128]{1,0:T(1,128)S(1)} %get-tuple-element.24.high, ...), custom_call_target="tpu_custom_call" | custom-call | tf_op jit(solution)/shard_map/first/pallas_call | solution.py:372
  62.6 11.4 %all_to_all.25.held = f32[16,16,128]{2,1,0:T(8,128)S(1)} all-to-all(f32[16,16,128]{2,1,0:T(8,128)S(1)} %get-tuple-element.31), channel_id=1, replica_groups=mesh['y'=4,'core'=2,'x'=4,'z'=8] {'y','x'}, dimensions={0} | all-to-all | bytes 262144 | tf_op jit(solution)/shard_map/all_to_all | solution.py:310
  74.0 3.0 %second.1 = f32[16,24,128]{2,1,0:T(8,128)S(1)} custom-call(f32[16,16,128]{2,1,0:T(8,128)S(1)} %all_to_all.25.held, bf16[160,2048]{1,0:T(8,128)(2,1)S(1)} %get-tuple-element.28.rows_in, bf16[2048,160]{1,0:T(8,128)(2,1)S(1)} %get-tuple-element.29.cols_in, f32[1]{0:T(128)S(6)} %copy.16.noise, s32[2]{0:T(128)S(1)} %pad_add_fusion.at), custom_call_target="tpu_custom_call" | custom-call | tf_op jit(solution)/shard_map/second/pallas_call | solution.py:382
  76.9 13.0 %all_to_all.26.held = f32[16,24,128]{2,1,0:T(8,128)S(1)} all-to-all(f32[16,24,128]{2,1,0:T(8,128)S(1)} %second.1), channel_id=1, replica_groups=mesh['y'=4,'core'=2,'x'=4,'z'=8] {'core','z'}, dimensions={0} | all-to-all | bytes 393216 | tf_op jit(solution)/shard_map/all_to_all | solution.py:310
  89.9 0.7 moments.1
  90.6 10.7 %all_to_all.27.held = f32[16,8,128]{2,1,0:T(8,128)S(1)} all-to-all(f32[16,8,128]{2,1,0:T(8,128)S(1)} %get-tuple-element.33), channel_id=1, replica_groups=mesh['y'=4,'core'=2,'x'=4,'z'=8] {'y','x'}, dimensions={0} | all-to-all | bytes 131072 | tf_op jit(solution)/shard_map/all_to_all | solution.py:310
  101.4 1.2 %final.1 = (f32[1,128]{1,0:T(1,128)}, f32[1,128]{1,0:T(1,128)}) custom-call(f32[16,8,128]{2,1,0:T(8,128)S(1)} %all_to_all.27.held, f32[8,128]{1,0:T(8,128)S(1)} %get-tuple-element.34.own), custom_call_target="tpu_custom_call" | custom-call | tf_op jit(solution)/shard_map/final/pallas_call | solution.py:401
  (15 shorter events, 0.1 us)
Async XLA Ops:
  0.6 8.4 %collective-permute-start = (f32[24,128]{1,0:T(8,128)}, f32[24,128]{1,0:T(8,128)S(1)}, u32[]{:S(2)}, u32[]{:S(2)}) collective-permute-start(f32[24,128]{1,0:T(8,128)} %points_hbm.1), channel_id=1, source_target_pairs={{0,4},{1,5},{2,6},{3,7},{4,0},{5,1},{6,2},{7,3},{8,12},{9,13},{10,... | collective-permute-start | bytes 36872 | tf_op jit(solution)/shard_map/ppermute | solution.py:306
  9.0 7.8 %copy-start.3 = (f32[24,128]{1,0:T(8,128)S(1)}, f32[24,128]{1,0:T(8,128)}, u32[]{:S(2)}) copy-start(f32[24,128]{1,0:T(8,128)} %points_hbm.1) | copy-start | bytes 36868
  9.0 24.4 %all-to-all-start = ((f32[16,128,128]{2,1,0:T(8,128)}), f32[16,128,128]{2,1,0:T(8,128)S(1)}, u32[]{:S(2)}, u32[]{:S(2)}) async-start(f32[16,128,128]{2,1,0:T(8,128)} %pack.1), calls=%async_computation | async-start | bytes 2097152 | tf_op jit(solution)/shard_map/all_to_all | solution.py:310
  16.8 4.1 %collective-permute-start.1 = (f32[2,24,128]{2,1,0:T(8,128)S(1)}, f32[2,24,128]{2,1,0:T(8,128)S(1)}, u32[]{:S(2)}, u32[]{:S(2)}) collective-permute-start(f32[2,24,128]{2,1,0:T(8,128)S(1)} %pad_maximum_fusion), channel_id=1, source_target_pairs={{0,1},{1,0},{2,3},{3,2},{4,5},{5,4},{6,7},{7,6},{8,9},{9,8},{10,11... | collective-permute-start | bytes 73736 | tf_op jit(solution)/shard_map/ppermute | solution.py:306
  17.9 4.7 %collective-permute-start.2 = (f32[2,24,128]{2,1,0:T(8,128)S(1)}, f32[2,24,128]{2,1,0:T(8,128)S(1)}, u32[]{:S(2)}, u32[]{:S(2)}) collective-permute-start(f32[2,24,128]{2,1,0:T(8,128)S(1)} %pad_maximum_fusion), channel_id=1, source_target_pairs={{0,2},{1,3},{2,0},{3,1},{4,6},{5,7},{6,4},{7,5},{8,10},{9,11},{10,... | collective-permute-start | bytes 73736 | tf_op jit(solution)/shard_map/ppermute | solution.py:306
  19.9 3.8 %collective-permute-start.3 = (f32[2,24,128]{2,1,0:T(8,128)S(1)}, f32[2,24,128]{2,1,0:T(8,128)S(1)}, u32[]{:S(2)}, u32[]{:S(2)}) collective-permute-start(f32[2,24,128]{2,1,0:T(8,128)S(1)} %pad_maximum_fusion), channel_id=1, source_target_pairs={{0,3},{1,2},{2,1},{3,0},{4,7},{5,6},{6,5},{7,4},{8,11},{9,10},{10,... | collective-permute-start | bytes 73736 | tf_op jit(solution)/shard_map/ppermute | solution.py:306
  25.9 0.7 copy-start
  25.9 0.7 copy-start.1
  25.9 0.7 copy-start.2
  43.7 15.4 %all-to-all-start.1 = ((f32[16,16,128]{2,1,0:T(8,128)}), f32[16,16,128]{2,1,0:T(8,128)S(1)}, u32[]{:S(2)}, u32[]{:S(2)}) async-start(f32[16,16,128]{2,1,0:T(8,128)} %get-tuple-element.25), calls=%async_computation.1 | async-start | bytes 262144 | tf_op jit(solution)/shard_map/all_to_all | solution.py:310

commit v7 on v6

--- a/solution.py
+++ b/solution.py
@@ -106,12 +106,14 @@
     return pl.ds(pl.multiple_of(block * LANES, LANES), LANES)
 
 
-def prep_kernel(points, len_low, len_high, high, at, out, scale_low, scale_high, high_out):
+def prep_kernel(points, len_low, len_high, high, at, out, rows_out, scale_low, scale_high, high_out):
     scale_low[...] = scale_column(len_low)
     scale_high[...] = scale_column(len_high)
     high_out[...] = high[...]
     for m in range(points.shape[0]):
-        out[place_of(m, at), :] = left(points[m], scale_low[...]).T.astype(BF16)
+        place = place_of(m, at)
+        out[place, :] = left(points[m], scale_low[...]).T.astype(BF16)
+        rows_out[:, place] = left(points[m], scale_high[...]).astype(BF16)
 
 
 def column_of(line, out, rows):
@@ -125,7 +127,7 @@
     return jnp.sum(term.reshape(count // 8, 8, wide), axis=0)
 
 
-def mu_kernel(held, rows_in, scale, high, rho, at, out, cols_out, even, odd, total, lines):
+def mu_kernel(held, rows_in, scale, scale_high, high, rho, noise, at, out, cols_out, even, odd, total, lines):
     blocks = held.shape[0]
 
     def side(r):
@@ -149,8 +151,8 @@
         if r + 1 < blocks:
             held_sides[(r + 1) % 2][...] = side(r + 1)
         work(r, held_sides[r % 2])
-    for r in range(blocks):
-        cols_out[r] = held[r, RUN_BLOCKS * FEATS : PACKED - 8, :]
+        cols = right(held[r, RUN_BLOCKS * FEATS : PACKED - 8, :], scale_high[...])
+        cols_out[r * LANES : (r + 1) * LANES, :] = cols.T.astype(BF16)
     for k in range(lines.shape[0]):
         lines[k : k + 1, :] = jnp.sum(total[k * LANES : (k + 1) * LANES, :].T, axis=0, keepdims=True)
     mu = lines[...]
@@ -164,13 +166,6 @@
 def lines_of(total):
     line = jnp.sum(total[...], axis=0, keepdims=True)
     return jnp.concatenate([line[:, k : k + LANES] for k in range(0, line.shape[1], LANES)], 0)
-
-
-def sides_kernel(points, cols, scale, at, rows_out, cols_out):
-    for m in range(points.shape[0]):
-        rows_out[:, place_of(m, at)] = left(points[m], scale[...]).astype(BF16)
-    for k in range(cols.shape[0]):
-        cols_out[k * LANES : (k + 1) * LANES, :] = right(cols[k], scale[...]).T.astype(BF16)
 
 
 def first_kernel(held, rows_in, cols_in, high, rho, noise, at, out, target_out, mu_out, sums):
@@ -338,18 +333,24 @@
     near = jnp.stack([points, far])
     by_row = jnp.concatenate([near] + [exchange_z(near, step, size) for step in (1, 2, 3)], 0)
     by_row = lax.all_gather(by_row, "core", axis=0, tiled=True)
-    row_low, scale_low, scale_high, high = pl.pallas_call(
+    row_low, row_parts, scale_low, scale_high, high = pl.pallas_call(
         prep_kernel,
-        out_shape=(shape((rows_len, DEPTH), BF16), shape((FEATS, LANES)), shape((FEATS, LANES)), shape((1, LANES))),
+        out_shape=(
+            shape((rows_len, DEPTH), BF16),
+            shape((DEPTH, rows_len), BF16),
+            shape((FEATS, LANES)),
+            shape((FEATS, LANES)),
+            shape((1, LANES)),
+        ),
         in_specs=[VMEM, SMEM, SMEM, VMEM, SMEM],
-        out_specs=(VMEM,) * 4,
+        out_specs=(VMEM,) * 5,
         compiler_params=params(4),
         name="prep",
     )(by_row, len_low, len_high, high, at)
-    mu_terms, col_points = pl.pallas_call(
+    mu_terms, col_parts = pl.pallas_call(
         mu_kernel,
-        out_shape=(shape((n_row, n_row, LANES)), shape((n_col, FEATS, LANES))),
-        in_specs=[VMEM] * 4 + [SMEM] * 2,
+        out_shape=(shape((n_row, n_row, LANES)), shape((cols_len, DEPTH), BF16)),
+        in_specs=[VMEM] * 5 + [SMEM] * 3,
         out_specs=(VMEM,) * 2,
         scratch_shapes=[
             pltpu.VMEM((DEPTH, RUN_BLOCKS * LANES), BF16),
@@ -359,16 +360,8 @@
         ],
         compiler_params=params(16),
         name="mu",
-    )(by_col, row_low, scale_low, high, rho, at)
+    )(by_col, row_low, scale_low, scale_high, high, rho, noise, at)
     mu_held = exchange(mu_terms, ROWS)
-    row_parts, col_parts = pl.pallas_call(
-        sides_kernel,
-        out_shape=(shape((DEPTH, rows_len), BF16), shape((cols_len, DEPTH), BF16)),
-        in_specs=[VMEM] * 3 + [SMEM],
-        out_specs=(VMEM,) * 2,
-        compiler_params=params(4),
-        name="sides",
-    )(by_row, col_points, scale_high, at)
     image_terms, target, mu = pl.pallas_call(
         first_kernel,
         out_shape=(shape((n_col, n_col, LANES)), shape((n_row, LANES)), shape((1, LANES))),

time: 103 us -> 102 us (level)
  blocking collectives: 37.2 us -> 52.1 us
  waiting for transfers between devices: 15.7 us -> 7.45 us
  starting transfers between devices: 24.2 us -> 17.9 us
  Pallas kernels: 22.6 us -> 21.4 us
    all_to_all x3 -> x4, blocking collectives: 35.1 us -> 49.9 us  [exchange(): return lax.all_to_all(blocks, axes, 0, 0, tiled=True)]
    all_to_all x2 -> x1, waiting for transfers between devices: 12.3 us -> 4.64 us  [exchange(): return lax.all_to_all(blocks, axes, 0, 0, tiled=True)]
    all_to_all x2 -> x1, starting transfers between devices: 14.3 us -> 7.05 us  [exchange(): return lax.all_to_all(blocks, axes, 0, 0, tiled=True)]
    pallas_call x1 -> x0, Pallas kernels: 1.11 us -> none  [local(): pl.pallas_call(sides_kernel, out_shape=(shape((DEPTH, rows_len), BF16), s...]
  transfers between devices with their start and end apart: 6 -> 5, of which waited for: 5 -> 2; matrix products, arithmetic and copies ran while one was open for 0% -> 0% of each run, Pallas kernels for 4% -> 3%
where the time goes in v7:
time: 102 us
  blocking collectives  52.1 us (51%)
  Pallas kernels  21.4 us (21%)
  starting transfers between devices  17.9 us (18%)
  waiting for transfers between devices  7.45 us (7%)
  between operations  2.03 us (2%)
    all_to_all x4, blocking collectives, exchange(): return lax.all_to_all(blocks, axes, 0, 0, tiled=True)  49.9 us
    ppermute x4, starting transfers between devices, exchange_z(): return lax.ppermute(blocks, 'z', [(i, i ^ step) for i in range(size)])  10.9 us
    pallas_call x1, Pallas kernels, local(): pl.pallas_call(mu_kernel, out_shape=(shape((n_row, n_row, LANES)), shape(...  9.96 us
    all_to_all x1, starting transfers between devices, exchange(): return lax.all_to_all(blocks, axes, 0, 0, tiled=True)  7.05 us
    all_to_all x1, waiting for transfers between devices, exchange(): return lax.all_to_all(blocks, axes, 0, 0, tiled=True)  4.64 us
    pallas_call x1, Pallas kernels, local(): pl.pallas_call(first_kernel, out_shape=(shape((n_col, n_col, LANES)), sha...  3.5 us
    pallas_call x1, Pallas kernels, local(): pl.pallas_call(second_kernel, out_shape=shape((n_row, n_row + 8, LANES)),...  2.97 us
    ppermute x4, waiting for transfers between devices, exchange_z(): return lax.ppermute(blocks, 'z', [(i, i ^ step) for i in range(size)])  2.81 us
  transfers between devices with their start and end apart: 5, of which 2 were waited for; matrix products, arithmetic and copies ran while one was open for 0% of the time, Pallas kernels for 3%

profile of v7, /device:TPU:32, one launch (start us, length us, event | category | flops | bytes accessed | tf_op | source)
XLA Modules:
  0.0 101.6 jit_solution(10564420439262418285)
XLA Ops:
  0.6 6.4 %collective-permute-start = (f32[24,128]{1,0:T(8,128)}, f32[24,128]{1,0:T(8,128)S(1)}, u32[]{:S(2)}, u32[]{:S(2)}) collective-permute-start(f32[24,128]{1,0:T(8,128)} %points_hbm.1), channel_id=1, source_target_pairs={{0,4},{1,5},{2,6},{3,7},{4,0},{5,1},{6,2},{7,3},{8,12},{9,13},{10,... | collective-permute-start | bytes 36872 | tf_op jit(solution)/shard_map/ppermute | solution.py:301
  7.0 2.0 %pack.1 = f32[16,128,128]{2,1,0:T(8,128)} custom-call(f32[24,512]{1,0:T(8,128)} %runs_hbm.1, f32[1,512]{1,0:T(1,128)} %bitcast.14, f32[24,128]{1,0:T(8,128)} %points_hbm.1), custom_call_target="tpu_custom_call" | custom-call | tf_op jit(solution)/shard_map/pack/pallas_call | solution.py:314
  9.0 0.0 copy-start.3
  9.0 7.0 %all-to-all-start = ((f32[16,128,128]{2,1,0:T(8,128)}), f32[16,128,128]{2,1,0:T(8,128)S(1)}, u32[]{:S(2)}, u32[]{:S(2)}) async-start(f32[16,128,128]{2,1,0:T(8,128)} %pack.1), calls=%async_computation | async-start | bytes 2097152 | tf_op jit(solution)/shard_map/all_to_all | solution.py:305
  16.0 0.1 pad_add_fusion.at
  17.5 1.7 %collective-permute-start.3 = (f32[2,24,128]{2,1,0:T(8,128)S(1)}, f32[2,24,128]{2,1,0:T(8,128)S(1)}, u32[]{:S(2)}, u32[]{:S(2)}) collective-permute-start(f32[2,24,128]{2,1,0:T(8,128)S(1)} %pad_maximum_fusion), channel_id=1, source_target_pairs={{0,3},{1,2},{2,1},{3,0},{4,7},{5,6},{6,5},{7,4},{8,11},{9,10},{10,... | collective-permute-start | bytes 73736 | tf_op jit(solution)/shard_map/ppermute | solution.py:301
  19.1 1.8 %collective-permute-start.2 = (f32[2,24,128]{2,1,0:T(8,128)S(1)}, f32[2,24,128]{2,1,0:T(8,128)S(1)}, u32[]{:S(2)}, u32[]{:S(2)}) collective-permute-start(f32[2,24,128]{2,1,0:T(8,128)S(1)} %pad_maximum_fusion), channel_id=1, source_target_pairs={{0,2},{1,3},{2,0},{3,1},{4,6},{5,7},{6,4},{7,5},{8,10},{9,11},{10,... | collective-permute-start | bytes 73736 | tf_op jit(solution)/shard_map/ppermute | solution.py:301
  20.9 1.0 %collective-permute-start.1 = (f32[2,24,128]{2,1,0:T(8,128)S(1)}, f32[2,24,128]{2,1,0:T(8,128)S(1)}, u32[]{:S(2)}, u32[]{:S(2)}) collective-permute-start(f32[2,24,128]{2,1,0:T(8,128)S(1)} %pad_maximum_fusion), channel_id=1, source_target_pairs={{0,1},{1,0},{2,3},{3,2},{4,5},{5,4},{6,7},{7,6},{8,9},{9,8},{10,11... | collective-permute-start | bytes 73736 | tf_op jit(solution)/shard_map/ppermute | solution.py:301
  21.9 2.8 %collective-permute-done.1 = f32[2,24,128]{2,1,0:T(8,128)S(1)} collective-permute-done((f32[2,24,128]{2,1,0:T(8,128)S(1)}, f32[2,24,128]{2,1,0:T(8,128)S(1)}, u32[]{:S(2)}, u32[]{:S(2)}) %collective-permute-start.1) | collective-permute-done | bytes 24608 | tf_op jit(solution)/shard_map/ppermute | solution.py:301
  24.8 2.1 %all_gather.3.points = f32[16,24,128]{2,1,0:T(8,128)S(1)} all-gather(f32[8,24,128]{2,1,0:T(8,128)S(1)} %constant_dynamic-update-slice_fusion), channel_id=1, replica_groups=mesh['y'=4,'core'=2,'x'=4,'z'=8] {'core'}, dimensions={0}, use_global_device_ids=true | all-gather | bytes 294912 | tf_op jit(solution)/shard_map/all_gather | solution.py:335
  26.9 0.6 copy-done
  27.6 0.0 copy-done.1
  27.6 0.0 copy-done.2
  27.6 1.1 %prep.1 = (bf16[2048,160]{1,0:T(8,128)(2,1)S(1)}, bf16[160,2048]{1,0:T(8,128)(2,1)S(1)}, f32[24,128]{1,0:T(8,128)S(1)}, f32[24,128]{1,0:T(8,128)S(1)}, f32[1,128]{1,0:T(1,128)S(1)}) custom-call(f32[16,24,128]{2,1,0:T(8,128)S(1)} %all_gather.3.points, f32[24]{0:T(128)S(1)} %copy-done, f32[24]{0:T(128)S(1)} %copy-done.1, f32[1,128]{1,0:T(1,128)S(1)} %bitcast.11, ...), custom_call_target="tpu_custom_call" | custom-call | tf_op jit(solution)/shard_map/prep/pallas_call | solution.py:336
  28.7 4.6 %all-to-all-done.held = f32[16,128,128]{2,1,0:T(8,128)S(1)} async-done(((f32[16,128,128]{2,1,0:T(8,128)}), f32[16,128,128]{2,1,0:T(8,128)S(1)}, u32[]{:S(2)}, u32[]{:S(2)}) %all-to-all-start) | async-done | bytes 1048608 | tf_op jit(solution)/shard_map/all_to_all | solution.py:305
  33.4 10.0 %mu.1 = (f32[16,16,128]{2,1,0:T(8,128)S(1)}, bf16[2048,160]{1,0:T(8,128)(2,1)S(1)}) custom-call(f32[16,128,128]{2,1,0:T(8,128)S(1)} %all-to-all-done.held, bf16[2048,160]{1,0:T(8,128)(2,1)S(1)} %get-tuple-element.21.rows_in, f32[24,128]{1,0:T(8,128)S(1)} %get-tuple-element.22.scale, f32[24,128]{1,0:T(8,128)S(1)} %get-tuple-element.23.scale_high, ...), custom_call_target="tpu_custom_call" | custom-call | tf_op jit(solution)/shard_map/mu/pallas_call | solution.py:350
  43.3 15.3 %all_to_all.25.held = f32[16,16,128]{2,1,0:T(8,128)S(1)} all-to-all(f32[16,16,128]{2,1,0:T(8,128)S(1)} %get-tuple-element.25), channel_id=1, replica_groups=mesh['y'=4,'core'=2,'x'=4,'z'=8] {'core','z'}, dimensions={0} | all-to-all | bytes 262144 | tf_op jit(solution)/shard_map/all_to_all | solution.py:305
  58.6 3.5 %first.1 = (f32[16,16,128]{2,1,0:T(8,128)S(1)}, f32[16,128]{1,0:T(8,128)S(1)}, f32[1,128]{1,0:T(1,128)}) custom-call(f32[16,16,128]{2,1,0:T(8,128)S(1)} %all_to_all.25.held, bf16[160,2048]{1,0:T(8,128)(2,1)S(1)} %get-tuple-element.26.rows_in, bf16[2048,160]{1,0:T(8,128)(2,1)S(1)} %get-tuple-element.27.cols_in, f32[1,128]{1,0:T(1,128)S(1)} %get-tuple-element.24.high, ...), custom_call_target="tpu_custom_call" | custom-call | tf_op jit(solution)/shard_map/first/pallas_call | solution.py:365
  62.1 10.9 %all_to_all.26.held = f32[16,16,128]{2,1,0:T(8,128)S(1)} all-to-all(f32[16,16,128]{2,1,0:T(8,128)S(1)} %get-tuple-element.29), channel_id=1, replica_groups=mesh['y'=4,'core'=2,'x'=4,'z'=8] {'y','x'}, dimensions={0} | all-to-all | bytes 262144 | tf_op jit(solution)/shard_map/all_to_all | solution.py:305
  73.0 3.0 %second.1 = f32[16,24,128]{2,1,0:T(8,128)S(1)} custom-call(f32[16,16,128]{2,1,0:T(8,128)S(1)} %all_to_all.26.held, bf16[160,2048]{1,0:T(8,128)(2,1)S(1)} %get-tuple-element.26.rows_in, bf16[2048,160]{1,0:T(8,128)(2,1)S(1)} %get-tuple-element.27.cols_in, f32[1]{0:T(128)S(6)} %copy.16.noise, s32[2]{0:T(128)S(1)} %pad_add_fusion.at), custom_call_target="tpu_custom_call" | custom-call | tf_op jit(solution)/shard_map/second/pallas_call | solution.py:375
  76.0 13.0 %all_to_all.27.held = f32[16,24,128]{2,1,0:T(8,128)S(1)} all-to-all(f32[16,24,128]{2,1,0:T(8,128)S(1)} %second.1), channel_id=1, replica_groups=mesh['y'=4,'core'=2,'x'=4,'z'=8] {'core','z'}, dimensions={0} | all-to-all | bytes 393216 | tf_op jit(solution)/shard_map/all_to_all | solution.py:305
  89.0 0.7 moments.1
  89.7 10.7 %all_to_all.28.held = f32[16,8,128]{2,1,0:T(8,128)S(1)} all-to-all(f32[16,8,128]{2,1,0:T(8,128)S(1)} %get-tuple-element.31), channel_id=1, replica_groups=mesh['y'=4,'core'=2,'x'=4,'z'=8] {'y','x'}, dimensions={0} | all-to-all | bytes 131072 | tf_op jit(solution)/shard_map/all_to_all | solution.py:305
  100.5 1.2 %final.1 = (f32[1,128]{1,0:T(1,128)}, f32[1,128]{1,0:T(1,128)}) custom-call(f32[16,8,128]{2,1,0:T(8,128)S(1)} %all_to_all.28.held, f32[8,128]{1,0:T(8,128)S(1)} %get-tuple-element.32.own), custom_call_target="tpu_custom_call" | custom-call | tf_op jit(solution)/shard_map/final/pallas_call | solution.py:394
  (13 shorter events, 0.0 us)
Async XLA Ops:
  0.6 8.3 %collective-permute-start = (f32[24,128]{1,0:T(8,128)}, f32[24,128]{1,0:T(8,128)S(1)}, u32[]{:S(2)}, u32[]{:S(2)}) collective-permute-start(f32[24,128]{1,0:T(8,128)} %points_hbm.1), channel_id=1, source_target_pairs={{0,4},{1,5},{2,6},{3,7},{4,0},{5,1},{6,2},{7,3},{8,12},{9,13},{10,... | collective-permute-start | bytes 36872 | tf_op jit(solution)/shard_map/ppermute | solution.py:301
  9.0 8.4 %copy-start.3 = (f32[24,128]{1,0:T(8,128)S(1)}, f32[24,128]{1,0:T(8,128)}, u32[]{:S(2)}) copy-start(f32[24,128]{1,0:T(8,128)} %points_hbm.1) | copy-start | bytes 36868
  9.0 24.4 %all-to-all-start = ((f32[16,128,128]{2,1,0:T(8,128)}), f32[16,128,128]{2,1,0:T(8,128)S(1)}, u32[]{:S(2)}, u32[]{:S(2)}) async-start(f32[16,128,128]{2,1,0:T(8,128)} %pack.1), calls=%async_computation | async-start | bytes 2097152 | tf_op jit(solution)/shard_map/all_to_all | solution.py:305
  17.5 7.3 %collective-permute-start.3 = (f32[2,24,128]{2,1,0:T(8,128)S(1)}, f32[2,24,128]{2,1,0:T(8,128)S(1)}, u32[]{:S(2)}, u32[]{:S(2)}) collective-permute-start(f32[2,24,128]{2,1,0:T(8,128)S(1)} %pad_maximum_fusion), channel_id=1, source_target_pairs={{0,3},{1,2},{2,1},{3,0},{4,7},{5,6},{6,5},{7,4},{8,11},{9,10},{10,... | collective-permute-start | bytes 73736 | tf_op jit(solution)/shard_map/ppermute | solution.py:301
  19.1 5.6 %collective-permute-start.2 = (f32[2,24,128]{2,1,0:T(8,128)S(1)}, f32[2,24,128]{2,1,0:T(8,128)S(1)}, u32[]{:S(2)}, u32[]{:S(2)}) collective-permute-start(f32[2,24,128]{2,1,0:T(8,128)S(1)} %pad_maximum_fusion), channel_id=1, source_target_pairs={{0,2},{1,3},{2,0},{3,1},{4,6},{5,7},{6,4},{7,5},{8,10},{9,11},{10,... | collective-permute-start | bytes 73736 | tf_op jit(solution)/shard_map/ppermute | solution.py:301
  20.9 3.8 %collective-permute-start.1 = (f32[2,24,128]{2,1,0:T(8,128)S(1)}, f32[2,24,128]{2,1,0:T(8,128)S(1)}, u32[]{:S(2)}, u32[]{:S(2)}) collective-permute-start(f32[2,24,128]{2,1,0:T(8,128)S(1)} %pad_maximum_fusion), channel_id=1, source_target_pairs={{0,1},{1,0},{2,3},{3,2},{4,5},{5,4},{6,7},{7,6},{8,9},{9,8},{10,11... | collective-permute-start | bytes 73736 | tf_op jit(solution)/shard_map/ppermute | solution.py:301
  26.9 0.7 copy-start
  26.9 0.7 copy-start.1
  26.9 0.7 copy-start.2

commit v8 on v7

--- a/solution.py
+++ b/solution.py
@@ -70,13 +70,23 @@
     return jnp.concatenate([high, mid, low, high, mid, high, norms, jnp.zeros_like(norms)], 0)
 
 
-def pack_kernel(runs_hbm, weights_hbm, points_hbm, out, runs, weights, points, block, sems, out_sems):
-    sources, held = (runs_hbm, weights_hbm, points_hbm), (runs, weights, points)
+def scale_column(lengths):
+    row = lax.broadcasted_iota(jnp.int32, (FEATS, LANES), 0)
+    column = jnp.ones((FEATS, LANES), F32)
+    for i in range(FEATS):
+        column = jnp.where(row == i, lengths[i], column)
+    return ROOT / column
+
+
+def pack_kernel(*refs):
+    sources, (out, scale_low, scale_high) = refs[:5], refs[5:8]
+    held, (block, sems, out_sems) = refs[8:13], refs[13:]
     copies = [pltpu.make_async_copy(a, b, sems.at[i]) for i, (a, b) in enumerate(zip(sources, held))]
     for copy in copies:
         copy.start()
     for copy in copies:
         copy.wait()
+    runs, weights, points, len_low, len_high = held
     last = jnp.broadcast_to(weights[:, :LANES], (8, LANES))
     row = lax.broadcasted_iota(jnp.int32, (8, LANES), 0)
     for q in range(RUN_BLOCKS):
@@ -89,16 +99,10 @@
     copies = [pltpu.make_async_copy(block, out.at[i], out_sems.at[i]) for i in range(out.shape[0])]
     for copy in copies:
         copy.start()
+    scale_low[...] = scale_column(len_low)
+    scale_high[...] = scale_column(len_high)
     for copy in copies:
         copy.wait()
-
-
-def scale_column(lengths):
-    row = lax.broadcasted_iota(jnp.int32, (FEATS, LANES), 0)
-    column = jnp.ones((FEATS, LANES), F32)
-    for i in range(FEATS):
-        column = jnp.where(row == i, lengths[i], column)
-    return ROOT / column
 
 
 def place_of(m, at):
@@ -106,9 +110,7 @@
     return pl.ds(pl.multiple_of(block * LANES, LANES), LANES)
 
 
-def prep_kernel(points, len_low, len_high, high, at, out, rows_out, scale_low, scale_high, high_out):
-    scale_low[...] = scale_column(len_low)
-    scale_high[...] = scale_column(len_high)
+def prep_kernel(points, scale_low, scale_high, high, at, out, rows_out, high_out):
     high_out[...] = high[...]
     for m in range(points.shape[0]):
         place = place_of(m, at)
@@ -210,10 +212,10 @@
     last = lines_of(total)
     row = lax.broadcasted_iota(jnp.int32, last.shape, 0)
     last = jnp.where(row == at[0], last + noise[0] * own, last)
-    extra = jnp.broadcast_to(own, (8, LANES))
     for i in range(out.shape[0]):
-        out[i, : last.shape[0], :] = last
-        out[i, last.shape[0] :, :] = extra
+        for k in range(last.shape[0]):
+            out[i, k] = last[k : k + 1, :]
+        out[i, last.shape[0]] = own
 
 
 def two_sum(a, b):
@@ -261,8 +263,9 @@
 
 def moments_kernel(held, target, at, out, own_out):
     count = target.shape[0]
-    last = jnp.sum(held[:, :count, :], axis=0)
-    image = held[:, count, :]
+    senders = range(held.shape[0])
+    last = jnp.concatenate([sum(held[j, k] for j in senders) for k in range(count)], 0)
+    image = jnp.concatenate([held[j, count] for j in senders], 0)
     b = target[...]
     for i, (p, q) in enumerate(((b, b), (b, image), (image, image), (image, last))):
         high, low = fold_rows(product(p, q))
@@ -311,42 +314,37 @@
     high = high.reshape(1, LANES)
     cols_len, rows_len = n_col * LANES, n_row * LANES
     size = lax.axis_size("z")
-    to_col = pl.pallas_call(
+    to_col, scale_low, scale_high = pl.pallas_call(
         pack_kernel,
-        out_shape=shape((n_col, PACKED, LANES)),
-        in_specs=[HBM] * 3,
-        out_specs=HBM,
+        out_shape=(shape((n_col, PACKED, LANES)), shape((FEATS, LANES)), shape((FEATS, LANES))),
+        in_specs=[HBM] * 5,
+        out_specs=(HBM, VMEM, VMEM),
         scratch_shapes=[
             pltpu.VMEM((FEATS, RUN_BLOCKS * LANES), F32),
             pltpu.VMEM((1, RUN_BLOCKS * LANES), F32),
             pltpu.VMEM((FEATS, LANES), F32),
+            pltpu.SMEM((FEATS,), F32),
+            pltpu.SMEM((FEATS,), F32),
             pltpu.VMEM((PACKED, LANES), F32),
-            pltpu.SemaphoreType.DMA((3,)),
+            pltpu.SemaphoreType.DMA((5,)),
             pltpu.SemaphoreType.DMA((n_col,)),
         ],
         compiler_params=params(60),
         name="pack",
-    )(runs, weights.reshape(1, RUN_BLOCKS * LANES), points)
+    )(runs, weights.reshape(1, RUN_BLOCKS * LANES), points, len_low, len_high)
     far = exchange_z(points, 4, size)
-    to_col, far = lax.optimization_barrier((to_col, far))
     by_col = exchange(to_col, COLS)
     near = jnp.stack([points, far])
     by_row = jnp.concatenate([near] + [exchange_z(near, step, size) for step in (1, 2, 3)], 0)
     by_row = lax.all_gather(by_row, "core", axis=0, tiled=True)
-    row_low, row_parts, scale_low, scale_high, high = pl.pallas_call(
+    row_low, row_parts, high = pl.pallas_call(
         prep_kernel,
-        out_shape=(
-            shape((rows_len, DEPTH), BF16),
-            shape((DEPTH, rows_len), BF16),
-            shape((FEATS, LANES)),
-            shape((FEATS, LANES)),
-            shape((1, LANES)),
-        ),
-        in_specs=[VMEM, SMEM, SMEM, VMEM, SMEM],
-        out_specs=(VMEM,) * 5,
+        out_shape=(shape((rows_len, DEPTH), BF16), shape((DEPTH, rows_len), BF16), shape((1, LANES))),
+        in_specs=[VMEM] * 4 + [SMEM],
+        out_specs=(VMEM,) * 3,
         compiler_params=params(4),
         name="prep",
-    )(by_row, len_low, len_high, high, at)
+    )(by_row, scale_low, scale_high, high, at)
     mu_terms, col_parts = pl.pallas_call(
         mu_kernel,
         out_shape=(shape((n_row, n_row, LANES)), shape((cols_len, DEPTH), BF16)),
@@ -374,7 +372,7 @@
     image_held = exchange(image_terms, COLS)
     last_terms = pl.pallas_call(
         second_kernel,
-        out_shape=shape((n_row, n_row + 8, LANES)),
+        out_shape=shape((n_row, n_row + 1, 1, LANES)),
         in_specs=[VMEM] * 3 + [SMEM] * 2,
         out_specs=VMEM,
         scratch_shapes=[pltpu.VMEM((cols_len, LANES), F32), pltpu.VMEM((8, rows_len), F32)],

time: 102 us -> 97.9 us (0.960)
  blocking collectives: 52.1 us -> 47.4 us
    all_to_all x4, blocking collectives: 49.9 us -> 45.3 us  [exchange(): return lax.all_to_all(blocks, axes, 0, 0, tiled=True)]
  transfers between devices with their start and end apart: 5 -> 5, of which waited for: 2 -> 2; matrix products, arithmetic and copies ran while one was open for 0% -> 0% of each run, Pallas kernels for 3% -> 4%
where the time goes in v8:
time: 97.9 us; the launch traced here: 97.4 us
  blocking collectives  47.4 us (48%)
  Pallas kernels  21.8 us (22%)
  starting transfers between devices  17 us (17%)
  waiting for transfers between devices  7.69 us (8%)
  between operations  2.04 us (2%)
  local copies, waits for them, and re-layouts  1.37 us (1%)
    all_to_all x4, blocking collectives, exchange(): return lax.all_to_all(blocks, axes, 0, 0, tiled=True)  45.3 us
    ppermute x4, starting transfers between devices, exchange_z(): return lax.ppermute(blocks, 'z', [(i, i ^ step) for i in range(size)])  9.95 us
    pallas_call x1, Pallas kernels, local(): pl.pallas_call(mu_kernel, out_shape=(shape((n_row, n_row, LANES)), shape(...  9.79 us
    all_to_all x1, starting transfers between devices, exchange(): return lax.all_to_all(blocks, axes, 0, 0, tiled=True)  7.05 us
    all_to_all x1, waiting for transfers between devices, exchange(): return lax.all_to_all(blocks, axes, 0, 0, tiled=True)  3.98 us
    ppermute x4, waiting for transfers between devices, exchange_z(): return lax.ppermute(blocks, 'z', [(i, i ^ step) for i in range(size)])  3.71 us
    pallas_call x1, Pallas kernels, local(): pl.pallas_call(first_kernel, out_shape=(shape((n_col, n_col, LANES)), sha...  3.49 us
    pallas_call x1, Pallas kernels, local(): pl.pallas_call(second_kernel, out_shape=shape((n_row, n_row + 1, 1, LANES...  2.98 us
  transfers between devices with their start and end apart: 5, of which 2 were waited for; matrix products, arithmetic and copies ran while one was open for 0% of the time, Pallas kernels for 4%

profile of v8, /device:TPU:32, one launch (start us, length us, event | category | flops | bytes accessed | tf_op | source)
XLA Modules:
  0.0 97.4 jit_solution(18268698660527854938)
XLA Ops:
  0.6 6.4 %collective-permute-start = (f32[24,128]{1,0:T(8,128)}, f32[24,128]{1,0:T(8,128)S(1)}, u32[]{:S(2)}, u32[]{:S(2)}) collective-permute-start(f32[24,128]{1,0:T(8,128)} %refs_2_.1), channel_id=1, source_target_pairs={{0,4},{1,5},{2,6},{3,7},{4,0},{5,1},{6,2},{7,3},{8,12},{9,13},{10,... | collective-permute-start | bytes 36872 | tf_op jit(solution)/shard_map/ppermute | solution.py:304
  7.0 2.6 %pack.1 = (f32[16,128,128]{2,1,0:T(8,128)}, f32[24,128]{1,0:T(8,128)}, f32[24,128]{1,0:T(8,128)}) custom-call(f32[24,512]{1,0:T(8,128)} %refs_0_.1, f32[1,512]{1,0:T(1,128)} %bitcast.14, f32[24,128]{1,0:T(8,128)} %refs_2_.1, f32[24]{0:T(128)} %refs_3_.1, f32[24]{0:T(128)} %refs_4_.1), custom_call_target="tpu_custom_call" | custom-call | tf_op jit(solution)/shard_map/pack/pallas_call | solution.py:317
  9.6 7.0 %all-to-all-start = ((f32[16,128,128]{2,1,0:T(8,128)}), f32[16,128,128]{2,1,0:T(8,128)S(1)}, u32[]{:S(2)}, u32[]{:S(2)}) async-start(f32[16,128,128]{2,1,0:T(8,128)} %get-tuple-element.18), calls=%async_computation | async-start | bytes 2097152 | tf_op jit(solution)/shard_map/all_to_all | solution.py:308
  16.7 0.0 copy-start.3
  16.7 0.7 copy-done.3
  17.4 0.1 pad_add_fusion.at
  18.8 0.0 collective-permute-done
  18.8 1.1 %collective-permute-start.3 = (f32[2,24,128]{2,1,0:T(8,128)S(1)}, f32[2,24,128]{2,1,0:T(8,128)S(1)}, u32[]{:S(2)}, u32[]{:S(2)}) collective-permute-start(f32[2,24,128]{2,1,0:T(8,128)S(1)} %pad_maximum_fusion), channel_id=1, source_target_pairs={{0,3},{1,2},{2,1},{3,0},{4,7},{5,6},{6,5},{7,4},{8,11},{9,10},{10,... | collective-permute-start | bytes 73736 | tf_op jit(solution)/shard_map/ppermute | solution.py:304
  19.9 2.4 %collective-permute-start.2 = (f32[2,24,128]{2,1,0:T(8,128)S(1)}, f32[2,24,128]{2,1,0:T(8,128)S(1)}, u32[]{:S(2)}, u32[]{:S(2)}) collective-permute-start(f32[2,24,128]{2,1,0:T(8,128)S(1)} %pad_maximum_fusion), channel_id=1, source_target_pairs={{0,2},{1,3},{2,0},{3,1},{4,6},{5,7},{6,4},{7,5},{8,10},{9,11},{10,... | collective-permute-start | bytes 73736 | tf_op jit(solution)/shard_map/ppermute | solution.py:304
  22.2 0.1 collective-permute-start.1
  22.4 3.7 %collective-permute-done.1 = f32[2,24,128]{2,1,0:T(8,128)S(1)} collective-permute-done((f32[2,24,128]{2,1,0:T(8,128)S(1)}, f32[2,24,128]{2,1,0:T(8,128)S(1)}, u32[]{:S(2)}, u32[]{:S(2)}) %collective-permute-start.1) | collective-permute-done | bytes 24608 | tf_op jit(solution)/shard_map/ppermute | solution.py:304
  26.1 2.1 %all_gather.3.points = f32[16,24,128]{2,1,0:T(8,128)S(1)} all-gather(f32[8,24,128]{2,1,0:T(8,128)S(1)} %constant_dynamic-update-slice_fusion), channel_id=1, replica_groups=mesh['y'=4,'core'=2,'x'=4,'z'=8] {'core'}, dimensions={0}, use_global_device_ids=true | all-gather | bytes 294912 | tf_op jit(solution)/shard_map/all_gather | solution.py:339
  28.3 0.6 copy-done.2
  28.9 1.1 %prep.1 = (bf16[2048,160]{1,0:T(8,128)(2,1)S(1)}, bf16[160,2048]{1,0:T(8,128)(2,1)S(1)}, f32[1,128]{1,0:T(1,128)S(1)}) custom-call(f32[16,24,128]{2,1,0:T(8,128)S(1)} %all_gather.3.points, f32[24,128]{1,0:T(8,128)S(1)} %copy-done, f32[24,128]{1,0:T(8,128)S(1)} %copy-done.1, f32[1,128]{1,0:T(1,128)S(1)} %bitcast.11, s32[2]{0:T(128)S(1)} %pad_add_fusion.at), custom_call_target="tpu_custom_call" | custom-call | tf_op jit(solution)/shard_map/prep/pallas_call | solution.py:340
  30.0 4.0 %all-to-all-done.held = f32[16,128,128]{2,1,0:T(8,128)S(1)} async-done(((f32[16,128,128]{2,1,0:T(8,128)}), f32[16,128,128]{2,1,0:T(8,128)S(1)}, u32[]{:S(2)}, u32[]{:S(2)}) %all-to-all-start) | async-done | bytes 1048608 | tf_op jit(solution)/shard_map/all_to_all | solution.py:308
  34.0 9.8 %mu.1 = (f32[16,16,128]{2,1,0:T(8,128)S(1)}, bf16[2048,160]{1,0:T(8,128)(2,1)S(1)}) custom-call(f32[16,128,128]{2,1,0:T(8,128)S(1)} %all-to-all-done.held, bf16[2048,160]{1,0:T(8,128)(2,1)S(1)} %get-tuple-element.21.rows_in, f32[24,128]{1,0:T(8,128)S(1)} %copy-done, f32[24,128]{1,0:T(8,128)S(1)} %copy-done.1, f32[1,128]{1,0:T(1,128)S(1)} %get-tuple-element.22.high, ...), custom_call_target="tpu_custom_call" | custom-call | tf_op jit(solution)/shard_map/mu/pallas_call | solution.py:348
  43.8 12.2 %all_to_all.25.held = f32[16,16,128]{2,1,0:T(8,128)S(1)} all-to-all(f32[16,16,128]{2,1,0:T(8,128)S(1)} %get-tuple-element.23), channel_id=1, replica_groups=mesh['y'=4,'core'=2,'x'=4,'z'=8] {'core','z'}, dimensions={0} | all-to-all | bytes 262144 | tf_op jit(solution)/shard_map/all_to_all | solution.py:308
  56.0 3.5 %first.1 = (f32[16,16,128]{2,1,0:T(8,128)S(1)}, f32[16,128]{1,0:T(8,128)S(1)}, f32[1,128]{1,0:T(1,128)}) custom-call(f32[16,16,128]{2,1,0:T(8,128)S(1)} %all_to_all.25.held, bf16[160,2048]{1,0:T(8,128)(2,1)S(1)} %get-tuple-element.24.rows_in, bf16[2048,160]{1,0:T(8,128)(2,1)S(1)} %get-tuple-element.25.cols_in, f32[1,128]{1,0:T(1,128)S(1)} %get-tuple-element.22.high, ...), custom_call_target="tpu_custom_call" | custom-call | tf_op jit(solution)/shard_map/first/pallas_call | solution.py:363
  59.5 10.6 %all_to_all.26.held = f32[16,16,128]{2,1,0:T(8,128)S(1)} all-to-all(f32[16,16,128]{2,1,0:T(8,128)S(1)} %get-tuple-element.27), channel_id=1, replica_groups=mesh['y'=4,'core'=2,'x'=4,'z'=8] {'y','x'}, dimensions={0} | all-to-all | bytes 262144 | tf_op jit(solution)/shard_map/all_to_all | solution.py:308
  70.1 3.0 %second.1 = f32[16,17,1,128]{3,2,1,0:T(1,128)S(1)} custom-call(f32[16,16,128]{2,1,0:T(8,128)S(1)} %all_to_all.26.held, bf16[160,2048]{1,0:T(8,128)(2,1)S(1)} %get-tuple-element.24.rows_in, bf16[2048,160]{1,0:T(8,128)(2,1)S(1)} %get-tuple-element.25.cols_in, f32[1]{0:T(128)S(6)} %copy.16.noise, s32[2]{0:T(128)S(1)} %pad_add_fusion.at), custom_call_target="tpu_custom_call" | custom-call | tf_op jit(solution)/shard_map/second/pallas_call | solution.py:373
  73.1 11.7 %all_to_all.27.held = f32[16,17,1,128]{3,2,1,0:T(1,128)S(1)} all-to-all(f32[16,17,1,128]{3,2,1,0:T(1,128)S(1)} %second.1), channel_id=1, replica_groups=mesh['y'=4,'core'=2,'x'=4,'z'=8] {'core','z'}, dimensions={0} | all-to-all | bytes 278528 | tf_op jit(solution)/shard_map/all_to_all | solution.py:308
  84.8 0.7 moments.1
  85.5 10.7 %all_to_all.28.held = f32[16,8,128]{2,1,0:T(8,128)S(1)} all-to-all(f32[16,8,128]{2,1,0:T(8,128)S(1)} %get-tuple-element.29), channel_id=1, replica_groups=mesh['y'=4,'core'=2,'x'=4,'z'=8] {'y','x'}, dimensions={0} | all-to-all | bytes 131072 | tf_op jit(solution)/shard_map/all_to_all | solution.py:308
  96.3 1.2 %final.1 = (f32[1,128]{1,0:T(1,128)}, f32[1,128]{1,0:T(1,128)}) custom-call(f32[16,8,128]{2,1,0:T(8,128)S(1)} %all_to_all.28.held, f32[8,128]{1,0:T(8,128)S(1)} %get-tuple-element.30.own), custom_call_target="tpu_custom_call" | custom-call | tf_op jit(solution)/shard_map/final/pallas_call | solution.py:392
  (13 shorter events, 0.0 us)
Async XLA Ops:
  0.6 18.1 %collective-permute-start = (f32[24,128]{1,0:T(8,128)}, f32[24,128]{1,0:T(8,128)S(1)}, u32[]{:S(2)}, u32[]{:S(2)}) collective-permute-start(f32[24,128]{1,0:T(8,128)} %refs_2_.1), channel_id=1, source_target_pairs={{0,4},{1,5},{2,6},{3,7},{4,0},{5,1},{6,2},{7,3},{8,12},{9,13},{10,... | collective-permute-start | bytes 36872 | tf_op jit(solution)/shard_map/ppermute | solution.py:304
  9.6 24.4 %all-to-all-start = ((f32[16,128,128]{2,1,0:T(8,128)}), f32[16,128,128]{2,1,0:T(8,128)S(1)}, u32[]{:S(2)}, u32[]{:S(2)}) async-start(f32[16,128,128]{2,1,0:T(8,128)} %get-tuple-element.18), calls=%async_computation | async-start | bytes 2097152 | tf_op jit(solution)/shard_map/all_to_all | solution.py:308
  16.7 0.7 copy-start.3
  18.8 7.3 %collective-permute-start.3 = (f32[2,24,128]{2,1,0:T(8,128)S(1)}, f32[2,24,128]{2,1,0:T(8,128)S(1)}, u32[]{:S(2)}, u32[]{:S(2)}) collective-permute-start(f32[2,24,128]{2,1,0:T(8,128)S(1)} %pad_maximum_fusion), channel_id=1, source_target_pairs={{0,3},{1,2},{2,1},{3,0},{4,7},{5,6},{6,5},{7,4},{8,11},{9,10},{10,... | collective-permute-start | bytes 73736 | tf_op jit(solution)/shard_map/ppermute | solution.py:304
  19.9 6.2 %collective-permute-start.2 = (f32[2,24,128]{2,1,0:T(8,128)S(1)}, f32[2,24,128]{2,1,0:T(8,128)S(1)}, u32[]{:S(2)}, u32[]{:S(2)}) collective-permute-start(f32[2,24,128]{2,1,0:T(8,128)S(1)} %pad_maximum_fusion), channel_id=1, source_target_pairs={{0,2},{1,3},{2,0},{3,1},{4,6},{5,7},{6,4},{7,5},{8,10},{9,11},{10,... | collective-permute-start | bytes 73736 | tf_op jit(solution)/shard_map/ppermute | solution.py:304
  22.2 3.8 %collective-permute-start.1 = (f32[2,24,128]{2,1,0:T(8,128)S(1)}, f32[2,24,128]{2,1,0:T(8,128)S(1)}, u32[]{:S(2)}, u32[]{:S(2)}) collective-permute-start(f32[2,24,128]{2,1,0:T(8,128)S(1)} %pad_maximum_fusion), channel_id=1, source_target_pairs={{0,1},{1,0},{2,3},{3,2},{4,5},{5,4},{6,7},{7,6},{8,9},{9,8},{10,11... | collective-permute-start | bytes 73736 | tf_op jit(solution)/shard_map/ppermute | solution.py:304
  26.1 2.2 %copy-start = (f32[24,128]{1,0:T(8,128)S(1)}, f32[24,128]{1,0:T(8,128)}, u32[]{:S(2)}) copy-start(f32[24,128]{1,0:T(8,128)} %get-tuple-element.19.scale_low.scale) | copy-start | bytes 36868
  26.1 2.1 %copy-start.1 = (f32[24,128]{1,0:T(8,128)S(1)}, f32[24,128]{1,0:T(8,128)}, u32[]{:S(2)}) copy-start(f32[24,128]{1,0:T(8,128)} %get-tuple-element.20.scale_high) | copy-start | bytes 36868
  28.2 0.7 copy-start.2

commit v9 on v8

--- a/solution.py
+++ b/solution.py
@@ -332,7 +332,8 @@
         compiler_params=params(60),
         name="pack",
     )(runs, weights.reshape(1, RUN_BLOCKS * LANES), points, len_low, len_high)
-    far = exchange_z(points, 4, size)
+    to_col, later_points = lax.optimization_barrier((to_col, points))
+    far = exchange_z(later_points, 4, size)
     by_col = exchange(to_col, COLS)
     near = jnp.stack([points, far])
     by_row = jnp.concatenate([near] + [exchange_z(near, step, size) for step in (1, 2, 3)], 0)

time: 97.9 us -> 101 us (1.032)
  blocking collectives: 47.4 us -> 55.4 us
  waiting for transfers between devices: 7.69 us -> 3.13 us
    all_to_all x4, blocking collectives: 45.3 us -> 53.3 us  [exchange(): return lax.all_to_all(blocks, axes, 0, 0, tiled=True)]
    all_to_all x1, waiting for transfers between devices: 3.98 us -> 0.01 us  [exchange(): return lax.all_to_all(blocks, axes, 0, 0, tiled=True)]
  transfers between devices with their start and end apart: 5 -> 5, of which waited for: 2 -> 2; matrix products, arithmetic and copies ran while one was open for 0% -> 0% of each run, Pallas kernels for 4% -> 1%
where the time goes in v9:
time: 101 us
  blocking collectives  55.4 us (55%)
  Pallas kernels  21.8 us (22%)
  starting transfers between devices  17.8 us (18%)
  waiting for transfers between devices  3.13 us (3%)
  between operations  2.03 us (2%)
    all_to_all x4, blocking collectives, exchange(): return lax.all_to_all(blocks, axes, 0, 0, tiled=True)  53.3 us
    ppermute x4, starting transfers between devices, exchange_z(): return lax.ppermute(blocks, 'z', [(i, i ^ step) for i in range(size)])  10.7 us
    pallas_call x1, Pallas kernels, local(): pl.pallas_call(mu_kernel, out_shape=(shape((n_row, n_row, LANES)), shape(...  9.8 us
    all_to_all x1, starting transfers between devices, exchange(): return lax.all_to_all(blocks, axes, 0, 0, tiled=True)  7.05 us
    pallas_call x1, Pallas kernels, local(): pl.pallas_call(first_kernel, out_shape=(shape((n_col, n_col, LANES)), sha...  3.49 us
    ppermute x4, waiting for transfers between devices, exchange_z(): return lax.ppermute(blocks, 'z', [(i, i ^ step) for i in range(size)])  3.13 us
    pallas_call x1, Pallas kernels, local(): pl.pallas_call(second_kernel, out_shape=shape((n_row, n_row + 1, 1, LANES...  2.98 us
    pallas_call x1, Pallas kernels, local(): pl.pallas_call(pack_kernel, out_shape=(shape((n_col, PACKED, LANES)), sha...  2.59 us
  transfers between devices with their start and end apart: 5, of which 2 were waited for; matrix products, arithmetic and copies ran while one was open for 0% of the time, Pallas kernels for 1%

profile of v9, /device:TPU:32, one launch (start us, length us, event | category | flops | bytes accessed | tf_op | source)
XLA Modules:
  0.0 100.9 jit_solution(6308394324616564349)
XLA Ops:
  0.6 2.6 %pack.1 = (f32[16,128,128]{2,1,0:T(8,128)}, f32[24,128]{1,0:T(8,128)}, f32[24,128]{1,0:T(8,128)}) custom-call(f32[24,512]{1,0:T(8,128)} %refs_0_.1, f32[1,512]{1,0:T(1,128)} %bitcast.14, f32[24,128]{1,0:T(8,128)} %refs_2_.1, f32[24]{0:T(128)} %refs_3_.1, f32[24]{0:T(128)} %refs_4_.1), custom_call_target="tpu_custom_call" | custom-call | tf_op jit(solution)/shard_map/pack/pallas_call | solution.py:317
  3.2 0.0 copy-start.3
  3.2 7.0 %all-to-all-start = ((f32[16,128,128]{2,1,0:T(8,128)}), f32[16,128,128]{2,1,0:T(8,128)S(1)}, u32[]{:S(2)}, u32[]{:S(2)}) async-start(f32[16,128,128]{2,1,0:T(8,128)} %get-tuple-element.21), calls=%async_computation | async-start | bytes 2097152 | tf_op jit(solution)/shard_map/all_to_all | solution.py:308
  10.3 6.4 %collective-permute-start = (f32[24,128]{1,0:T(8,128)S(1)}, f32[24,128]{1,0:T(8,128)S(1)}, u32[]{:S(2)}, u32[]{:S(2)}) collective-permute-start(f32[24,128]{1,0:T(8,128)S(1)} %copy-done.3), channel_id=1, source_target_pairs={{0,4},{1,5},{2,6},{3,7},{4,0},{5,1},{6,2},{7,3},{8,12},{9,13},{10,... | collective-permute-start | bytes 36872 | tf_op jit(solution)/shard_map/ppermute | solution.py:304
  16.7 0.1 pad_add_fusion.at
  18.1 0.3 collective-permute-done
  18.4 1.5 %collective-permute-start.3 = (f32[2,24,128]{2,1,0:T(8,128)S(1)}, f32[2,24,128]{2,1,0:T(8,128)S(1)}, u32[]{:S(2)}, u32[]{:S(2)}) collective-permute-start(f32[2,24,128]{2,1,0:T(8,128)S(1)} %pad_maximum_fusion), channel_id=1, source_target_pairs={{0,3},{1,2},{2,1},{3,0},{4,7},{5,6},{6,5},{7,4},{8,11},{9,10},{10,... | collective-permute-start | bytes 73736 | tf_op jit(solution)/shard_map/ppermute | solution.py:304
  19.9 1.8 %collective-permute-start.2 = (f32[2,24,128]{2,1,0:T(8,128)S(1)}, f32[2,24,128]{2,1,0:T(8,128)S(1)}, u32[]{:S(2)}, u32[]{:S(2)}) collective-permute-start(f32[2,24,128]{2,1,0:T(8,128)S(1)} %pad_maximum_fusion), channel_id=1, source_target_pairs={{0,2},{1,3},{2,0},{3,1},{4,6},{5,7},{6,4},{7,5},{8,10},{9,11},{10,... | collective-permute-start | bytes 73736 | tf_op jit(solution)/shard_map/ppermute | solution.py:304
  21.7 1.0 collective-permute-start.1
  22.7 2.8 %collective-permute-done.1 = f32[2,24,128]{2,1,0:T(8,128)S(1)} collective-permute-done((f32[2,24,128]{2,1,0:T(8,128)S(1)}, f32[2,24,128]{2,1,0:T(8,128)S(1)}, u32[]{:S(2)}, u32[]{:S(2)}) %collective-permute-start.1) | collective-permute-done | bytes 24608 | tf_op jit(solution)/shard_map/ppermute | solution.py:304
  25.6 0.0 collective-permute-done.2
  25.6 0.0 collective-permute-done.3
  25.6 2.1 %all_gather.3.points = f32[16,24,128]{2,1,0:T(8,128)S(1)} all-gather(f32[8,24,128]{2,1,0:T(8,128)S(1)} %constant_dynamic-update-slice_fusion), channel_id=1, replica_groups=mesh['y'=4,'core'=2,'x'=4,'z'=8] {'core'}, dimensions={0}, use_global_device_ids=true | all-gather | bytes 294912 | tf_op jit(solution)/shard_map/all_gather | solution.py:340
  27.8 0.6 copy-done.2
  28.4 1.1 %prep.1 = (bf16[2048,160]{1,0:T(8,128)(2,1)S(1)}, bf16[160,2048]{1,0:T(8,128)(2,1)S(1)}, f32[1,128]{1,0:T(1,128)S(1)}) custom-call(f32[16,24,128]{2,1,0:T(8,128)S(1)} %all_gather.3.points, f32[24,128]{1,0:T(8,128)S(1)} %copy-done, f32[24,128]{1,0:T(8,128)S(1)} %copy-done.1, f32[1,128]{1,0:T(1,128)S(1)} %bitcast.11, s32[2]{0:T(128)S(1)} %pad_add_fusion.at), custom_call_target="tpu_custom_call" | custom-call | tf_op jit(solution)/shard_map/prep/pallas_call | solution.py:341
  29.5 9.8 %mu.1 = (f32[16,16,128]{2,1,0:T(8,128)S(1)}, bf16[2048,160]{1,0:T(8,128)(2,1)S(1)}) custom-call(f32[16,128,128]{2,1,0:T(8,128)S(1)} %all-to-all-done.held, bf16[2048,160]{1,0:T(8,128)(2,1)S(1)} %get-tuple-element.25.rows_in, f32[24,128]{1,0:T(8,128)S(1)} %copy-done, f32[24,128]{1,0:T(8,128)S(1)} %copy-done.1, f32[1,128]{1,0:T(1,128)S(1)} %get-tuple-element.26.high, ...), custom_call_target="tpu_custom_call" | custom-call | tf_op jit(solution)/shard_map/mu/pallas_call | solution.py:349
  39.3 15.8 %all_to_all.25.held = f32[16,16,128]{2,1,0:T(8,128)S(1)} all-to-all(f32[16,16,128]{2,1,0:T(8,128)S(1)} %get-tuple-element.27), channel_id=1, replica_groups=mesh['y'=4,'core'=2,'x'=4,'z'=8] {'core','z'}, dimensions={0} | all-to-all | bytes 262144 | tf_op jit(solution)/shard_map/all_to_all | solution.py:308
  55.1 3.5 %first.1 = (f32[16,16,128]{2,1,0:T(8,128)S(1)}, f32[16,128]{1,0:T(8,128)S(1)}, f32[1,128]{1,0:T(1,128)}) custom-call(f32[16,16,128]{2,1,0:T(8,128)S(1)} %all_to_all.25.held, bf16[160,2048]{1,0:T(8,128)(2,1)S(1)} %get-tuple-element.28.rows_in, bf16[2048,160]{1,0:T(8,128)(2,1)S(1)} %get-tuple-element.29.cols_in, f32[1,128]{1,0:T(1,128)S(1)} %get-tuple-element.26.high, ...), custom_call_target="tpu_custom_call" | custom-call | tf_op jit(solution)/shard_map/first/pallas_call | solution.py:364
  58.6 15.0 %all_to_all.26.held = f32[16,16,128]{2,1,0:T(8,128)S(1)} all-to-all(f32[16,16,128]{2,1,0:T(8,128)S(1)} %get-tuple-element.31), channel_id=1, replica_groups=mesh['y'=4,'core'=2,'x'=4,'z'=8] {'y','x'}, dimensions={0} | all-to-all | bytes 262144 | tf_op jit(solution)/shard_map/all_to_all | solution.py:308
  73.6 3.0 %second.1 = f32[16,17,1,128]{3,2,1,0:T(1,128)S(1)} custom-call(f32[16,16,128]{2,1,0:T(8,128)S(1)} %all_to_all.26.held, bf16[160,2048]{1,0:T(8,128)(2,1)S(1)} %get-tuple-element.28.rows_in, bf16[2048,160]{1,0:T(8,128)(2,1)S(1)} %get-tuple-element.29.cols_in, f32[1]{0:T(128)S(6)} %copy.16.noise, s32[2]{0:T(128)S(1)} %pad_add_fusion.at), custom_call_target="tpu_custom_call" | custom-call | tf_op jit(solution)/shard_map/second/pallas_call | solution.py:374
  76.6 11.7 %all_to_all.27.held = f32[16,17,1,128]{3,2,1,0:T(1,128)S(1)} all-to-all(f32[16,17,1,128]{3,2,1,0:T(1,128)S(1)} %second.1), channel_id=1, replica_groups=mesh['y'=4,'core'=2,'x'=4,'z'=8] {'core','z'}, dimensions={0} | all-to-all | bytes 278528 | tf_op jit(solution)/shard_map/all_to_all | solution.py:308
  88.3 0.7 moments.1
  89.0 10.7 %all_to_all.28.held = f32[16,8,128]{2,1,0:T(8,128)S(1)} all-to-all(f32[16,8,128]{2,1,0:T(8,128)S(1)} %get-tuple-element.33), channel_id=1, replica_groups=mesh['y'=4,'core'=2,'x'=4,'z'=8] {'y','x'}, dimensions={0} | all-to-all | bytes 131072 | tf_op jit(solution)/shard_map/all_to_all | solution.py:308
  99.8 1.2 %final.1 = (f32[1,128]{1,0:T(1,128)}, f32[1,128]{1,0:T(1,128)}) custom-call(f32[16,8,128]{2,1,0:T(8,128)S(1)} %all_to_all.28.held, f32[8,128]{1,0:T(8,128)S(1)} %get-tuple-element.34.own), custom_call_target="tpu_custom_call" | custom-call | tf_op jit(solution)/shard_map/final/pallas_call | solution.py:393
  (13 shorter events, 0.0 us)
Async XLA Ops:
  3.2 7.1 %copy-start.3 = (f32[24,128]{1,0:T(8,128)S(1)}, f32[24,128]{1,0:T(8,128)}, u32[]{:S(2)}) copy-start(f32[24,128]{1,0:T(8,128)} %refs_2_.1) | copy-start | bytes 36868
  3.2 26.3 %all-to-all-start = ((f32[16,128,128]{2,1,0:T(8,128)}), f32[16,128,128]{2,1,0:T(8,128)S(1)}, u32[]{:S(2)}, u32[]{:S(2)}) async-start(f32[16,128,128]{2,1,0:T(8,128)} %get-tuple-element.21), calls=%async_computation | async-start | bytes 2097152 | tf_op jit(solution)/shard_map/all_to_all | solution.py:308
  10.3 8.1 %collective-permute-start = (f32[24,128]{1,0:T(8,128)S(1)}, f32[24,128]{1,0:T(8,128)S(1)}, u32[]{:S(2)}, u32[]{:S(2)}) collective-permute-start(f32[24,128]{1,0:T(8,128)S(1)} %copy-done.3), channel_id=1, source_target_pairs={{0,4},{1,5},{2,6},{3,7},{4,0},{5,1},{6,2},{7,3},{8,12},{9,13},{10,... | collective-permute-start | bytes 36872 | tf_op jit(solution)/shard_map/ppermute | solution.py:304
  18.4 7.2 %collective-permute-start.3 = (f32[2,24,128]{2,1,0:T(8,128)S(1)}, f32[2,24,128]{2,1,0:T(8,128)S(1)}, u32[]{:S(2)}, u32[]{:S(2)}) collective-permute-start(f32[2,24,128]{2,1,0:T(8,128)S(1)} %pad_maximum_fusion), channel_id=1, source_target_pairs={{0,3},{1,2},{2,1},{3,0},{4,7},{5,6},{6,5},{7,4},{8,11},{9,10},{10,... | collective-permute-start | bytes 73736 | tf_op jit(solution)/shard_map/ppermute | solution.py:304
  19.9 5.6 %collective-permute-start.2 = (f32[2,24,128]{2,1,0:T(8,128)S(1)}, f32[2,24,128]{2,1,0:T(8,128)S(1)}, u32[]{:S(2)}, u32[]{:S(2)}) collective-permute-start(f32[2,24,128]{2,1,0:T(8,128)S(1)} %pad_maximum_fusion), channel_id=1, source_target_pairs={{0,2},{1,3},{2,0},{3,1},{4,6},{5,7},{6,4},{7,5},{8,10},{9,11},{10,... | collective-permute-start | bytes 73736 | tf_op jit(solution)/shard_map/ppermute | solution.py:304
  21.7 3.8 %collective-permute-start.1 = (f32[2,24,128]{2,1,0:T(8,128)S(1)}, f32[2,24,128]{2,1,0:T(8,128)S(1)}, u32[]{:S(2)}, u32[]{:S(2)}) collective-permute-start(f32[2,24,128]{2,1,0:T(8,128)S(1)} %pad_maximum_fusion), channel_id=1, source_target_pairs={{0,1},{1,0},{2,3},{3,2},{4,5},{5,4},{6,7},{7,6},{8,9},{9,8},{10,11... | collective-permute-start | bytes 73736 | tf_op jit(solution)/shard_map/ppermute | solution.py:304
  25.6 2.2 %copy-start = (f32[24,128]{1,0:T(8,128)S(1)}, f32[24,128]{1,0:T(8,128)}, u32[]{:S(2)}) copy-start(f32[24,128]{1,0:T(8,128)} %get-tuple-element.23.scale_low.scale) | copy-start | bytes 36868
  25.6 2.1 %copy-start.1 = (f32[24,128]{1,0:T(8,128)S(1)}, f32[24,128]{1,0:T(8,128)}, u32[]{:S(2)}) copy-start(f32[24,128]{1,0:T(8,128)} %get-tuple-element.24.scale_high) | copy-start | bytes 36868
  27.7 0.7 copy-start.2

commit v10 on v8

--- a/solution.py
+++ b/solution.py
@@ -106,12 +106,11 @@
 
 
 def place_of(m, at):
-    block = (m >> 3) * 8 + ((at[0] & 7) ^ (m >> 1 & 3) ^ 4 * (m & 1))
+    block = (m >> 3) * 8 + ((at[0] & 7) ^ (m & 7))
     return pl.ds(pl.multiple_of(block * LANES, LANES), LANES)
 
 
-def prep_kernel(points, scale_low, scale_high, high, at, out, rows_out, high_out):
-    high_out[...] = high[...]
+def prep_kernel(points, scale_low, scale_high, at, out, rows_out):
     for m in range(points.shape[0]):
         place = place_of(m, at)
         out[place, :] = left(points[m], scale_low[...]).T.astype(BF16)
@@ -311,7 +310,7 @@
 def local(runs, weights, points, high, len_low, len_high, rho, noise):
     n_row, n_col = lax.axis_size(ROWS), lax.axis_size(COLS)
     at = jnp.stack([lax.axis_index(ROWS), lax.axis_index(COLS)]).astype(jnp.int32)
-    high = high.reshape(1, LANES)
+    high = jnp.where(at[1] >= 0, high, 0.0).reshape(1, LANES)
     cols_len, rows_len = n_col * LANES, n_row * LANES
     size = lax.axis_size("z")
     to_col, scale_low, scale_high = pl.pallas_call(
@@ -332,19 +331,19 @@
         compiler_params=params(60),
         name="pack",
     )(runs, weights.reshape(1, RUN_BLOCKS * LANES), points, len_low, len_high)
-    far = exchange_z(points, 4, size)
+    far = exchange_z(points, 1, size)
     by_col = exchange(to_col, COLS)
     near = jnp.stack([points, far])
-    by_row = jnp.concatenate([near] + [exchange_z(near, step, size) for step in (1, 2, 3)], 0)
+    by_row = jnp.concatenate([near] + [exchange_z(near, step, size) for step in (2, 4, 6)], 0)
     by_row = lax.all_gather(by_row, "core", axis=0, tiled=True)
-    row_low, row_parts, high = pl.pallas_call(
+    row_low, row_parts = pl.pallas_call(
         prep_kernel,
-        out_shape=(shape((rows_len, DEPTH), BF16), shape((DEPTH, rows_len), BF16), shape((1, LANES))),
-        in_specs=[VMEM] * 4 + [SMEM],
-        out_specs=(VMEM,) * 3,
+        out_shape=(shape((rows_len, DEPTH), BF16), shape((DEPTH, rows_len), BF16)),
+        in_specs=[VMEM] * 3 + [SMEM],
+        out_specs=(VMEM,) * 2,
         compiler_params=params(4),
         name="prep",
-    )(by_row, scale_low, scale_high, high, at)
+    )(by_row, scale_low, scale_high, at)
     mu_terms, col_parts = pl.pallas_call(
         mu_kernel,
         out_shape=(shape((n_row, n_row, LANES)), shape((cols_len, DEPTH), BF16)),

time: 97.9 us -> 99.4 us (1.015)
  blocking collectives: 47.4 us -> 52.9 us
  waiting for transfers between devices: 7.69 us -> 5.27 us
    all_to_all x4, blocking collectives: 45.3 us -> 50.7 us  [exchange(): return lax.all_to_all(blocks, axes, 0, 0, tiled=True)]
    all_to_all x1, waiting for transfers between devices: 3.98 us -> 0.01 us  [exchange(): return lax.all_to_all(blocks, axes, 0, 0, tiled=True)]
    all_to_all x1, starting transfers between devices: 7.05 us -> 5.31 us  [exchange(): return lax.all_to_all(blocks, axes, 0, 0, tiled=True)]
    ppermute x4, waiting for transfers between devices: 3.71 us -> 5.27 us  [exchange_z(): return lax.ppermute(blocks, 'z', [(i, i ^ step) for i in range(size)])]
where the time goes in v10:
time: 99.4 us; the launch traced here: 98.9 us
  blocking collectives  52.9 us (53%)
  Pallas kernels  21.9 us (22%)
  starting transfers between devices  16.1 us (16%)
  waiting for transfers between devices  5.27 us (5%)
  between operations  2.06 us (2%)
    all_to_all x4, blocking collectives, exchange(): return lax.all_to_all(blocks, axes, 0, 0, tiled=True)  50.7 us
    ppermute x4, starting transfers between devices, exchange_z(): return lax.ppermute(blocks, 'z', [(i, i ^ step) for i in range(size)])  10.8 us
    pallas_call x1, Pallas kernels, local(): pl.pallas_call(mu_kernel, out_shape=(shape((n_row, n_row, LANES)), shape(...  9.8 us
    all_to_all x1, starting transfers between devices, exchange(): return lax.all_to_all(blocks, axes, 0, 0, tiled=True)  5.31 us
    ppermute x4, waiting for transfers between devices, exchange_z(): return lax.ppermute(blocks, 'z', [(i, i ^ step) for i in range(size)])  5.27 us
    pallas_call x1, Pallas kernels, local(): pl.pallas_call(first_kernel, out_shape=(shape((n_col, n_col, LANES)), sha...  3.52 us
    pallas_call x1, Pallas kernels, local(): pl.pallas_call(second_kernel, out_shape=shape((n_row, n_row + 1, 1, LANES...  2.98 us
    pallas_call x1, Pallas kernels, local(): pl.pallas_call(pack_kernel, out_shape=(shape((n_col, PACKED, LANES)), sha...  2.59 us
  transfers between devices with their start and end apart: 5, of which 2 were waited for; matrix products, arithmetic and copies ran while one was open for 0% of the time, Pallas kernels for 4%

profile of v10, /device:TPU:32, one launch (start us, length us, event | category | flops | bytes accessed | tf_op | source)
XLA Modules:
  0.0 98.9 jit_solution(1605478402542793742)
XLA Ops:
  0.6 1.9 %collective-permute-start = (f32[24,128]{1,0:T(8,128)}, f32[24,128]{1,0:T(8,128)S(1)}, u32[]{:S(2)}, u32[]{:S(2)}) collective-permute-start(f32[24,128]{1,0:T(8,128)} %refs_2_.1), channel_id=1, source_target_pairs={{0,1},{1,0},{2,3},{3,2},{4,5},{5,4},{6,7},{7,6},{8,9},{9,8},{10,11... | collective-permute-start | bytes 36872 | tf_op jit(solution)/shard_map/ppermute | solution.py:303
  2.6 2.6 %pack.1 = (f32[16,128,128]{2,1,0:T(8,128)}, f32[24,128]{1,0:T(8,128)}, f32[24,128]{1,0:T(8,128)}) custom-call(f32[24,512]{1,0:T(8,128)} %refs_0_.1, f32[1,512]{1,0:T(1,128)} %bitcast.14, f32[24,128]{1,0:T(8,128)} %refs_2_.1, f32[24]{0:T(128)} %refs_3_.1, f32[24]{0:T(128)} %refs_4_.1), custom_call_target="tpu_custom_call" | custom-call | tf_op jit(solution)/shard_map/pack/pallas_call | solution.py:316
  5.2 0.0 copy-start.2
  5.2 5.3 %all-to-all-start = ((f32[16,128,128]{2,1,0:T(8,128)}), f32[16,128,128]{2,1,0:T(8,128)S(1)}, u32[]{:S(2)}, u32[]{:S(2)}) async-start(f32[16,128,128]{2,1,0:T(8,128)} %get-tuple-element.17), calls=%async_computation | async-start | bytes 2097152 | tf_op jit(solution)/shard_map/all_to_all | solution.py:307
  10.5 0.0 copy-start.3
  10.5 0.6 copy-done.3
  11.2 0.1 pad_add_fusion.at
  12.6 6.4 %collective-permute-start.3 = (f32[2,24,128]{2,1,0:T(8,128)S(1)}, f32[2,24,128]{2,1,0:T(8,128)S(1)}, u32[]{:S(2)}, u32[]{:S(2)}) collective-permute-start(f32[2,24,128]{2,1,0:T(8,128)S(1)} %pad_maximum_fusion), channel_id=1, source_target_pairs={{0,6},{1,7},{2,4},{3,5},{4,2},{5,3},{6,0},{7,1},{8,14},{9,15},{10,... | collective-permute-start | bytes 73736 | tf_op jit(solution)/shard_map/ppermute | solution.py:303
  19.0 1.0 %collective-permute-start.2 = (f32[2,24,128]{2,1,0:T(8,128)S(1)}, f32[2,24,128]{2,1,0:T(8,128)S(1)}, u32[]{:S(2)}, u32[]{:S(2)}) collective-permute-start(f32[2,24,128]{2,1,0:T(8,128)S(1)} %pad_maximum_fusion), channel_id=1, source_target_pairs={{0,4},{1,5},{2,6},{3,7},{4,0},{5,1},{6,2},{7,3},{8,12},{9,13},{10,... | collective-permute-start | bytes 73736 | tf_op jit(solution)/shard_map/ppermute | solution.py:303
  20.0 1.5 %collective-permute-start.1 = (f32[2,24,128]{2,1,0:T(8,128)S(1)}, f32[2,24,128]{2,1,0:T(8,128)S(1)}, u32[]{:S(2)}, u32[]{:S(2)}) collective-permute-start(f32[2,24,128]{2,1,0:T(8,128)S(1)} %pad_maximum_fusion), channel_id=1, source_target_pairs={{0,2},{1,3},{2,0},{3,1},{4,6},{5,7},{6,4},{7,5},{8,10},{9,11},{10,... | collective-permute-start | bytes 73736 | tf_op jit(solution)/shard_map/ppermute | solution.py:303
  21.4 3.6 %collective-permute-done.1 = f32[2,24,128]{2,1,0:T(8,128)S(1)} collective-permute-done((f32[2,24,128]{2,1,0:T(8,128)S(1)}, f32[2,24,128]{2,1,0:T(8,128)S(1)}, u32[]{:S(2)}, u32[]{:S(2)}) %collective-permute-start.1) | collective-permute-done | bytes 24608 | tf_op jit(solution)/shard_map/ppermute | solution.py:303
  25.0 1.7 %collective-permute-done.2 = f32[2,24,128]{2,1,0:T(8,128)S(1)} collective-permute-done((f32[2,24,128]{2,1,0:T(8,128)S(1)}, f32[2,24,128]{2,1,0:T(8,128)S(1)}, u32[]{:S(2)}, u32[]{:S(2)}) %collective-permute-start.2) | collective-permute-done | bytes 24608 | tf_op jit(solution)/shard_map/ppermute | solution.py:303
  26.7 0.0 collective-permute-done.3
  26.7 2.1 %all_gather.3.points = f32[16,24,128]{2,1,0:T(8,128)S(1)} all-gather(f32[8,24,128]{2,1,0:T(8,128)S(1)} %constant_dynamic-update-slice_fusion), channel_id=1, replica_groups=mesh['y'=4,'core'=2,'x'=4,'z'=8] {'core'}, dimensions={0}, use_global_device_ids=true | all-gather | bytes 294912 | tf_op jit(solution)/shard_map/all_gather | solution.py:338
  28.9 1.1 %prep.1 = (bf16[2048,160]{1,0:T(8,128)(2,1)S(1)}, bf16[160,2048]{1,0:T(8,128)(2,1)S(1)}) custom-call(f32[16,24,128]{2,1,0:T(8,128)S(1)} %all_gather.3.points, f32[24,128]{1,0:T(8,128)S(1)} %copy-done, f32[24,128]{1,0:T(8,128)S(1)} %copy-done.1, s32[2]{0:T(128)S(1)} %pad_add_fusion.at), custom_call_target="tpu_custom_call" | custom-call | tf_op jit(solution)/shard_map/prep/pallas_call | solution.py:339
  30.0 9.8 %mu.1 = (f32[16,16,128]{2,1,0:T(8,128)S(1)}, bf16[2048,160]{1,0:T(8,128)(2,1)S(1)}) custom-call(f32[16,128,128]{2,1,0:T(8,128)S(1)} %all-to-all-done.held, bf16[2048,160]{1,0:T(8,128)(2,1)S(1)} %get-tuple-element.20.rows_in, f32[24,128]{1,0:T(8,128)S(1)} %copy-done, f32[24,128]{1,0:T(8,128)S(1)} %copy-done.1, f32[1,128]{1,0:T(1,128)S(1)} %fusion.high, ...), custom_call_target="tpu_custom_call" | custom-call | tf_op jit(solution)/shard_map/mu/pallas_call | solution.py:347
  39.8 15.3 %all_to_all.25.held = f32[16,16,128]{2,1,0:T(8,128)S(1)} all-to-all(f32[16,16,128]{2,1,0:T(8,128)S(1)} %get-tuple-element.21), channel_id=1, replica_groups=mesh['y'=4,'core'=2,'x'=4,'z'=8] {'core','z'}, dimensions={0} | all-to-all | bytes 262144 | tf_op jit(solution)/shard_map/all_to_all | solution.py:307
  55.1 3.5 %first.1 = (f32[16,16,128]{2,1,0:T(8,128)S(1)}, f32[16,128]{1,0:T(8,128)S(1)}, f32[1,128]{1,0:T(1,128)}) custom-call(f32[16,16,128]{2,1,0:T(8,128)S(1)} %all_to_all.25.held, bf16[160,2048]{1,0:T(8,128)(2,1)S(1)} %get-tuple-element.22.rows_in, bf16[2048,160]{1,0:T(8,128)(2,1)S(1)} %get-tuple-element.23.cols_in, f32[1,128]{1,0:T(1,128)S(1)} %fusion.high, ...), custom_call_target="tpu_custom_call" | custom-call | tf_op jit(solution)/shard_map/first/pallas_call | solution.py:362
  58.6 12.9 %all_to_all.26.held = f32[16,16,128]{2,1,0:T(8,128)S(1)} all-to-all(f32[16,16,128]{2,1,0:T(8,128)S(1)} %get-tuple-element.25), channel_id=1, replica_groups=mesh['y'=4,'core'=2,'x'=4,'z'=8] {'y','x'}, dimensions={0} | all-to-all | bytes 262144 | tf_op jit(solution)/shard_map/all_to_all | solution.py:307
  71.6 3.0 %second.1 = f32[16,17,1,128]{3,2,1,0:T(1,128)S(1)} custom-call(f32[16,16,128]{2,1,0:T(8,128)S(1)} %all_to_all.26.held, bf16[160,2048]{1,0:T(8,128)(2,1)S(1)} %get-tuple-element.22.rows_in, bf16[2048,160]{1,0:T(8,128)(2,1)S(1)} %get-tuple-element.23.cols_in, f32[1]{0:T(128)S(6)} %copy.16.noise, s32[2]{0:T(128)S(1)} %pad_add_fusion.at), custom_call_target="tpu_custom_call" | custom-call | tf_op jit(solution)/shard_map/second/pallas_call | solution.py:372
  74.5 11.7 %all_to_all.27.held = f32[16,17,1,128]{3,2,1,0:T(1,128)S(1)} all-to-all(f32[16,17,1,128]{3,2,1,0:T(1,128)S(1)} %second.1), channel_id=1, replica_groups=mesh['y'=4,'core'=2,'x'=4,'z'=8] {'core','z'}, dimensions={0} | all-to-all | bytes 278528 | tf_op jit(solution)/shard_map/all_to_all | solution.py:307
  86.3 0.7 moments.1
  87.0 10.7 %all_to_all.28.held = f32[16,8,128]{2,1,0:T(8,128)S(1)} all-to-all(f32[16,8,128]{2,1,0:T(8,128)S(1)} %get-tuple-element.27), channel_id=1, replica_groups=mesh['y'=4,'core'=2,'x'=4,'z'=8] {'y','x'}, dimensions={0} | all-to-all | bytes 131072 | tf_op jit(solution)/shard_map/all_to_all | solution.py:307
  97.7 1.2 %final.1 = (f32[1,128]{1,0:T(1,128)}, f32[1,128]{1,0:T(1,128)}) custom-call(f32[16,8,128]{2,1,0:T(8,128)S(1)} %all_to_all.28.held, f32[8,128]{1,0:T(8,128)S(1)} %get-tuple-element.28.own), custom_call_target="tpu_custom_call" | custom-call | tf_op jit(solution)/shard_map/final/pallas_call | solution.py:391
  (14 shorter events, 0.0 us)
Async XLA Ops:
  0.6 11.9 %collective-permute-start = (f32[24,128]{1,0:T(8,128)}, f32[24,128]{1,0:T(8,128)S(1)}, u32[]{:S(2)}, u32[]{:S(2)}) collective-permute-start(f32[24,128]{1,0:T(8,128)} %refs_2_.1), channel_id=1, source_target_pairs={{0,1},{1,0},{2,3},{3,2},{4,5},{5,4},{6,7},{7,6},{8,9},{9,8},{10,11... | collective-permute-start | bytes 36872 | tf_op jit(solution)/shard_map/ppermute | solution.py:303
  5.2 5.3 %copy-start.2 = (f32[24,128]{1,0:T(8,128)S(1)}, f32[24,128]{1,0:T(8,128)}, u32[]{:S(2)}) copy-start(f32[24,128]{1,0:T(8,128)} %refs_2_.1) | copy-start | bytes 36868
  5.2 24.8 %all-to-all-start = ((f32[16,128,128]{2,1,0:T(8,128)}), f32[16,128,128]{2,1,0:T(8,128)S(1)}, u32[]{:S(2)}, u32[]{:S(2)}) async-start(f32[16,128,128]{2,1,0:T(8,128)} %get-tuple-element.17), calls=%async_computation | async-start | bytes 2097152 | tf_op jit(solution)/shard_map/all_to_all | solution.py:307
  10.5 0.7 copy-start.3
  12.6 14.1 %collective-permute-start.3 = (f32[2,24,128]{2,1,0:T(8,128)S(1)}, f32[2,24,128]{2,1,0:T(8,128)S(1)}, u32[]{:S(2)}, u32[]{:S(2)}) collective-permute-start(f32[2,24,128]{2,1,0:T(8,128)S(1)} %pad_maximum_fusion), channel_id=1, source_target_pairs={{0,6},{1,7},{2,4},{3,5},{4,2},{5,3},{6,0},{7,1},{8,14},{9,15},{10,... | collective-permute-start | bytes 73736 | tf_op jit(solution)/shard_map/ppermute | solution.py:303
  19.0 7.7 %collective-permute-start.2 = (f32[2,24,128]{2,1,0:T(8,128)S(1)}, f32[2,24,128]{2,1,0:T(8,128)S(1)}, u32[]{:S(2)}, u32[]{:S(2)}) collective-permute-start(f32[2,24,128]{2,1,0:T(8,128)S(1)} %pad_maximum_fusion), channel_id=1, source_target_pairs={{0,4},{1,5},{2,6},{3,7},{4,0},{5,1},{6,2},{7,3},{8,12},{9,13},{10,... | collective-permute-start | bytes 73736 | tf_op jit(solution)/shard_map/ppermute | solution.py:303
  20.0 5.0 %collective-permute-start.1 = (f32[2,24,128]{2,1,0:T(8,128)S(1)}, f32[2,24,128]{2,1,0:T(8,128)S(1)}, u32[]{:S(2)}, u32[]{:S(2)}) collective-permute-start(f32[2,24,128]{2,1,0:T(8,128)S(1)} %pad_maximum_fusion), channel_id=1, source_target_pairs={{0,2},{1,3},{2,0},{3,1},{4,6},{5,7},{6,4},{7,5},{8,10},{9,11},{10,... | collective-permute-start | bytes 73736 | tf_op jit(solution)/shard_map/ppermute | solution.py:303
  26.7 2.2 %copy-start = (f32[24,128]{1,0:T(8,128)S(1)}, f32[24,128]{1,0:T(8,128)}, u32[]{:S(2)}) copy-start(f32[24,128]{1,0:T(8,128)} %get-tuple-element.18.scale_low.scale) | copy-start | bytes 36868
  26.7 2.1 %copy-start.1 = (f32[24,128]{1,0:T(8,128)S(1)}, f32[24,128]{1,0:T(8,128)}, u32[]{:S(2)}) copy-start(f32[24,128]{1,0:T(8,128)} %get-tuple-element.19.scale_high) | copy-start | bytes 36868

commit v11 on v10

--- a/solution.py
+++ b/solution.py
@@ -106,7 +106,7 @@
 
 
 def place_of(m, at):
-    block = (m >> 3) * 8 + ((at[0] & 7) ^ (m & 7))
+    block = (m >> 3) * 8 + ((at[0] & 7) ^ (m >> 1 & 3) ^ 4 * (m & 1))
     return pl.ds(pl.multiple_of(block * LANES, LANES), LANES)
 
 
@@ -169,7 +169,7 @@
     return jnp.concatenate([line[:, k : k + LANES] for k in range(0, line.shape[1], LANES)], 0)
 
 
-def first_kernel(held, rows_in, cols_in, high, rho, noise, at, out, target_out, mu_out, sums):
+def first_kernel(held, rows_in, cols_in, high, rho, noise, at, at_col, out, target_out, mu_out, sums):
     total = jnp.sum(held[...], axis=0)
     row = lax.broadcasted_iota(jnp.int32, total.shape, 0)
     own = row == at[0]
@@ -191,14 +191,14 @@
             at_row = (k + q) // LANES
             sums[at_row : at_row + 1, :] = jnp.sum(acc[q : q + LANES, :].T, axis=0, keepdims=True)
     image = sums[...]
-    image = jnp.where(lax.broadcasted_iota(jnp.int32, image.shape, 0) == at[1], image + noise[0] * own_target, image)
+    image = jnp.where(lax.broadcasted_iota(jnp.int32, image.shape, 0) == at_col[0], image + noise[0] * own_target, image)
     for i in range(out.shape[0]):
         out[i] = image
 
 
-def second_kernel(held, rows_in, cols_in, noise, at, out, column, total):
+def second_kernel(held, rows_in, cols_in, noise, at, at_col, out, column, total):
     image = jnp.sum(held[...], axis=0)
-    mine = lax.broadcasted_iota(jnp.int32, image.shape, 0) == at[1]
+    mine = lax.broadcasted_iota(jnp.int32, image.shape, 0) == at_col[0]
     own = jnp.sum(jnp.where(mine, image, 0.0), axis=0, keepdims=True)
     for k in range(image.shape[0]):
         column_of(image[k : k + 1, :], column, slice(k * LANES, (k + 1) * LANES))
@@ -309,8 +309,9 @@
 
 def local(runs, weights, points, high, len_low, len_high, rho, noise):
     n_row, n_col = lax.axis_size(ROWS), lax.axis_size(COLS)
-    at = jnp.stack([lax.axis_index(ROWS), lax.axis_index(COLS)]).astype(jnp.int32)
-    high = jnp.where(at[1] >= 0, high, 0.0).reshape(1, LANES)
+    place = lax.axis_index(COLS)
+    at, at_col = lax.axis_index(ROWS).reshape(1), place.reshape(1)
+    high = jnp.where(place >= 0, high, 0.0).reshape(1, LANES)
     cols_len, rows_len = n_col * LANES, n_row * LANES
     size = lax.axis_size("z")
     to_col, scale_low, scale_high = pl.pallas_call(
@@ -331,10 +332,10 @@
         compiler_params=params(60),
         name="pack",
     )(runs, weights.reshape(1, RUN_BLOCKS * LANES), points, len_low, len_high)
-    far = exchange_z(points, 1, size)
+    far = exchange_z(points, 4, size)
     by_col = exchange(to_col, COLS)
     near = jnp.stack([points, far])
-    by_row = jnp.concatenate([near] + [exchange_z(near, step, size) for step in (2, 4, 6)], 0)
+    by_row = jnp.concatenate([near] + [exchange_z(near, step, size) for step in (1, 2, 3)], 0)
     by_row = lax.all_gather(by_row, "core", axis=0, tiled=True)
     row_low, row_parts = pl.pallas_call(
         prep_kernel,
@@ -362,22 +363,22 @@
     image_terms, target, mu = pl.pallas_call(
         first_kernel,
         out_shape=(shape((n_col, n_col, LANES)), shape((n_row, LANES)), shape((1, LANES))),
-        in_specs=[VMEM] * 4 + [SMEM] * 3,
+        in_specs=[VMEM] * 4 + [SMEM] * 4,
         out_specs=(VMEM,) * 3,
         scratch_shapes=[pltpu.VMEM((n_col, LANES), F32)],
         compiler_params=params(4),
         name="first",
-    )(mu_held, row_parts, col_parts, high, rho, noise, at)
+    )(mu_held, row_parts, col_parts, high, rho, noise, at, at_col)
     image_held = exchange(image_terms, COLS)
     last_terms = pl.pallas_call(
         second_kernel,
         out_shape=shape((n_row, n_row + 1, 1, LANES)),
-        in_specs=[VMEM] * 3 + [SMEM] * 2,
+        in_specs=[VMEM] * 3 + [SMEM] * 3,
         out_specs=VMEM,
         scratch_shapes=[pltpu.VMEM((cols_len, LANES), F32), pltpu.VMEM((8, rows_len), F32)],
         compiler_params=params(8),
         name="second",
-    )(image_held, row_parts, col_parts, noise, at)
+    )(image_held, row_parts, col_parts, noise, at, at_col)
     last_held = exchange(last_terms, ROWS)
     moments, own = pl.pallas_call(
         moments_kernel,

time: 99.4 us -> 95.8 us (0.964)
  blocking collectives: 52.9 us -> 47.4 us
  waiting for transfers between devices: 5.27 us -> 8.99 us
  Pallas kernels: 21.9 us -> 19.2 us
    all_to_all x4, blocking collectives: 50.7 us -> 45.3 us  [exchange(): return lax.all_to_all(blocks, axes, 0, 0, tiled=True)]
    all_to_all x1, waiting for transfers between devices: 0.01 us -> 5.27 us  [exchange(): return lax.all_to_all(blocks, axes, 0, 0, tiled=True)]
    all_to_all x1, starting transfers between devices: 5.31 us -> 7.05 us  [exchange(): return lax.all_to_all(blocks, axes, 0, 0, tiled=True)]
    ppermute x4, waiting for transfers between devices: 5.27 us -> 3.71 us  [exchange_z(): return lax.ppermute(blocks, 'z', [(i, i ^ step) for i in range(size)])]
  transfers between devices with their start and end apart: 5 -> 5, of which waited for: 2 -> 2; matrix products, arithmetic and copies ran while one was open for 0% -> 0% of each run, Pallas kernels for 4% -> 3%
where the time goes in v11:
time: 95.8 us; the launch traced here: 95.3 us
  blocking collectives  47.4 us (49%)
  Pallas kernels  19.2 us (20%)
  starting transfers between devices  17 us (18%)
  waiting for transfers between devices  8.99 us (9%)
  between operations  2.07 us (2%)
    all_to_all x4, blocking collectives, exchange(): return lax.all_to_all(blocks, axes, 0, 0, tiled=True)  45.3 us
    ppermute x4, starting transfers between devices, exchange_z(): return lax.ppermute(blocks, 'z', [(i, i ^ step) for i in range(size)])  9.95 us
    pallas_call x1, Pallas kernels, local(): pl.pallas_call(mu_kernel, out_shape=(shape((n_row, n_row, LANES)), shape(...  9.3 us
    all_to_all x1, starting transfers between devices, exchange(): return lax.all_to_all(blocks, axes, 0, 0, tiled=True)  7.05 us
    all_to_all x1, waiting for transfers between devices, exchange(): return lax.all_to_all(blocks, axes, 0, 0, tiled=True)  5.27 us
    ppermute x4, waiting for transfers between devices, exchange_z(): return lax.ppermute(blocks, 'z', [(i, i ^ step) for i in range(size)])  3.71 us
    pallas_call x1, Pallas kernels, local(): pl.pallas_call(first_kernel, out_shape=(shape((n_col, n_col, LANES)), sha...  2.96 us
    pallas_call x1, Pallas kernels, local(): pl.pallas_call(pack_kernel, out_shape=(shape((n_col, PACKED, LANES)), sha...  2.59 us
  transfers between devices with their start and end apart: 5, of which 2 were waited for; matrix products, arithmetic and copies ran while one was open for 0% of the time, Pallas kernels for 3%

profile of v11, /device:TPU:32, one launch (start us, length us, event | category | flops | bytes accessed | tf_op | source)
XLA Modules:
  0.0 95.3 jit_solution(17688337190721722917)
XLA Ops:
  0.6 6.4 %collective-permute-start = (f32[24,128]{1,0:T(8,128)}, f32[24,128]{1,0:T(8,128)S(1)}, u32[]{:S(2)}, u32[]{:S(2)}) collective-permute-start(f32[24,128]{1,0:T(8,128)} %refs_2_.1), channel_id=1, source_target_pairs={{0,4},{1,5},{2,6},{3,7},{4,0},{5,1},{6,2},{7,3},{8,12},{9,13},{10,... | collective-permute-start | bytes 36872 | tf_op jit(solution)/shard_map/ppermute | solution.py:303
  7.0 2.6 %pack.1 = (f32[16,128,128]{2,1,0:T(8,128)}, f32[24,128]{1,0:T(8,128)}, f32[24,128]{1,0:T(8,128)}) custom-call(f32[24,512]{1,0:T(8,128)} %refs_0_.1, f32[1,512]{1,0:T(1,128)} %bitcast.14, f32[24,128]{1,0:T(8,128)} %refs_2_.1, f32[24]{0:T(128)} %refs_3_.1, f32[24]{0:T(128)} %refs_4_.1), custom_call_target="tpu_custom_call" | custom-call | tf_op jit(solution)/shard_map/pack/pallas_call | solution.py:317
  9.6 0.0 copy-start.2
  9.6 7.0 %all-to-all-start = ((f32[16,128,128]{2,1,0:T(8,128)}), f32[16,128,128]{2,1,0:T(8,128)S(1)}, u32[]{:S(2)}, u32[]{:S(2)}) async-start(f32[16,128,128]{2,1,0:T(8,128)} %get-tuple-element.17), calls=%async_computation | async-start | bytes 2097152 | tf_op jit(solution)/shard_map/all_to_all | solution.py:307
  16.7 0.0 copy-start.3
  16.7 0.6 copy-done.3
  18.7 0.0 collective-permute-done
  18.7 1.1 %collective-permute-start.3 = (f32[2,24,128]{2,1,0:T(8,128)S(1)}, f32[2,24,128]{2,1,0:T(8,128)S(1)}, u32[]{:S(2)}, u32[]{:S(2)}) collective-permute-start(f32[2,24,128]{2,1,0:T(8,128)S(1)} %pad_maximum_fusion), channel_id=1, source_target_pairs={{0,3},{1,2},{2,1},{3,0},{4,7},{5,6},{6,5},{7,4},{8,11},{9,10},{10,... | collective-permute-start | bytes 73736 | tf_op jit(solution)/shard_map/ppermute | solution.py:303
  19.8 2.4 %collective-permute-start.2 = (f32[2,24,128]{2,1,0:T(8,128)S(1)}, f32[2,24,128]{2,1,0:T(8,128)S(1)}, u32[]{:S(2)}, u32[]{:S(2)}) collective-permute-start(f32[2,24,128]{2,1,0:T(8,128)S(1)} %pad_maximum_fusion), channel_id=1, source_target_pairs={{0,2},{1,3},{2,0},{3,1},{4,6},{5,7},{6,4},{7,5},{8,10},{9,11},{10,... | collective-permute-start | bytes 73736 | tf_op jit(solution)/shard_map/ppermute | solution.py:303
  22.1 0.1 collective-permute-start.1
  22.3 3.7 %collective-permute-done.1 = f32[2,24,128]{2,1,0:T(8,128)S(1)} collective-permute-done((f32[2,24,128]{2,1,0:T(8,128)S(1)}, f32[2,24,128]{2,1,0:T(8,128)S(1)}, u32[]{:S(2)}, u32[]{:S(2)}) %collective-permute-start.1) | collective-permute-done | bytes 24608 | tf_op jit(solution)/shard_map/ppermute | solution.py:303
  26.0 0.0 collective-permute-done.2
  26.0 2.1 %all_gather.3.points = f32[16,24,128]{2,1,0:T(8,128)S(1)} all-gather(f32[8,24,128]{2,1,0:T(8,128)S(1)} %constant_dynamic-update-slice_fusion), channel_id=1, replica_groups=mesh['y'=4,'core'=2,'x'=4,'z'=8] {'core'}, dimensions={0}, use_global_device_ids=true | all-gather | bytes 294912 | tf_op jit(solution)/shard_map/all_gather | solution.py:339
  28.2 0.6 prep.1
  28.7 5.3 %all-to-all-done.held = f32[16,128,128]{2,1,0:T(8,128)S(1)} async-done(((f32[16,128,128]{2,1,0:T(8,128)}), f32[16,128,128]{2,1,0:T(8,128)S(1)}, u32[]{:S(2)}, u32[]{:S(2)}) %all-to-all-start) | async-done | bytes 1048608 | tf_op jit(solution)/shard_map/all_to_all | solution.py:307
  34.0 9.3 %mu.1 = (f32[16,16,128]{2,1,0:T(8,128)S(1)}, bf16[2048,160]{1,0:T(8,128)(2,1)S(1)}) custom-call(f32[16,128,128]{2,1,0:T(8,128)S(1)} %all-to-all-done.held, bf16[2048,160]{1,0:T(8,128)(2,1)S(1)} %get-tuple-element.20.rows_in, f32[24,128]{1,0:T(8,128)S(1)} %copy-done, f32[24,128]{1,0:T(8,128)S(1)} %copy-done.1, f32[1,128]{1,0:T(1,128)S(1)} %fusion.high, ...), custom_call_target="tpu_custom_call" | custom-call | tf_op jit(solution)/shard_map/mu/pallas_call | solution.py:348
  43.3 12.2 %all_to_all.25.held = f32[16,16,128]{2,1,0:T(8,128)S(1)} all-to-all(f32[16,16,128]{2,1,0:T(8,128)S(1)} %get-tuple-element.21), channel_id=1, replica_groups=mesh['y'=4,'core'=2,'x'=4,'z'=8] {'core','z'}, dimensions={0} | all-to-all | bytes 262144 | tf_op jit(solution)/shard_map/all_to_all | solution.py:307
  55.5 3.0 %first.1 = (f32[16,16,128]{2,1,0:T(8,128)S(1)}, f32[16,128]{1,0:T(8,128)S(1)}, f32[1,128]{1,0:T(1,128)}) custom-call(f32[16,16,128]{2,1,0:T(8,128)S(1)} %all_to_all.25.held, bf16[160,2048]{1,0:T(8,128)(2,1)S(1)} %get-tuple-element.22.rows_in, bf16[2048,160]{1,0:T(8,128)(2,1)S(1)} %get-tuple-element.23.cols_in, f32[1,128]{1,0:T(1,128)S(1)} %fusion.high, ...), custom_call_target="tpu_custom_call" | custom-call | tf_op jit(solution)/shard_map/first/pallas_call | solution.py:363
  58.5 10.6 %all_to_all.26.held = f32[16,16,128]{2,1,0:T(8,128)S(1)} all-to-all(f32[16,16,128]{2,1,0:T(8,128)S(1)} %get-tuple-element.25), channel_id=1, replica_groups=mesh['y'=4,'core'=2,'x'=4,'z'=8] {'y','x'}, dimensions={0} | all-to-all | bytes 262144 | tf_op jit(solution)/shard_map/all_to_all | solution.py:307
  69.1 2.4 %second.1 = f32[16,17,1,128]{3,2,1,0:T(1,128)S(1)} custom-call(f32[16,16,128]{2,1,0:T(8,128)S(1)} %all_to_all.26.held, bf16[160,2048]{1,0:T(8,128)(2,1)S(1)} %get-tuple-element.22.rows_in, bf16[2048,160]{1,0:T(8,128)(2,1)S(1)} %get-tuple-element.23.cols_in, f32[1]{0:T(128)S(6)} %copy.16.noise, s32[1]{0:T(128)} %bitcast.3.at, s32[1]{0:T(128)} %bitcast.5.at_col), custom_call_target="tpu_custom_call" | custom-call | tf_op jit(solution)/shard_map/second/pallas_call | solution.py:373
  71.5 11.8 %all_to_all.27.held = f32[16,17,1,128]{3,2,1,0:T(1,128)S(1)} all-to-all(f32[16,17,1,128]{3,2,1,0:T(1,128)S(1)} %second.1), channel_id=1, replica_groups=mesh['y'=4,'core'=2,'x'=4,'z'=8] {'core','z'}, dimensions={0} | all-to-all | bytes 278528 | tf_op jit(solution)/shard_map/all_to_all | solution.py:307
  83.3 0.2 moments.1
  83.4 10.7 %all_to_all.28.held = f32[16,8,128]{2,1,0:T(8,128)S(1)} all-to-all(f32[16,8,128]{2,1,0:T(8,128)S(1)} %get-tuple-element.27), channel_id=1, replica_groups=mesh['y'=4,'core'=2,'x'=4,'z'=8] {'y','x'}, dimensions={0} | all-to-all | bytes 131072 | tf_op jit(solution)/shard_map/all_to_all | solution.py:307
  94.2 1.2 %final.1 = (f32[1,128]{1,0:T(1,128)}, f32[1,128]{1,0:T(1,128)}) custom-call(f32[16,8,128]{2,1,0:T(8,128)S(1)} %all_to_all.28.held, f32[8,128]{1,0:T(8,128)S(1)} %get-tuple-element.28.own), custom_call_target="tpu_custom_call" | custom-call | tf_op jit(solution)/shard_map/final/pallas_call | solution.py:392
  (13 shorter events, 0.0 us)
Async XLA Ops:
  0.6 18.0 %collective-permute-start = (f32[24,128]{1,0:T(8,128)}, f32[24,128]{1,0:T(8,128)S(1)}, u32[]{:S(2)}, u32[]{:S(2)}) collective-permute-start(f32[24,128]{1,0:T(8,128)} %refs_2_.1), channel_id=1, source_target_pairs={{0,4},{1,5},{2,6},{3,7},{4,0},{5,1},{6,2},{7,3},{8,12},{9,13},{10,... | collective-permute-start | bytes 36872 | tf_op jit(solution)/shard_map/ppermute | solution.py:303
  9.6 7.1 %copy-start.2 = (f32[24,128]{1,0:T(8,128)S(1)}, f32[24,128]{1,0:T(8,128)}, u32[]{:S(2)}) copy-start(f32[24,128]{1,0:T(8,128)} %refs_2_.1) | copy-start | bytes 36868
  9.6 24.4 %all-to-all-start = ((f32[16,128,128]{2,1,0:T(8,128)}), f32[16,128,128]{2,1,0:T(8,128)S(1)}, u32[]{:S(2)}, u32[]{:S(2)}) async-start(f32[16,128,128]{2,1,0:T(8,128)} %get-tuple-element.17), calls=%async_computation | async-start | bytes 2097152 | tf_op jit(solution)/shard_map/all_to_all | solution.py:307
  16.7 0.7 copy-start.3
  18.7 7.3 %collective-permute-start.3 = (f32[2,24,128]{2,1,0:T(8,128)S(1)}, f32[2,24,128]{2,1,0:T(8,128)S(1)}, u32[]{:S(2)}, u32[]{:S(2)}) collective-permute-start(f32[2,24,128]{2,1,0:T(8,128)S(1)} %pad_maximum_fusion), channel_id=1, source_target_pairs={{0,3},{1,2},{2,1},{3,0},{4,7},{5,6},{6,5},{7,4},{8,11},{9,10},{10,... | collective-permute-start | bytes 73736 | tf_op jit(solution)/shard_map/ppermute | solution.py:303
  19.8 6.2 %collective-permute-start.2 = (f32[2,24,128]{2,1,0:T(8,128)S(1)}, f32[2,24,128]{2,1,0:T(8,128)S(1)}, u32[]{:S(2)}, u32[]{:S(2)}) collective-permute-start(f32[2,24,128]{2,1,0:T(8,128)S(1)} %pad_maximum_fusion), channel_id=1, source_target_pairs={{0,2},{1,3},{2,0},{3,1},{4,6},{5,7},{6,4},{7,5},{8,10},{9,11},{10,... | collective-permute-start | bytes 73736 | tf_op jit(solution)/shard_map/ppermute | solution.py:303
  22.1 3.8 %collective-permute-start.1 = (f32[2,24,128]{2,1,0:T(8,128)S(1)}, f32[2,24,128]{2,1,0:T(8,128)S(1)}, u32[]{:S(2)}, u32[]{:S(2)}) collective-permute-start(f32[2,24,128]{2,1,0:T(8,128)S(1)} %pad_maximum_fusion), channel_id=1, source_target_pairs={{0,1},{1,0},{2,3},{3,2},{4,5},{5,4},{6,7},{7,6},{8,9},{9,8},{10,11... | collective-permute-start | bytes 73736 | tf_op jit(solution)/shard_map/ppermute | solution.py:303
  26.0 2.2 %copy-start = (f32[24,128]{1,0:T(8,128)S(1)}, f32[24,128]{1,0:T(8,128)}, u32[]{:S(2)}) copy-start(f32[24,128]{1,0:T(8,128)} %get-tuple-element.18.scale_low.scale) | copy-start | bytes 36868
  26.0 2.1 %copy-start.1 = (f32[24,128]{1,0:T(8,128)S(1)}, f32[24,128]{1,0:T(8,128)}, u32[]{:S(2)}) copy-start(f32[24,128]{1,0:T(8,128)} %get-tuple-element.19.scale_high) | copy-start | bytes 36868

commit v12 on v11

--- a/solution.py
+++ b/solution.py
@@ -278,7 +278,12 @@
         own_out[i : i + 1, :] = jnp.sum(jnp.where(own, v, 0.0), axis=0, keepdims=True)
 
 
-def final_kernel(held, own, x_out, r_out):
+def final_kernel(held, own, mu, mu_out, x_out, r_out, x_held, r_held, sems):
+    copies = [
+        pltpu.make_async_copy(a, b, sems.at[i])
+        for i, (a, b) in enumerate(((mu, mu_out), (x_held, x_out), (r_held, r_out)))
+    ]
+    copies[0].start()
     pairs = [(held[j], pltpu.roll(held[j], 4, 0)) for j in range(held.shape[0])]
     while len(pairs) > 1:
         pairs = [pair_add(a, b) for a, b in zip(pairs[::2], pairs[1::2])]
@@ -295,8 +300,12 @@
     alpha0, grow = alpha[0], scale[0]
     alpha1 = (v1[0] + v1[1]) / (v2[0] + v2[1])
     b, image, last = own[0:1, :], own[1:2, :], own[2:3, :]
-    x_out[...] = alpha0 * b + alpha1 * (grow * b - alpha0 * image)
-    r_out[...] = (b - alpha0 * image) - alpha1 * (grow * image - alpha0 * last)
+    x_held[...] = alpha0 * b + alpha1 * (grow * b - alpha0 * image)
+    copies[1].start()
+    r_held[...] = (b - alpha0 * image) - alpha1 * (grow * image - alpha0 * last)
+    copies[2].start()
+    for copy in copies:
+        copy.wait()
 
 
 def exchange_z(blocks, step, size):
@@ -389,14 +398,15 @@
         name="moments",
     )(last_held, target, at)
     moments_held = exchange(moments, COLS)
-    x, r = pl.pallas_call(
+    mu, x, r = pl.pallas_call(
         final_kernel,
-        out_shape=(shape((1, LANES)), shape((1, LANES))),
-        in_specs=[VMEM] * 2,
-        out_specs=(VMEM,) * 2,
+        out_shape=(shape((1, LANES)),) * 3,
+        in_specs=[VMEM] * 3,
+        out_specs=(HBM,) * 3,
+        scratch_shapes=[pltpu.VMEM((1, LANES), F32), pltpu.VMEM((1, LANES), F32), pltpu.SemaphoreType.DMA((3,))],
         compiler_params=params(4),
         name="final",
-    )(moments_held, own)
+    )(moments_held, own, mu)
     return mu.reshape(LANES), x.reshape(LANES), r.reshape(LANES)
 
 

time: 95.8 us -> 95.6 us (level)
  no operation moved by 1% of the time
where the time goes in v12:
time: 95.6 us; the launch traced here: 95.1 us
  blocking collectives  47.4 us (50%)
  Pallas kernels  18.7 us (20%)
  starting transfers between devices  17 us (18%)
  waiting for transfers between devices  8.99 us (9%)
  between operations  2.25 us (2%)
    all_to_all x4, blocking collectives, exchange(): return lax.all_to_all(blocks, axes, 0, 0, tiled=True)  45.3 us
    ppermute x4, starting transfers between devices, exchange_z(): return lax.ppermute(blocks, 'z', [(i, i ^ step) for i in range(size)])  9.95 us
    pallas_call x1, Pallas kernels, local(): pl.pallas_call(mu_kernel, out_shape=(shape((n_row, n_row, LANES)), shape(...  9.3 us
    all_to_all x1, starting transfers between devices, exchange(): return lax.all_to_all(blocks, axes, 0, 0, tiled=True)  7.05 us
    all_to_all x1, waiting for transfers between devices, exchange(): return lax.all_to_all(blocks, axes, 0, 0, tiled=True)  5.27 us
    ppermute x4, waiting for transfers between devices, exchange_z(): return lax.ppermute(blocks, 'z', [(i, i ^ step) for i in range(size)])  3.71 us
    pallas_call x1, Pallas kernels, local(): pl.pallas_call(pack_kernel, out_shape=(shape((n_col, PACKED, LANES)), sha...  2.59 us
    pallas_call x1, Pallas kernels, local(): pl.pallas_call(first_kernel, out_shape=(shape((n_col, n_col, LANES)), sha...  2.52 us
  transfers between devices with their start and end apart: 5, of which 2 were waited for; matrix products, arithmetic and copies ran while one was open for 0% of the time, Pallas kernels for 3%

profile of v12, /device:TPU:32, one launch (start us, length us, event | category | flops | bytes accessed | tf_op | source)
XLA Modules:
  0.0 95.1 jit_solution(13699274863432208630)
XLA Ops:
  0.6 6.4 %collective-permute-start = (f32[24,128]{1,0:T(8,128)}, f32[24,128]{1,0:T(8,128)S(1)}, u32[]{:S(2)}, u32[]{:S(2)}) collective-permute-start(f32[24,128]{1,0:T(8,128)} %refs_2_.1), channel_id=1, source_target_pairs={{0,4},{1,5},{2,6},{3,7},{4,0},{5,1},{6,2},{7,3},{8,12},{9,13},{10,... | collective-permute-start | bytes 36872 | tf_op jit(solution)/shard_map/ppermute | solution.py:312
  7.0 2.6 %pack.1 = (f32[16,128,128]{2,1,0:T(8,128)}, f32[24,128]{1,0:T(8,128)}, f32[24,128]{1,0:T(8,128)}) custom-call(f32[24,512]{1,0:T(8,128)} %refs_0_.1, f32[1,512]{1,0:T(1,128)} %bitcast.14, f32[24,128]{1,0:T(8,128)} %refs_2_.1, f32[24]{0:T(128)} %refs_3_.1, f32[24]{0:T(128)} %refs_4_.1), custom_call_target="tpu_custom_call" | custom-call | tf_op jit(solution)/shard_map/pack/pallas_call | solution.py:326
  9.6 0.0 copy-start.2
  9.6 7.0 %all-to-all-start = ((f32[16,128,128]{2,1,0:T(8,128)}), f32[16,128,128]{2,1,0:T(8,128)S(1)}, u32[]{:S(2)}, u32[]{:S(2)}) async-start(f32[16,128,128]{2,1,0:T(8,128)} %get-tuple-element.18), calls=%async_computation | async-start | bytes 2097152 | tf_op jit(solution)/shard_map/all_to_all | solution.py:316
  16.7 0.0 copy-start.3
  16.7 0.6 copy-done.3
  18.7 0.0 collective-permute-done
  18.7 1.1 %collective-permute-start.3 = (f32[2,24,128]{2,1,0:T(8,128)S(1)}, f32[2,24,128]{2,1,0:T(8,128)S(1)}, u32[]{:S(2)}, u32[]{:S(2)}) collective-permute-start(f32[2,24,128]{2,1,0:T(8,128)S(1)} %pad_maximum_fusion), channel_id=1, source_target_pairs={{0,3},{1,2},{2,1},{3,0},{4,7},{5,6},{6,5},{7,4},{8,11},{9,10},{10,... | collective-permute-start | bytes 73736 | tf_op jit(solution)/shard_map/ppermute | solution.py:312
  19.8 2.4 %collective-permute-start.2 = (f32[2,24,128]{2,1,0:T(8,128)S(1)}, f32[2,24,128]{2,1,0:T(8,128)S(1)}, u32[]{:S(2)}, u32[]{:S(2)}) collective-permute-start(f32[2,24,128]{2,1,0:T(8,128)S(1)} %pad_maximum_fusion), channel_id=1, source_target_pairs={{0,2},{1,3},{2,0},{3,1},{4,6},{5,7},{6,4},{7,5},{8,10},{9,11},{10,... | collective-permute-start | bytes 73736 | tf_op jit(solution)/shard_map/ppermute | solution.py:312
  22.1 0.1 collective-permute-start.1
  22.3 3.7 %collective-permute-done.1 = f32[2,24,128]{2,1,0:T(8,128)S(1)} collective-permute-done((f32[2,24,128]{2,1,0:T(8,128)S(1)}, f32[2,24,128]{2,1,0:T(8,128)S(1)}, u32[]{:S(2)}, u32[]{:S(2)}) %collective-permute-start.1) | collective-permute-done | bytes 24608 | tf_op jit(solution)/shard_map/ppermute | solution.py:312
  26.0 0.0 collective-permute-done.2
  26.0 2.1 %all_gather.3.points = f32[16,24,128]{2,1,0:T(8,128)S(1)} all-gather(f32[8,24,128]{2,1,0:T(8,128)S(1)} %constant_dynamic-update-slice_fusion), channel_id=1, replica_groups=mesh['y'=4,'core'=2,'x'=4,'z'=8] {'core'}, dimensions={0}, use_global_device_ids=true | all-gather | bytes 294912 | tf_op jit(solution)/shard_map/all_gather | solution.py:348
  28.2 0.6 prep.1
  28.7 5.3 %all-to-all-done.held = f32[16,128,128]{2,1,0:T(8,128)S(1)} async-done(((f32[16,128,128]{2,1,0:T(8,128)}), f32[16,128,128]{2,1,0:T(8,128)S(1)}, u32[]{:S(2)}, u32[]{:S(2)}) %all-to-all-start) | async-done | bytes 1048608 | tf_op jit(solution)/shard_map/all_to_all | solution.py:316
  34.0 9.3 %mu.1 = (f32[16,16,128]{2,1,0:T(8,128)S(1)}, bf16[2048,160]{1,0:T(8,128)(2,1)S(1)}) custom-call(f32[16,128,128]{2,1,0:T(8,128)S(1)} %all-to-all-done.held, bf16[2048,160]{1,0:T(8,128)(2,1)S(1)} %get-tuple-element.21.rows_in, f32[24,128]{1,0:T(8,128)S(1)} %copy-done, f32[24,128]{1,0:T(8,128)S(1)} %copy-done.1, f32[1,128]{1,0:T(1,128)S(1)} %fusion.high, ...), custom_call_target="tpu_custom_call" | custom-call | tf_op jit(solution)/shard_map/mu/pallas_call | solution.py:357
  43.3 12.2 %all_to_all.25.held = f32[16,16,128]{2,1,0:T(8,128)S(1)} all-to-all(f32[16,16,128]{2,1,0:T(8,128)S(1)} %get-tuple-element.22), channel_id=1, replica_groups=mesh['y'=4,'core'=2,'x'=4,'z'=8] {'core','z'}, dimensions={0} | all-to-all | bytes 262144 | tf_op jit(solution)/shard_map/all_to_all | solution.py:316
  55.5 2.5 %first.1 = (f32[16,16,128]{2,1,0:T(8,128)S(1)}, f32[16,128]{1,0:T(8,128)S(1)}, f32[1,128]{1,0:T(1,128)S(1)}) custom-call(f32[16,16,128]{2,1,0:T(8,128)S(1)} %all_to_all.25.held, bf16[160,2048]{1,0:T(8,128)(2,1)S(1)} %get-tuple-element.23.rows_in, bf16[2048,160]{1,0:T(8,128)(2,1)S(1)} %get-tuple-element.24.cols_in, f32[1,128]{1,0:T(1,128)S(1)} %fusion.high, ...), custom_call_target="tpu_custom_call" | custom-call | tf_op jit(solution)/shard_map/first/pallas_call | solution.py:372
  58.1 10.6 %all_to_all.26.held = f32[16,16,128]{2,1,0:T(8,128)S(1)} all-to-all(f32[16,16,128]{2,1,0:T(8,128)S(1)} %get-tuple-element.25), channel_id=1, replica_groups=mesh['y'=4,'core'=2,'x'=4,'z'=8] {'y','x'}, dimensions={0} | all-to-all | bytes 262144 | tf_op jit(solution)/shard_map/all_to_all | solution.py:316
  68.6 2.4 %second.1 = f32[16,17,1,128]{3,2,1,0:T(1,128)S(1)} custom-call(f32[16,16,128]{2,1,0:T(8,128)S(1)} %all_to_all.26.held, bf16[160,2048]{1,0:T(8,128)(2,1)S(1)} %get-tuple-element.23.rows_in, bf16[2048,160]{1,0:T(8,128)(2,1)S(1)} %get-tuple-element.24.cols_in, f32[1]{0:T(128)S(6)} %copy.16.noise, s32[1]{0:T(128)} %bitcast.3.at, s32[1]{0:T(128)} %bitcast.5.at_col), custom_call_target="tpu_custom_call" | custom-call | tf_op jit(solution)/shard_map/second/pallas_call | solution.py:382
  71.1 11.8 %all_to_all.27.held = f32[16,17,1,128]{3,2,1,0:T(1,128)S(1)} all-to-all(f32[16,17,1,128]{3,2,1,0:T(1,128)S(1)} %second.1), channel_id=1, replica_groups=mesh['y'=4,'core'=2,'x'=4,'z'=8] {'core','z'}, dimensions={0} | all-to-all | bytes 278528 | tf_op jit(solution)/shard_map/all_to_all | solution.py:316
  82.8 0.2 moments.1
  83.0 10.7 %all_to_all.28.held = f32[16,8,128]{2,1,0:T(8,128)S(1)} all-to-all(f32[16,8,128]{2,1,0:T(8,128)S(1)} %get-tuple-element.27), channel_id=1, replica_groups=mesh['y'=4,'core'=2,'x'=4,'z'=8] {'y','x'}, dimensions={0} | all-to-all | bytes 131072 | tf_op jit(solution)/shard_map/all_to_all | solution.py:316
  93.7 1.2 %final.1 = (f32[1,128]{1,0:T(1,128)}, f32[1,128]{1,0:T(1,128)}, f32[1,128]{1,0:T(1,128)}) custom-call(f32[16,8,128]{2,1,0:T(8,128)S(1)} %all_to_all.28.held, f32[8,128]{1,0:T(8,128)S(1)} %get-tuple-element.28.own, f32[1,128]{1,0:T(1,128)S(1)} %get-tuple-element.29.mu), custom_call_target="tpu_custom_call" | custom-call | tf_op jit(solution)/shard_map/final/pallas_call | solution.py:401
  (13 shorter events, 0.0 us)
Async XLA Ops:
  0.6 18.0 %collective-permute-start = (f32[24,128]{1,0:T(8,128)}, f32[24,128]{1,0:T(8,128)S(1)}, u32[]{:S(2)}, u32[]{:S(2)}) collective-permute-start(f32[24,128]{1,0:T(8,128)} %refs_2_.1), channel_id=1, source_target_pairs={{0,4},{1,5},{2,6},{3,7},{4,0},{5,1},{6,2},{7,3},{8,12},{9,13},{10,... | collective-permute-start | bytes 36872 | tf_op jit(solution)/shard_map/ppermute | solution.py:312
  9.6 7.1 %copy-start.2 = (f32[24,128]{1,0:T(8,128)S(1)}, f32[24,128]{1,0:T(8,128)}, u32[]{:S(2)}) copy-start(f32[24,128]{1,0:T(8,128)} %refs_2_.1) | copy-start | bytes 36868
  9.6 24.4 %all-to-all-start = ((f32[16,128,128]{2,1,0:T(8,128)}), f32[16,128,128]{2,1,0:T(8,128)S(1)}, u32[]{:S(2)}, u32[]{:S(2)}) async-start(f32[16,128,128]{2,1,0:T(8,128)} %get-tuple-element.18), calls=%async_computation | async-start | bytes 2097152 | tf_op jit(solution)/shard_map/all_to_all | solution.py:316
  16.7 0.7 copy-start.3
  18.7 7.3 %collective-permute-start.3 = (f32[2,24,128]{2,1,0:T(8,128)S(1)}, f32[2,24,128]{2,1,0:T(8,128)S(1)}, u32[]{:S(2)}, u32[]{:S(2)}) collective-permute-start(f32[2,24,128]{2,1,0:T(8,128)S(1)} %pad_maximum_fusion), channel_id=1, source_target_pairs={{0,3},{1,2},{2,1},{3,0},{4,7},{5,6},{6,5},{7,4},{8,11},{9,10},{10,... | collective-permute-start | bytes 73736 | tf_op jit(solution)/shard_map/ppermute | solution.py:312
  19.8 6.2 %collective-permute-start.2 = (f32[2,24,128]{2,1,0:T(8,128)S(1)}, f32[2,24,128]{2,1,0:T(8,128)S(1)}, u32[]{:S(2)}, u32[]{:S(2)}) collective-permute-start(f32[2,24,128]{2,1,0:T(8,128)S(1)} %pad_maximum_fusion), channel_id=1, source_target_pairs={{0,2},{1,3},{2,0},{3,1},{4,6},{5,7},{6,4},{7,5},{8,10},{9,11},{10,... | collective-permute-start | bytes 73736 | tf_op jit(solution)/shard_map/ppermute | solution.py:312
  22.1 3.8 %collective-permute-start.1 = (f32[2,24,128]{2,1,0:T(8,128)S(1)}, f32[2,24,128]{2,1,0:T(8,128)S(1)}, u32[]{:S(2)}, u32[]{:S(2)}) collective-permute-start(f32[2,24,128]{2,1,0:T(8,128)S(1)} %pad_maximum_fusion), channel_id=1, source_target_pairs={{0,1},{1,0},{2,3},{3,2},{4,5},{5,4},{6,7},{7,6},{8,9},{9,8},{10,11... | collective-permute-start | bytes 73736 | tf_op jit(solution)/shard_map/ppermute | solution.py:312
  26.0 2.2 %copy-start = (f32[24,128]{1,0:T(8,128)S(1)}, f32[24,128]{1,0:T(8,128)}, u32[]{:S(2)}) copy-start(f32[24,128]{1,0:T(8,128)} %get-tuple-element.19.scale_low.scale) | copy-start | bytes 36868
  26.0 2.1 %copy-start.1 = (f32[24,128]{1,0:T(8,128)S(1)}, f32[24,128]{1,0:T(8,128)}, u32[]{:S(2)}) copy-start(f32[24,128]{1,0:T(8,128)} %get-tuple-element.20.scale_high) | copy-start | bytes 36868
